TPU v7x, 32 devices: a whole 2x2x4 slice. The times are simulated.
32 devices in a mesh: dp: 16 (over z, y, x), seq: 2 (over core).
Axes of the slice: x: 2, y: 2, z: 4, core: 2. Of those that a mesh axis runs over, the one named last changes fastest.
Arguments:
- inputs: bfloat16 [64, 1024, 256], P('dp', 'seq'), may hold values from -6 to 6
- cotangent: bfloat16 [64, 1024, 256], P('dp', 'seq'), may hold values from -6 to 6
- loss_mask: int32 [64, 1024], P('dp', 'seq'), may hold values from 0 to 1, as said below
- complement_map: int32 [256], replicated, may hold values from 0 to 255, each once
- owners: int32 [32], replicated, may hold values from 0 to 15, as said below
- weights: float32 [64, 13696], P('dp'), as said below
- first_moment: float32 [64, 13696], P('dp'), as said below
- second_moment: float32 [64, 13696], P('dp'), as said below
Outputs:
- output: bfloat16 [64, 1024, 256], P('dp', 'seq')
- grad_input: float32 [64, 1024, 256], P('dp', 'seq')
- new_weights: float32 [64, 13696], P('dp')
- new_first: float32 [64, 13696], P('dp')
- new_second: float32 [64, 13696], P('dp')
Inputs may be any that keep to these rules, and one draw needn't show every extreme that they name: `loss_mask`: 1 marks a loss token; each window has its own rate, drawn between 8 and 22 percent. `complement_map`: each channel appears once. `owners`: at most 4 blocks share an owner, and some owner holds exactly 4. `weights`: rows that no block fills are zero. `first_moment`: rows that no block fills are zero. `second_moment`: entries of filled rows are positive; rows that no block fills are zero.
All inputs are finite; a program needn't handle non-finite values.
Results may differ from a plain program's by a relative error of at most 0.0093.
Values may be sent and summed in bfloat16 or wider, within the bound.
No kernel may reach another device: no remote copies, remote signals or barrier semaphores. Data moves between devices by JAX's collectives and lax.ppermute only.
A program may use at most 320 MiB of HBM per device.

v0:
```python
import math

import jax
import jax.numpy as jnp
from jax import lax
from jax.sharding import PartitionSpec as P

D = 256
INNER = 512
STATE = 16
RANK = 16
KERNEL = 4
SCAN_BLOCK = 64
SLOTS = 4
STEP_COUNT = 10
PARAMS = 438016
MATRIX_END = 425984


BETA_ONE = 0.9
BETA_TWO = 0.95
ADAM_EPSILON = 1e-08
RATE_MATRIX = 0.1
RATE_VECTOR = 0.5
WEIGHT_DECAY = 0.1
NORM_EPSILON = 1e-05
HIGHEST_PREC = lax.Precision.HIGHEST


def param_shapes():
    return [
        (D, 2 * INNER),
        (INNER, RANK + 2 * STATE),
        (RANK, INNER),
        (INNER, D),
        (INNER, KERNEL),
        (INNER,),
        (INNER,),
        (INNER, STATE),
        (INNER,),
        (D,),
    ]


def unpack_params(flat):
    pieces = []
    offset = 0
    for shape in param_shapes():
        count = math.prod(shape)
        pieces.append(flat[offset : offset + count].reshape(shape))
        offset += count
    return pieces


def slot_index(owners):
    count = owners.shape[0]
    order = jnp.arange(count, dtype=jnp.int32)
    same = (owners[None, :] == owners[:, None]) & (order[None, :] < order[:, None])
    return owners * SLOTS + jnp.sum(same.astype(jnp.int32), axis=1)


def norm_piece(tokens, gain):
    mean_square = jnp.mean(tokens * tokens, axis=-1, keepdims=True)
    return tokens * lax.rsqrt(mean_square + NORM_EPSILON) * gain


def front_piece(inner_in, conv_w, conv_b, w_x):
    length = inner_in.shape[2]
    padded = jnp.pad(inner_in, ((0, 0), (0, 0), (KERNEL - 1, 0), (0, 0)))
    conv_out = conv_b + sum(
        (conv_w[:, index] * padded[:, :, index : index + length] for index in range(KERNEL))
    )
    act = jax.nn.silu(conv_out)
    return (act, jnp.einsum("wkte,ef->wktf", act, w_x, precision=HIGHEST_PREC))


def scan_piece(act, gate_in, proj, w_dt, dt_bias, a_log, d_skip):
    low_rank = proj[..., :RANK]
    entry = proj[..., RANK : RANK + STATE]
    readout = proj[..., RANK + STATE :]
    delta = jax.nn.softplus(
        jnp.einsum("wktr,re->wkte", low_rank, w_dt, precision=HIGHEST_PREC) + dt_bias
    )
    decay_rate = -jnp.exp(a_log)
    blocks = act.shape[2] // SCAN_BLOCK

    def to_blocks(value):
        shaped = value.reshape(value.shape[:2] + (blocks, SCAN_BLOCK) + value.shape[3:])
        return jnp.moveaxis(shaped, 2, 0)

    @jax.checkpoint
    def run_block(state, pieces):
        step_delta, step_act, step_entry, step_read = pieces
        outputs = []
        for index in range(SCAN_BLOCK):
            moment = step_delta[:, :, index]
            state = (
                jnp.exp(moment[..., None] * decay_rate) * state
                + (moment * step_act[:, :, index])[..., None] * step_entry[:, :, index, None, :]
            )
            outputs.append(jnp.sum(state * step_read[:, :, index, None, :], axis=-1))
        return (state, jnp.stack(outputs, axis=2))

    start = jnp.zeros(act.shape[:2] + (act.shape[3], STATE), jnp.float32)
    final_state, outputs = lax.scan(
        run_block, start, tuple((to_blocks(value) for value in (delta, act, entry, readout)))
    )
    scanned = jnp.moveaxis(outputs, 0, 2).reshape(act.shape) + d_skip * act
    return scanned * jax.nn.silu(gate_in)


def on_device(
    inputs, cotangent, loss_mask, complement_map, owners, weights, first_moment, second_moment
):
    slots = slot_index(owners)
    every = lax.all_gather(weights, "dp", axis=0, tiled=True)
    theta = every[slots].reshape(-1)
    w_in, w_x, w_dt, w_out, conv_w, conv_b, dt_bias, a_log, d_skip, gain = unpack_params(theta)
    width = INNER // lax.axis_size("seq")
    begin = lax.axis_index("seq") * width

    def mine(value, axis):
        return lax.dynamic_slice_in_dim(value, begin, width, axis)

    conv_w_mine = mine(conv_w, 0)
    conv_b_mine = mine(conv_b, 0)
    w_x_mine = mine(w_x, 0)
    w_dt_mine = mine(w_dt, 1)
    dt_bias_mine = mine(dt_bias, 0)
    a_log_mine = mine(a_log, 0)
    d_skip_mine = mine(d_skip, 0)
    tokens = inputs.astype(jnp.float32)
    normed_full, norm_back = jax.vjp(norm_piece, tokens, gain)
    normed = normed_full.astype(jnp.bfloat16)
    perm_low = (complement_map[:, None] == jnp.arange(D, dtype=jnp.int32)[None, :]).astype(
        jnp.bfloat16
    )
    mirror = jnp.einsum("wtd,cd->wtc", normed, perm_low, preferred_element_type=jnp.float32).astype(
        jnp.bfloat16
    )
    copies = jnp.stack([normed, mirror], axis=1)
    w_in_low = w_in.astype(jnp.bfloat16).reshape(D, 2, INNER)
    projected = jnp.einsum(
        "wktd,dqe->wkqte", copies, w_in_low, preferred_element_type=jnp.float32
    ).astype(jnp.bfloat16)
    channels = lax.all_to_all(projected, "seq", split_axis=4, concat_axis=3, tiled=True)
    channels = jnp.stack([channels[:, 0], channels[:, 1, :, ::-1]], axis=1).astype(jnp.float32)
    inner_in = channels[:, :, 0]
    gate_in = channels[:, :, 1]
    (act, partial_proj), front_back = jax.vjp(
        front_piece, inner_in, conv_w_mine, conv_b_mine, w_x_mine
    )
    proj = lax.psum(partial_proj, "seq")
    gated_full, scan_back = jax.vjp(
        scan_piece, act, gate_in, proj, w_dt_mine, dt_bias_mine, a_log_mine, d_skip_mine
    )
    gated = gated_full.astype(jnp.bfloat16)
    gated = jnp.stack([gated[:, 0], gated[:, 1, ::-1]], axis=1)
    rows = lax.all_to_all(gated, "seq", split_axis=2, concat_axis=3, tiled=True)
    out_low = w_out.astype(jnp.bfloat16)
    out_mirror = jnp.dot(out_low, perm_low, preferred_element_type=jnp.float32).astype(jnp.bfloat16)
    out_pair = jnp.stack([out_low, out_mirror])
    mixed = jnp.einsum("wkte,ked->wtd", rows, out_pair, preferred_element_type=jnp.float32)
    output = (tokens + mixed).astype(jnp.bfloat16)
    upstream = cotangent.astype(jnp.float32) * loss_mask.astype(jnp.float32)[..., None]
    upstream_low = upstream.astype(jnp.bfloat16)
    pair_grad = jnp.einsum("wkte,wtd->ked", rows, upstream_low, preferred_element_type=jnp.float32)
    grad_w_out = pair_grad[0] + jnp.take(pair_grad[1], complement_map, axis=1)
    grad_rows = jnp.einsum(
        "wtd,ked->wkte", upstream_low, out_pair, preferred_element_type=jnp.float32
    ).astype(jnp.bfloat16)
    grad_gated = lax.all_to_all(grad_rows, "seq", split_axis=3, concat_axis=2, tiled=True)
    grad_gated = jnp.stack([grad_gated[:, 0], grad_gated[:, 1, ::-1]], axis=1).astype(jnp.float32)
    grad_act, grad_gate_in, grad_proj_part, grad_w_dt, grad_dt_bias, grad_a_log, grad_d_skip = (
        scan_back(grad_gated)
    )
    grad_proj = lax.psum(grad_proj_part.astype(jnp.bfloat16), "seq").astype(jnp.float32)
    grad_inner_in, grad_conv_w, grad_conv_b, grad_w_x = front_back((grad_act, grad_proj))
    grad_channels = jnp.stack([grad_inner_in, grad_gate_in], axis=2).astype(jnp.bfloat16)
    grad_channels = jnp.stack([grad_channels[:, 0], grad_channels[:, 1, :, ::-1]], axis=1)
    grad_projected = lax.all_to_all(grad_channels, "seq", split_axis=3, concat_axis=4, tiled=True)
    grad_w_in = jnp.einsum(
        "wktd,wkqte->dqe", copies, grad_projected, preferred_element_type=jnp.float32
    ).reshape(D, 2 * INNER)
    grad_copies = jnp.einsum(
        "wkqte,dqe->wktd", grad_projected, w_in_low, preferred_element_type=jnp.float32
    )
    grad_normed = grad_copies[:, 0] + jnp.einsum(
        "wtc,cd->wtd", grad_copies[:, 1], perm_low.astype(jnp.float32), precision=HIGHEST_PREC
    )
    grad_norm_in, grad_gain = norm_back(grad_normed)
    grad_input = upstream + grad_norm_in

    def place(value, axis, shape):
        return lax.dynamic_update_slice_in_dim(jnp.zeros(shape, jnp.float32), value, begin, axis)

    pieces = [
        grad_w_in,
        place(grad_w_x, 0, (INNER, RANK + 2 * STATE)),
        place(grad_w_dt, 1, (RANK, INNER)),
        grad_w_out,
        place(grad_conv_w, 0, (INNER, KERNEL)),
        place(grad_conv_b, 0, (INNER,)),
        place(grad_dt_bias, 0, (INNER,)),
        place(grad_a_log, 0, (INNER, STATE)),
        place(grad_d_skip, 0, (INNER,)),
        grad_gain,
    ]
    blocks_count = owners.shape[0]
    block_len = weights.shape[1]
    flat_grad = jnp.concatenate([item.reshape(-1) for item in pieces])
    grad_blocks = jnp.pad(flat_grad, (0, blocks_count * block_len - PARAMS)).reshape(
        blocks_count, block_len
    )
    my_slots = lax.axis_index("dp") * SLOTS + jnp.arange(SLOTS, dtype=jnp.int32)
    matches = slots[None, :] == my_slots[:, None]
    occupied = jnp.any(matches, axis=1)
    block_of = jnp.sum(
        jnp.where(matches, jnp.arange(blocks_count, dtype=jnp.int32)[None, :], 0), axis=1
    )
    summed = lax.psum(grad_blocks, "seq")
    owned = lax.psum_scatter(
        jnp.zeros((lax.axis_size("dp") * SLOTS, block_len), jnp.float32).at[slots].set(summed),
        "dp",
        scatter_dimension=0,
        tiled=True,
    )
    new_first = BETA_ONE * first_moment + (1.0 - BETA_ONE) * owned
    new_second = BETA_TWO * second_moment + (1.0 - BETA_TWO) * owned * owned
    position = block_of[:, None] * block_len + jnp.arange(block_len, dtype=jnp.int32)[None, :]
    is_matrix = position < MATRIX_END
    rate = jnp.where(is_matrix, RATE_MATRIX, RATE_VECTOR)
    decay = jnp.where(is_matrix, WEIGHT_DECAY, 0.0)
    corrected = (
        new_first
        / (1.0 - BETA_ONE**STEP_COUNT)
        / (jnp.sqrt(new_second / (1.0 - BETA_TWO**STEP_COUNT)) + ADAM_EPSILON)
    )
    new_theta = weights - rate * (corrected + decay * weights)
    keep = occupied[:, None]
    return (
        output,
        grad_input,
        jnp.where(keep, new_theta, 0.0),
        jnp.where(keep, new_first, 0.0),
        jnp.where(keep, new_second, 0.0),
    )


def solution(mesh):
    in_specs = (
        P("dp", "seq", None),
        P("dp", "seq", None),
        P("dp", "seq"),
        P(),
        P(),
        P("dp", None),
        P("dp", None),
        P("dp", None),
    )
    out_specs = (
        P("dp", "seq", None),
        P("dp", "seq", None),
        P("dp", None),
        P("dp", None),
        P("dp", None),
    )
    return jax.shard_map(
        on_device, mesh=mesh, in_specs=in_specs, out_specs=out_specs, check_vma=False
    )
```

profile of v0, /device:TPU:1, one launch (start us, length us, event | category | flops | bytes accessed | tf_op | source)
XLA Modules:
  0.0 1846.8 jit_solution(7780981367416574337)
XLA Ops:
  15.5 67.3 %all-gather.3.cloned.1.call-done = f32[16,4,13696]{2,1,0:T(4,128)} async-done(((f32[1,4,13696]{2,1,0:T(4,128)}), f32[16,4,13696]{2,1,0:T(4,128)}) %all-gather.3.cloned.1.call-update) | async-done | bytes 3506192 | tf_op jit(solution)/shard_map/all_gather | solution.py:116
  96.0 78.3 %slice.3451 = f32[109568,4]{1,0:T(8,128)} reshape(f32[32,13696]{1,0:T(8,128)S(1)} %copy-done.1) | data formatting | bytes 3506176 | tf_op jit(solution)/shard_map/slice | solution.py:50
  194.5 17.8 copy.152
  212.3 13.3 all_to_all.72
  225.6 20.9 %copy.153 = bf16[4,2,2,512,2,256]{5,3,4,1,0,2:T(8,128)(2,1)} copy(bf16[4,2,2,512,2,256]{3,1,0,2,5,4:T(2,128)(2,1)} %bitcast.2861) | data formatting | bytes 16777216 | tf_op jit(solution)/shard_map/all_to_all | solution.py:146
  252.3 59.7 %rev.12 = bf16[4,1,2,1024,256]{4,3,1,0,2:T(8,128)(2,1)} reverse(bf16[4,1,2,1024,256]{4,3,1,0,2:T(8,128)(2,1)} %get-tuple-element.2040), dimensions={3} | reverse | bytes 8388608 | tf_op jit(solution)/shard_map/rev | solution.py:147
  322.4 11.8 fusion.152
  335.3 18.0 fusion.81
  353.3 12.8 fusion.128
  405.6 15.5 copy.253
  421.1 25.3 %rev.14 = bf16[4,1,1024,256]{3,2,1,0:T(8,128)(2,1)S(1)} reverse(bf16[4,1,1024,256]{3,2,1,0:T(8,128)(2,1)} %get-tuple-element.2042), dimensions={2} | reverse | bytes 4194304 | tf_op jit(solution)/shard_map/rev | solution.py:173
  454.2 13.9 compare_select_fusion.1
  484.9 213.5 %while.41 = (s32[]{:T(128)}, f32[4,2,256,16]{2,3,1,0:T(8,128)S(1)}, f32[16,4,2,64,256]{4,3,2,1,0:T(8,128)}, f32[16,4,2,256,16]{3,4,2,1,0:T(8,128)}, f32[16,4,2,6...) while((s32[]{:T(128)}, f32[4,2,256,16]{2,3,1,0:T(8,128)S(1)}, ...), condition=%wide.region_68.69_spmd.clone, body=%wide.region_3.68_spmd.clone.sunk | while | flops 18972676 | bytes 15443073 | solution.py:105
  719.5 582.3 %while.42 = (s32[]{:T(128)}, f32[256,16]{0,1:T(8,128)S(1)}, f32[4,2,256,16]{2,3,1,0:T(8,128)S(1)}, f32[16,4,2,64,256]{4,2,1,3,0:T(2,128)}, f32[16,4,2,64,256]{4,...) while((s32[]{:T(128)}, f32[256,16]{0,1:T(8,128)S(1)}, ...), condition=%wide.region_390.391_spmd.clone, body=%wide.region_69.390_spmd.clone.sunk | while | flops 74584064 | bytes 40205012 | solution.py:105
  1367.0 18.1 broadcast_multiply_fusion
  1385.1 35.4 %multiply_reduce_fusion.384 = (f32[256]{0:T(256)S(1)}, f32[256]{0:T(256)S(1)}, f32[256]{0:T(256)S(1)}, f32[256]{0:T(256)S(1)}, f32[256]{0:T(256)S(1)}, /*index=5...) fusion(f32[4,2,1024,256]{3,2,1,0:T(8,128)} %get-tuple-element.1, ...), kind=kLoop, calls=%fused_computation.1597 | loop fusion | flops 69204480 | bytes 88090624 | tf_op jit(solution)/shard_map/transpose(jvp())/reduce_sum | solution.py:108
  1430.6 12.1 fusion.83
  1446.3 59.7 %rev.15 = bf16[4,1,2,1024,256]{4,3,1,0,2:T(8,128)(2,1)} reverse(bf16[4,1,2,1024,256]{4,3,1,0,2:T(8,128)(2,1)} %get-tuple-element.2038), dimensions={3} | reverse | bytes 8388608 | tf_op jit(solution)/shard_map/rev | solution.py:180
  1513.5 14.5 copy.172
  1538.5 16.3 copy.252
  1554.8 14.2 all_to_all.67
  1578.7 20.2 %rev.13 = bf16[4,1,1024,256]{3,2,1,0:T(8,128)(2,1)} reverse(bf16[4,1,1024,256]{3,2,1,0:T(8,128)(2,1)S(1)} %get-tuple-element.2044), dimensions={2} | reverse | bytes 4194304 | tf_op jit(solution)/shard_map/rev | solution.py:158
  1657.5 19.4 %all-reduce.279.cloned.1.call-done = f32[32,13696]{1,0:T(8,128)} async-done(((f32[32,13696]{1,0:T(8,128)}), f32[32,13696]{1,0:T(8,128)}) %all-reduce.279.cloned.1.call-update) | async-done | bytes 1753104 | tf_op jit(solution)/shard_map/psum | solution.py:221
  1690.6 147.1 %all-reduce.281.cloned.1.call-done = f32[64,13696]{1,0:T(8,128)} async-done(((f32[64,13696]{1,0:T(8,128)}), f32[64,13696]{1,0:T(8,128)}) %all-reduce.281.cloned.1.call-update) | async-done | bytes 3506192
  (3335 shorter events, 1100.8 us)
Async XLA Ops:
  7.2 75.6 %all-gather.3.cloned.1.call-start = ((), (), s32[]{:S(2)}) async-start(), calls=%async_computation.7 | async-start | bytes 3725312 | tf_op jit(solution)/shard_map/all_gather | solution.py:116
  7.9 446.3 %all-reduce.275.cloned.1.call-start = ((), (), s32[]{:S(2)}) async-start(), calls=%async_computation.4 | async-start | bytes 3145728 | tf_op jit(solution)/shard_map/psum | solution.py:153
  8.7 369.7 %copy-start.31 = (f32[4,512]{1,0:T(4,128)}, f32[4,512]{1,0:T(4,128)S(1)}, u32[]{:S(2)}) copy-start(f32[4,512]{1,0:T(4,128)S(1)} %convert_element_type.75) | copy-start | bytes 24580
  15.5 77.9 %copy-start.33 = (f32[4,512]{1,0:T(4,128)}, f32[4,512]{1,0:T(4,128)S(1)}, u32[]{:S(2)}) copy-start(f32[4,512]{1,0:T(4,128)S(1)} %fusion.142) | copy-start | bytes 24580
  190.4 21.9 %copy-start.13 = (bf16[256,1024]{0,1:T(8,128)(2,1)}, bf16[256,1024]{0,1:T(8,128)(2,1)S(1)}, u32[]{:S(2)}) copy-start(bf16[256,1024]{0,1:T(8,128)(2,1)S(1)} %copy.207) | copy-start | bytes 1572868
  334.3 19.0 %copy-start.26 = (f32[512,48]{1,0:T(8,128)}, f32[512,48]{1,0:T(8,128)S(1)}, u32[]{:S(2)}) copy-start(f32[512,48]{1,0:T(8,128)S(1)} %reshape.4258) | copy-start | bytes 294916
  353.3 25.2 %copy-start.8 = (bf16[4,512,256]{2,1,0:T(8,128)(2,1)S(1)}, bf16[4,512,256]{2,1,0:T(8,128)(2,1)}, u32[]{:S(2)}) copy-start(bf16[4,512,256]{2,1,0:T(8,128)(2,1)} %param.13) | copy-start | bytes 3145732
  353.3 25.2 %copy-start.19 = (bf16[1,512,256]{2,1,0:T(8,128)(2,1)S(1)}, bf16[1,512,256]{2,1,0:T(8,128)(2,1)}, u32[]{:S(2)}) copy-start(bf16[1,512,256]{2,1,0:T(8,128)(2,1)} %fusion.108) | copy-start | bytes 786436
  366.1 1000.9 %all-reduce.277.cloned.1.call-start = ((), (), s32[]{:S(2)}) async-start(), calls=%async_computation.5 | async-start | bytes 1572864 | tf_op jit(solution)/shard_map/psum | solution.py:177
  378.5 25.8 %copy-start.16 = (f32[512,16]{1,0:T(8,128)}, f32[512,16]{1,0:T(8,128)S(1)}, u32[]{:S(2)}) copy-start(f32[512,16]{1,0:T(8,128)S(1)} %slice.4272) | copy-start | bytes 98308
  405.6 40.8 %copy-start.17 = (f32[512,16]{1,0:T(8,128)S(1)}, f32[512,16]{1,0:T(8,128)}, u32[]{:S(2)}) copy-start(f32[512,16]{1,0:T(8,128)} %copy-done.16) | copy-start | bytes 98308
  1343.7 333.2 %all-reduce.279.cloned.1.call-start = ((), (), s32[]{:S(2)}) async-start(), calls=%async_computation.6 | async-start | bytes 3506176 | tf_op jit(solution)/shard_map/psum | solution.py:221
  1366.9 18.1 copy-start.38
  1385.1 35.8 %copy-start.24 = (bf16[4,2,1024,48]{2,3,1,0:T(8,128)(2,1)S(1)}, bf16[4,2,1024,48]{2,3,1,0:T(8,128)(2,1)}, u32[]{:S(2)}) copy-start(bf16[4,2,1024,48]{2,3,1,0:T(8,128)(2,1)} %all-reduce.277.cloned.1.call-done) | copy-start | bytes 2359300
  1646.5 34.8 %copy-start.54 = (u32[32]{0:T(128)S(1)}, u32[32]{0:T(128)}, u32[]{:S(2)}) copy-start(u32[32]{0:T(128)} %constant.712) | copy-start | bytes 388
  1646.5 36.1 %copy-start.53 = (s32[32]{0:T(128)S(1)}, s32[32]{0:T(128)}, u32[]{:S(2)}) copy-start(s32[32]{0:T(128)} %get-tuple-element.1317) | copy-start | bytes 388
  1646.5 36.5 %copy-start.36 = (f32[4,512]{1,0:T(4,128)S(1)}, f32[4,512]{1,0:T(4,128)}, u32[]{:S(2)}) copy-start(f32[4,512]{1,0:T(4,128)} %copy-done.35) | copy-start | bytes 24580
  1657.4 25.6 %copy-start.10 = (bf16[4,512,256]{2,1,0:T(8,128)(2,1)S(1)}, bf16[4,512,256]{2,1,0:T(8,128)(2,1)}, u32[]{:S(2)}) copy-start(bf16[4,512,256]{2,1,0:T(8,128)(2,1)} %param.13) | copy-start | bytes 3145732
  1657.4 28.8 %copy-start.20 = (bf16[1,512,256]{2,1,0:T(8,128)(2,1)S(1)}, bf16[1,512,256]{2,1,0:T(8,128)(2,1)}, u32[]{:S(2)}) copy-start(bf16[1,512,256]{2,1,0:T(8,128)(2,1)} %fusion.108) | copy-start | bytes 786436
  1657.4 28.8 %copy-start.21 = (bf16[1,512,256]{2,1,0:T(8,128)(2,1)S(1)}, bf16[1,512,256]{2,1,0:T(8,128)(2,1)}, u32[]{:S(2)}) copy-start(bf16[1,512,256]{2,1,0:T(8,128)(2,1)} %slice_bitcast_fusion.520) | copy-start | bytes 786436
  1657.5 180.2 %all-reduce.281.cloned.1.call-start = ((), (), s32[]{:S(2)}) async-start(), calls=%async_computation.8 | async-start | bytes 7012352
  1681.3 156.4 %copy-start.23 = (f32[4,13696]{1,0:T(4,128)S(1)}, f32[4,13696]{1,0:T(4,128)}, u32[]{:S(2)}) copy-start(f32[4,13696]{1,0:T(4,128)} %param.17) | copy-start | bytes 657412
  1681.3 156.4 %copy-start.29 = (f32[4,13696]{1,0:T(4,128)S(1)}, f32[4,13696]{1,0:T(4,128)}, u32[]{:S(2)}) copy-start(f32[4,13696]{1,0:T(4,128)} %param.19) | copy-start | bytes 657412
  1681.3 156.4 %copy-start.30 = (f32[4,13696]{1,0:T(4,128)S(1)}, f32[4,13696]{1,0:T(4,128)}, u32[]{:S(2)}) copy-start(f32[4,13696]{1,0:T(4,128)} %param.18) | copy-start | bytes 657412
  (40 other events, 333.2 us)
Sparse Core Ops, SparseCore 0:
  10.8 71.9 all-gather.2
  366.2 19.0 all-reduce.274
  1343.8 17.8 all-reduce.276
  1657.6 19.2 all-reduce.278
  1683.6 154.1 all-reduce.280
where the time goes:
time: 1870 us; the launch traced here: 1850 us
  other arithmetic  741 us (40%)
  local copies, waits for them, and re-layouts  684 us (37%)
  waiting for transfers between devices  235 us (13%)
  matrix products  101 us (5%)
  blocking collectives  40.6 us (2%)
  loops' own time  19 us (1%)
    reduce_sum x512, other arithmetic, run_block(): moment[..., None] * decay_rate  277 us
    dynamic_update_slice x80, other arithmetic, scan_piece(): lax.scan(run_block, start, tuple((to_blocks(value) for value in (delta, a...  156 us
    unnamed x6, waiting for transfers between devices  148 us
    reduce_sum x272, other arithmetic, run_block(): outputs.append(jnp.sum(state * step_read[:, :, index, None, :], axis=-1))  104 us
    squeeze x80, local copies, waits for them, and re-layouts, scan_piece(): lax.scan(run_block, start, tuple((to_blocks(value) for value in (delta, a...  99 us
    slice x14, local copies, waits for them, and re-layouts, unpack_params(): pieces.append(flat[offset:offset + count].reshape(shape))  92 us
    all_gather x1, waiting for transfers between devices, on_device(): every = lax.all_gather(weights, 'dp', axis=0, tiled=True)  67.3 us
    rev x1, local copies, waits for them, and re-layouts, on_device(): channels[:, 1, :, ::-1]  59.7 us
  transfers between devices with their start and end apart: 5, of which 3 were waited for; matrix products, arithmetic and copies ran while one was open for 6% of the time, Pallas kernels for 0%

commit v1 on v0

v1 whole, which is shorter than its diff:
```python
import functools
import math

import jax
import jax.numpy as jnp
from jax import lax
from jax.experimental import pallas as pl
from jax.experimental.pallas import tpu as pltpu
from jax.sharding import PartitionSpec as P

D = 256
INNER = 512
STATE = 16
RANK = 16
KERNEL = 4
SLOTS = 4
STEP_COUNT = 10
PARAMS = 438016
MATRIX_END = 425984
BETA_ONE = 0.9
BETA_TWO = 0.95
ADAM_EPSILON = 1e-08
RATE_MATRIX = 0.1
RATE_VECTOR = 0.5
WEIGHT_DECAY = 0.1
NORM_EPSILON = 1e-05
LOG2E = 1.4426950408889634
LN2 = 0.6931471805599453
CHUNK = 128
GROUP = 16
LANES = 128
BF = jnp.bfloat16
F32 = jnp.float32
NT = (((1,), (1,)), ((), ()))
TN = (((0,), (0,)), ((), ()))


def split_low(value):
    high = value.astype(BF)
    return high, (value - high.astype(F32)).astype(BF)


def dot(a, b, dims=None):
    if dims is None:
        return jnp.dot(a, b, preferred_element_type=F32)
    return lax.dot_general(a, b, dims, preferred_element_type=F32)


def row_sum(value):
    return jnp.sum(value.reshape(value.shape[0] // 8, 8, value.shape[1]), axis=0)


def rows_of(ref, start, count):
    return ref.at[pl.ds(pl.multiple_of(start, count), count)]


def layer_kernel(
    chunks,
    x_ref,
    up_ref,
    flip_ref,
    w_in_ref,
    w_out_ref,
    wx_ref,
    wdt_ref,
    vec_ref,
    rate_ref,
    gain_ref,
    tile_ref,
    sums_ref,
    fold_ref,
    mask_ref,
    out_ref,
    gin_ref,
    gwin_ref,
    gwout_ref,
    gsmall_ref,
    gvec_ref,
    ggain_ref,
    states,
    act_s,
    slope_s,
    delta_s,
    ratio_s,
    dscan_s,
    inner_s,
    proj_s,
    projt_s,
    dread_s,
    dproj_s,
    gated_s,
    copy_s,
    dmix_s,
    mixed_s,
    dnorm_s,
    chunk_a,
    chunk_p,
    y_s,
    u_s,
    gslope_s,
    gsilu_s,
    halo_s,
    dconv_s,
    wide_s,
    diag_s,
    state_s,
):
    window = pl.program_id(0)
    natural = pl.program_id(1)
    phase = pl.program_id(2)
    forward = phase < chunks
    chunk = jnp.where(forward, phase, 2 * chunks - 1 - phase)
    place = jnp.where(natural == 1, chunk, chunks - 1 - chunk)
    row = pl.multiple_of(chunk * CHUNK, CHUNK)
    nat_row = pl.multiple_of(place * CHUNK, CHUNK)
    here = pl.ds(row, CHUNK)
    there = pl.ds(nat_row, CHUNK)
    groups = CHUNK // GROUP
    block = 32
    pieces = range(0, CHUNK, block)

    @pl.when((window == 0) & (natural == 0) & (phase == 0))
    def _():
        gwin_ref[...] = jnp.zeros_like(gwin_ref)
        gwout_ref[...] = jnp.zeros_like(gwout_ref)
        gsmall_ref[...] = jnp.zeros_like(gsmall_ref)
        gvec_ref[...] = jnp.zeros_like(gvec_ref)
        ggain_ref[...] = jnp.zeros_like(ggain_ref)

    @pl.when(phase == 0)
    def _():
        state_s[...] = jnp.zeros_like(state_s)
        halo_s[0:8, :] = jnp.zeros((8, INNER), F32)

    @pl.when(phase == chunks)
    def _():
        state_s[...] = jnp.zeros_like(state_s)
        dconv_s[0:8, :] = jnp.zeros((8, INNER), F32)

    def norm_parts():
        xf = x_ref[0].astype(F32)
        inv = lax.rsqrt(jnp.mean(xf * xf, axis=-1, keepdims=True) + NORM_EPSILON)
        return xf, inv

    def diagonal(high, low, which):
        for part, value in enumerate((high, low)):
            wide = dot(value, tile_ref[which])
            for g in range(groups):
                diag_s[g, part * GROUP : (part + 1) * GROUP, :] = (
                    wide[g * GROUP : (g + 1) * GROUP] * mask_ref[...]
                ).astype(BF)

    def spread(value, index):
        return jnp.broadcast_to(value[index : index + 1, :], (8, LANES))

    @pl.when(forward)
    def _():
        xf, inv = norm_parts()
        normed = (xf * inv * gain_ref[...]).astype(BF)
        copy = dot(flip_ref[0], normed).astype(BF)
        dmix = dot(flip_ref[0], up_ref[0]).astype(BF)
        copy_s[here, :] = copy
        dmix_s[here, :] = dmix
        halo_s[8:, :] = dot(copy, w_in_ref[0, :, :INNER]).astype(BF).astype(F32)
        gate_all = dot(copy, w_in_ref[0, :, INNER:])
        dgated_all = dot(dmix, w_out_ref[0], NT)
        for a in pieces:
            conv = vec_ref[4:5, :]
            for j in range(KERNEL):
                conv = conv + vec_ref[j : j + 1, :] * halo_s[a + 5 + j : a + 5 + j + block, :]
            inner_s[pl.ds(row + a, block), :] = halo_s[8 + a : 8 + a + block, :]
            sig = 1.0 / (1.0 + jnp.exp(-conv))
            act_s[pl.ds(row + a, block), :] = conv * sig
            slope_s[pl.ds(row + a, block), :] = sig * (1.0 + conv * (1.0 - sig))
            gate = gate_all[a : a + block].astype(BF).astype(F32)
            dgated = dgated_all[a : a + block].astype(BF).astype(F32)
            gsig = 1.0 / (1.0 + jnp.exp(-gate))
            gsilu = gate * gsig
            gsilu_s[a : a + block, :] = gsilu
            dscan_s[pl.ds(row + a, block), :] = dgated * gsilu
            gslope_s[a : a + block, :] = dgated * gsig * (1.0 + gate * (1.0 - gsig))
        halo_s[0:8, :] = halo_s[CHUNK : CHUNK + 8, :]
        act_high, act_low = split_low(act_s[here, :])
        proj = dot(act_high, wx_ref[0]) + dot(act_low, wx_ref[0]) + dot(act_high, wx_ref[1])
        proj_s[here, :] = proj
        columns = jnp.transpose(proj)
        projt_s[chunk] = columns[: 3 * STATE]
        proj_high, proj_low = split_low(proj)
        pre_all = (
            dot(proj_high, wdt_ref[0]) + dot(proj_low, wdt_ref[0]) + dot(proj_high, wdt_ref[1])
        )
        for a in pieces:
            pre = pre_all[a : a + block] + vec_ref[5:6, :]
            small = jnp.exp(-jnp.abs(pre))
            delta = jnp.maximum(pre, 0.0) + jnp.log1p(small)
            sig = jnp.where(pre >= 0.0, 1.0, small) / (1.0 + small)
            delta_s[pl.ds(row + a, block), :] = delta
            ratio_s[pl.ds(row + a, block), :] = jnp.where(delta > 1e-30, sig / delta, 1.0)
            u_s[a : a + block, :] = delta * act_s[pl.ds(row + a, block), :]
        diagonal(proj_high, proj_low, 1)
        state = [
            [state_s[8 * h : 8 * h + 8, LANES * e : LANES * (e + 1)] for e in range(4)]
            for h in range(2)
        ]
        last = [
            jnp.concatenate([state[0][e], state[1][e]], axis=0).astype(BF) for e in range(4)
        ]
        for g in range(groups):
            base = pl.multiple_of(row + g * GROUP, GROUP)
            steps = delta_s[pl.ds(base, GROUP), :]
            feeds = u_s[g * GROUP : (g + 1) * GROUP, :]
            for t in range(GROUP):
                at = g * GROUP + t
                entry = [
                    jnp.broadcast_to(
                        columns[STATE + 8 * h : STATE + 8 * h + 8, at : at + 1], (8, LANES)
                    )
                    for h in range(2)
                ]
                for e in range(4):
                    lanes = slice(LANES * e, LANES * (e + 1))
                    step = spread(steps[:, lanes], t)
                    feed = spread(feeds[:, lanes], t)
                    for h in range(2):
                        decay = jnp.exp2(step * rate_ref[8 * h : 8 * h + 8, lanes])
                        state[h][e] = decay * state[h][e] + feed * entry[h]
                    states[pl.ds(pl.multiple_of((base + t) * STATE, STATE), STATE), lanes] = last[e]
                    last[e] = jnp.concatenate([state[0][e], state[1][e]], axis=0).astype(BF)
                    chunk_a[at * STATE : (at + 1) * STATE, lanes] = last[e]
            held = chunk_a[g * GROUP * STATE : (g + 1) * GROUP * STATE, :]
            pair = dot(diag_s[g], held)
            y_s[g * GROUP : (g + 1) * GROUP, :] = pair[:GROUP] + pair[GROUP:]
            found = dot(dscan_s[pl.ds(base, GROUP), :].astype(BF), held, NT)
            wide_s[g * GROUP : (g + 1) * GROUP, :] = (found * mask_ref[...]).astype(BF)
        for h in range(2):
            for e in range(4):
                state_s[8 * h : 8 * h + 8, LANES * e : LANES * (e + 1)] = state[h][e]
        dread_s[here, :] = dot(wide_s[...], fold_ref[1])
        for a in pieces:
            scanned = y_s[a : a + block, :] + vec_ref[6:7, :] * act_s[pl.ds(row + a, block), :]
            gated_s[pl.ds(row + a, block), :] = (scanned * gsilu_s[a : a + block, :]).astype(BF)
            dproj_s[pl.ds(row + a, block), INNER:] = (
                scanned * gslope_s[a : a + block, :]
            ).astype(BF)
        back = dot(flip_ref[0], gated_s[here, :]).astype(BF)
        mixed = dot(back, w_out_ref[0])

        @pl.when(natural == 0)
        def _():
            mixed_s[there, :] = mixed

        @pl.when(natural == 1)
        def _():
            out_ref[0] = (x_ref[0].astype(F32) + (mixed + mixed_s[there, :])).astype(BF)

        @pl.when(phase == chunks - 1)
        def _():
            gwout_ref[1 - natural] += dot(gated_s[...], dmix_s[...], TN)

    @pl.when(jnp.logical_not(forward))
    def _():
        dconv_s[CHUNK : CHUNK + 8, :] = dconv_s[0:8, :]
        proj = proj_s[here, :]
        proj_high, proj_low = split_low(proj)
        diagonal(proj_high, proj_low, 0)
        columns = projt_s[chunk]
        for a in pieces:
            u_s[a : a + block, :] = (
                delta_s[pl.ds(row + a, block), :] * act_s[pl.ds(row + a, block), :]
            )
        carry = [
            [state_s[8 * h : 8 * h + 8, LANES * e : LANES * (e + 1)] for e in range(4)]
            for h in range(2)
        ]
        rate_sum = None
        for g in reversed(range(groups)):
            base = pl.multiple_of(row + g * GROUP, GROUP)
            steps = delta_s[pl.ds(base, GROUP), :]
            feeds = dscan_s[pl.ds(base, GROUP), :]
            for t in reversed(range(GROUP)):
                at = g * GROUP + t
                read = [
                    jnp.broadcast_to(
                        columns[2 * STATE + 8 * h : 2 * STATE + 8 * h + 8, at : at + 1], (8, LANES)
                    )
                    for h in range(2)
                ]
                for e in range(4):
                    lanes = slice(LANES * e, LANES * (e + 1))
                    step = spread(steps[:, lanes], t)
                    feed = spread(feeds[:, lanes], t)
                    before = states[
                        pl.ds(pl.multiple_of((base + t) * STATE, STATE), STATE), lanes
                    ].astype(F32)
                    lams = []
                    prods = []
                    for h in range(2):
                        power = step * rate_ref[8 * h : 8 * h + 8, lanes]
                        lam = feed * read[h] + carry[h][e]
                        carry[h][e] = jnp.exp2(power) * lam
                        lams.append(lam)
                        prods.append(power * (carry[h][e] * before[8 * h : 8 * h + 8]))
                    chunk_a[at * STATE : (at + 1) * STATE, lanes] = jnp.concatenate(
                        lams, axis=0
                    ).astype(BF)
                    chunk_p[at * STATE : (at + 1) * STATE, lanes] = jnp.concatenate(
                        prods, axis=0
                    ).astype(BF)
            span = slice(g * GROUP * STATE, (g + 1) * GROUP * STATE)
            held = chunk_a[span, :]
            pair = dot(diag_s[g], held)
            y_s[g * GROUP : (g + 1) * GROUP, :] = pair[:GROUP] + pair[GROUP:]
            both = dot(sums_ref[...], chunk_p[span, :])
            gslope_s[g * GROUP : (g + 1) * GROUP, :] = both[:GROUP]
            rate_sum = both[GROUP:] if rate_sum is None else rate_sum + both[GROUP:]
            found = dot(u_s[g * GROUP : (g + 1) * GROUP, :].astype(BF), held, NT)
            wide_s[g * GROUP : (g + 1) * GROUP, :] = (found * mask_ref[...]).astype(BF)
        for h in range(2):
            for e in range(4):
                state_s[8 * h : 8 * h + 8, LANES * e : LANES * (e + 1)] = carry[h][e]
        gsmall_ref[0:STATE, :] += rate_sum * LN2
        for a in pieces:
            here_a = pl.ds(row + a, block)
            dfeed = y_s[a : a + block, :]
            dpre = ratio_s[here_a, :] * (
                gslope_s[a : a + block, :] * LN2 + dfeed * u_s[a : a + block, :]
            )
            gsilu_s[a : a + block, :] = dpre
            dscan = dscan_s[here_a, :]
            y_s[a : a + block, :] = dscan * vec_ref[6:7, :] + dfeed * delta_s[here_a, :]
            gvec_ref[5] += row_sum(dpre)
            gvec_ref[6] += row_sum(dscan * act_s[here_a, :])
        dpre_high, dpre_low = split_low(gsilu_s[...])
        dproj = (
            dot(dpre_high, wdt_ref[0], NT)
            + dot(dpre_low, wdt_ref[0], NT)
            + dot(dpre_high, wdt_ref[1], NT)
            + dot(wide_s[...], fold_ref[0])
            + dread_s[here, :]
        )
        dproj_high, dproj_low = split_low(dproj)
        gsmall_ref[STATE : 2 * STATE, :] += dot(columns[:RANK].astype(BF), dpre_high)
        turned = jnp.transpose(dproj)[: 3 * STATE].astype(BF)
        gsmall_ref[2 * STATE : 5 * STATE, :] += dot(turned, act_s[here, :].astype(BF))
        extra = (
            dot(dproj_high, wx_ref[0], NT)
            + dot(dproj_low, wx_ref[0], NT)
            + dot(dproj_high, wx_ref[1], NT)
        )
        for a in pieces:
            dconv_s[a : a + block, :] = (
                y_s[a : a + block, :] + extra[a : a + block]
            ) * slope_s[pl.ds(row + a, block), :]
        for a in pieces:
            inner = inner_s[pl.ds(row + a, block), :]
            dinner = None
            for j in range(KERNEL):
                moved = dconv_s[a + 3 - j : a + 3 - j + block, :]
                term = vec_ref[j : j + 1, :] * moved
                dinner = term if dinner is None else dinner + term
                gvec_ref[j] += row_sum(moved * inner)
                if j == KERNEL - 1:
                    gvec_ref[4] += row_sum(moved)
            dproj_s[pl.ds(row + a, block), :INNER] = dinner.astype(BF)
        back = dot(flip_ref[0], dproj_s[here, :]).astype(BF)
        dnorm = dot(back, w_in_ref[0], NT)

        @pl.when(natural == 0)
        def _():
            dnorm_s[there, :] = dnorm

        @pl.when(natural == 1)
        def _():
            xf, inv = norm_parts()
            total = dnorm + dnorm_s[there, :]
            scaled = total * gain_ref[...]
            hat = xf * inv
            ggain_ref[...] += row_sum(total * hat)
            mean = jnp.mean(scaled * hat, axis=-1, keepdims=True)
            gin_ref[0] = up_ref[0].astype(F32) + inv * (scaled - hat * mean)

        @pl.when(phase == 2 * chunks - 1)
        def _():
            gwin_ref[1 - natural] += dot(copy_s[...], dproj_s[...], TN)


def run_layer(x, up, w_in, w_x, w_dt, w_out, conv_w, conv_b, dt_bias, a_log, d_skip, gain, perm):
    windows, length, _ = x.shape
    chunks = length // CHUNK
    w_in_pair = jnp.stack([w_in, dot(perm, w_in, TN).astype(BF)])
    w_out_pair = jnp.stack([w_out, dot(w_out, perm).astype(BF)])
    wx_pair = jnp.pad(jnp.stack(w_x), ((0, 0), (0, 0), (0, LANES - w_x[0].shape[1])))
    wdt_pair = jnp.pad(jnp.stack(w_dt), ((0, 0), (0, LANES - RANK), (0, 0)))
    vec = jnp.concatenate(
        [conv_w.T, conv_b[None], dt_bias[None], d_skip[None], jnp.zeros((1, INNER), F32)], axis=0
    )
    rate = (-LOG2E) * jnp.exp(a_log).T
    flip = jnp.stack([jnp.eye(CHUNK, dtype=BF), jnp.eye(CHUNK, dtype=BF)[::-1]])
    wide = GROUP * STATE
    lane = jnp.arange(wide)
    narrow = jnp.arange(LANES)
    tile = jnp.stack(
        [(narrow[:, None] == base + lane[None, :] % STATE) for base in (STATE, 2 * STATE)]
    ).astype(BF)
    fold = jnp.swapaxes(tile, 1, 2)
    mask = jnp.arange(GROUP)[:, None] == lane[None, :] // STATE
    sums = jnp.concatenate([mask, jnp.arange(STATE)[:, None] == lane[None, :] % STATE]).astype(BF)
    mask = mask.astype(F32)

    def of_chunk(w, q, p):
        c = jnp.where(p < chunks, p, 2 * chunks - 1 - p)
        return (w, jnp.where(q == 1, c, chunks - 1 - c), 0)

    def out_chunk(w, q, p):
        return (w, jnp.where(q == 1, jnp.minimum(p, chunks - 1), 0), 0)

    def gin_chunk(w, q, p):
        return (w, jnp.where(q == 1, jnp.minimum(2 * chunks - 1 - p, chunks - 1), chunks - 1), 0)

    def whole(shape):
        return pl.BlockSpec(shape, lambda w, q, p: (0,) * len(shape))

    def of_copy(shape):
        return pl.BlockSpec((1,) + shape[1:], lambda w, q, p: (1 - q,) + (0,) * (len(shape) - 1))

    piece = (1, CHUNK, D)
    operands = (
        x, up, flip, w_in_pair, w_out_pair, wx_pair, wdt_pair, vec, rate, gain[None], tile, sums, fold, mask,
    )
    in_specs = [
        pl.BlockSpec(piece, of_chunk),
        pl.BlockSpec(piece, of_chunk),
        of_copy(flip.shape),
        of_copy(w_in_pair.shape),
        of_copy(w_out_pair.shape),
    ] + [whole(item.shape) for item in operands[5:]]
    grads = [
        jax.ShapeDtypeStruct((2, D, 2 * INNER), F32),
        jax.ShapeDtypeStruct((2, INNER, D), F32),
        jax.ShapeDtypeStruct((5 * STATE, INNER), F32),
        jax.ShapeDtypeStruct((7, 8, INNER), F32),
        jax.ShapeDtypeStruct((8, D), F32),
    ]
    wide_f32 = pltpu.VMEM((length, INNER), F32)
    chunk_f32 = pltpu.VMEM((CHUNK, INNER), F32)
    return pl.pallas_call(
        functools.partial(layer_kernel, chunks),
        grid=(windows, 2, 2 * chunks),
        in_specs=in_specs,
        out_specs=[pl.BlockSpec(piece, out_chunk), pl.BlockSpec(piece, gin_chunk)]
        + [whole(item.shape) for item in grads],
        out_shape=[
            jax.ShapeDtypeStruct(x.shape, BF),
            jax.ShapeDtypeStruct(x.shape, F32),
        ]
        + grads,
        scratch_shapes=[
            pltpu.VMEM((length * STATE, INNER), BF),
            wide_f32,
            wide_f32,
            wide_f32,
            wide_f32,
            wide_f32,
            wide_f32,
            pltpu.VMEM((length, LANES), F32),
            pltpu.VMEM((chunks, 3 * STATE, CHUNK), F32),
            pltpu.VMEM((length, LANES), F32),
            pltpu.VMEM((length, 2 * INNER), BF),
            pltpu.VMEM((length, INNER), BF),
            pltpu.VMEM((length, D), BF),
            pltpu.VMEM((length, D), BF),
            pltpu.VMEM((length, D), F32),
            pltpu.VMEM((length, D), F32),
            pltpu.VMEM((CHUNK * STATE, INNER), BF),
            pltpu.VMEM((CHUNK * STATE, INNER), BF),
            chunk_f32,
            chunk_f32,
            chunk_f32,
            chunk_f32,
            pltpu.VMEM((CHUNK + 8, INNER), F32),
            pltpu.VMEM((CHUNK + 8, INNER), F32),
            pltpu.VMEM((CHUNK, wide), BF),
            pltpu.VMEM((CHUNK // GROUP, 2 * GROUP, wide), BF),
            pltpu.VMEM((STATE, INNER), F32),
        ],
        compiler_params=pltpu.CompilerParams(vmem_limit_bytes=62 * 2**20),
    )(*operands)


def layer_grads(results, complement_map):
    gwin, gwout, gsmall, gvec, ggain = results
    vec = jnp.sum(gvec, axis=1)
    return [
        gwin[0] + jnp.take(gwin[1], complement_map, axis=0),
        gsmall[2 * STATE :].T,
        gsmall[STATE : 2 * STATE],
        gwout[0] + jnp.take(gwout[1], complement_map, axis=1),
        vec[:KERNEL].T,
        vec[4],
        vec[5],
        gsmall[:STATE].T,
        vec[6],
        jnp.sum(ggain, axis=0),
    ]


def param_shapes():
    return [
        (D, 2 * INNER),
        (INNER, RANK + 2 * STATE),
        (RANK, INNER),
        (INNER, D),
        (INNER, KERNEL),
        (INNER,),
        (INNER,),
        (INNER, STATE),
        (INNER,),
        (D,),
    ]


def bounds():
    edges = [0]
    for shape in param_shapes():
        edges.append(edges[-1] + math.prod(shape))
    return edges


def slot_index(owners):
    count = owners.shape[0]
    order = jnp.arange(count, dtype=jnp.int32)
    same = (owners[None, :] == owners[:, None]) & (order[None, :] < order[:, None])
    return jnp.sum(same.astype(jnp.int32), axis=1)


def swap(value, axis, bit, size):
    return lax.ppermute(value, axis, [(i, i ^ bit) for i in range(size)])


def fine_blocks(block_len):
    edges = bounds()
    wanted = []
    for begin, end in ((edges[1], edges[3]), (edges[4], edges[10])):
        wanted.extend(range(begin // block_len, (end - 1) // block_len + 1))
    return sorted(set(wanted))


def gather_params(weights, owners, rank, matches):
    size = lax.axis_size("dp")
    me = lax.axis_index("dp")
    core = lax.axis_index("seq")
    block_len = weights.shape[1]
    half = block_len // 2
    mine = lax.dynamic_slice_in_dim(weights, core * half, half, 1)
    high, low = split_low(mine)
    special = fine_blocks(block_len)
    fine = jnp.sum(
        jnp.where(
            matches[:, special].T[:, :, None], low.astype(F32)[None], 0.0
        ),
        axis=1,
    ).astype(BF)
    many = high[None]
    spot = jnp.zeros_like(owners)
    bit = size // 2
    step = 0
    while bit:
        both = jnp.concatenate([many.reshape(-1, half), fine], axis=0)
        got = swap(both, "dp", bit, size)
        count = many.shape[0]
        many = jnp.concatenate([many, got[: count * SLOTS].reshape(count, SLOTS, half)], axis=0)
        fine = fine + got[count * SLOTS :]
        spot = spot + jnp.where(((owners ^ me) & bit) != 0, 1 << step, 0)
        step += 1
        bit //= 2
    rows = many.reshape(-1, half)[spot * SLOTS + rank]
    both = jnp.concatenate([rows, fine], axis=0)
    other = swap(both, "seq", 1, 2)
    first = jnp.where(core == 0, both, other)
    second = jnp.where(core == 0, other, both)
    full = jnp.concatenate([first, second], axis=1)
    blocks = owners.shape[0]
    return full[:blocks].reshape(-1), full[blocks:], special


def fine_range(table, special, block_len, begin, end):
    first, last = begin // block_len, (end - 1) // block_len
    rows = table[special.index(first) : special.index(last) + 1].reshape(-1)
    return rows[begin - first * block_len : end - first * block_len]


def on_device(
    inputs, cotangent, loss_mask, complement_map, owners, weights, first_moment, second_moment
):
    size = lax.axis_size("dp")
    me = lax.axis_index("dp")
    core = lax.axis_index("seq")
    blocks_count = owners.shape[0]
    block_len = weights.shape[1]
    half = block_len // 2
    upstream = cotangent * loss_mask.astype(BF)[..., None]
    sent = jnp.concatenate([inputs, upstream], axis=2)
    held = lax.all_to_all(sent, "seq", split_axis=0, concat_axis=1, tiled=True)
    x, up = held[:, :, :D], held[:, :, D:]

    rank = slot_index(owners)
    order = jnp.arange(blocks_count, dtype=jnp.int32)
    matches = (owners[None, :] == me) & (
        rank[None, :] == jnp.arange(SLOTS, dtype=jnp.int32)[:, None]
    )
    occupied = jnp.any(matches, axis=1)
    block_of = jnp.sum(jnp.where(matches, order[None, :], 0), axis=1)
    theta, fine, special = gather_params(weights, owners, rank, matches)
    edges = bounds()
    shapes = param_shapes()

    def high_of(index):
        return theta[edges[index] : edges[index + 1]].reshape(shapes[index])

    def low_of(index):
        return fine_range(fine, special, block_len, edges[index], edges[index + 1]).reshape(
            shapes[index]
        )

    def full_of(index):
        return high_of(index).astype(F32) + low_of(index).astype(F32)

    perm = (complement_map[:, None] == jnp.arange(D, dtype=jnp.int32)[None, :]).astype(BF)
    results = run_layer(
        x,
        up,
        high_of(0),
        (high_of(1), low_of(1)),
        (high_of(2), low_of(2)),
        high_of(3),
        *[full_of(index) for index in range(4, 10)],
        perm,
    )
    output, grad_input = results[:2]
    output = lax.all_to_all(output, "seq", split_axis=1, concat_axis=0, tiled=True)
    grad_input = lax.all_to_all(grad_input, "seq", split_axis=1, concat_axis=0, tiled=True)

    pieces = layer_grads(results[2:], complement_map)
    flat_grad = jnp.concatenate([item.reshape(-1) for item in pieces])
    grad_blocks = jnp.pad(flat_grad, (0, blocks_count * block_len - PARAMS)).reshape(
        blocks_count, block_len
    )
    given = lax.dynamic_slice_in_dim(grad_blocks, (1 - core) * half, half, 1)
    kept = lax.dynamic_slice_in_dim(grad_blocks, core * half, half, 1)
    chip = kept + swap(given, "seq", 1, 2)
    slot_of = owners * SLOTS + rank
    source = jnp.full((size * SLOTS,), blocks_count, jnp.int32).at[slot_of].set(order)
    padded = jnp.concatenate([chip.astype(BF), jnp.zeros((1, half), BF)], axis=0)
    routed = lax.all_to_all(padded[source], "dp", split_axis=0, concat_axis=0, tiled=True)
    owned_half = jnp.sum(routed.reshape(size, SLOTS, half).astype(F32), axis=0)
    other_half = swap(owned_half, "seq", 1, 2)
    owned = jnp.where(
        core == 0,
        jnp.concatenate([owned_half, other_half], axis=1),
        jnp.concatenate([other_half, owned_half], axis=1),
    )
    new_first = BETA_ONE * first_moment + (1.0 - BETA_ONE) * owned
    new_second = BETA_TWO * second_moment + (1.0 - BETA_TWO) * owned * owned
    position = block_of[:, None] * block_len + jnp.arange(block_len, dtype=jnp.int32)[None, :]
    is_matrix = position < MATRIX_END
    rate = jnp.where(is_matrix, RATE_MATRIX, RATE_VECTOR)
    decay = jnp.where(is_matrix, WEIGHT_DECAY, 0.0)
    corrected = (
        new_first
        / (1.0 - BETA_ONE**STEP_COUNT)
        / (jnp.sqrt(new_second / (1.0 - BETA_TWO**STEP_COUNT)) + ADAM_EPSILON)
    )
    new_theta = weights - rate * (corrected + decay * weights)
    keep = occupied[:, None]
    return (
        output,
        grad_input,
        jnp.where(keep, new_theta, 0.0),
        jnp.where(keep, new_first, 0.0),
        jnp.where(keep, new_second, 0.0),
    )


def solution(mesh):
    in_specs = (
        P("dp", "seq", None),
        P("dp", "seq", None),
        P("dp", "seq"),
        P(),
        P(),
        P("dp", None),
        P("dp", None),
        P("dp", None),
    )
    out_specs = (
        P("dp", "seq", None),
        P("dp", "seq", None),
        P("dp", None),
        P("dp", None),
        P("dp", None),
    )
    return jax.shard_map(
        on_device, mesh=mesh, in_specs=in_specs, out_specs=out_specs, check_vma=False
    )
```

time: 1870 us -> 499 us (0.27)
  other arithmetic: 741 us -> 23.9 us
  local copies, waits for them, and re-layouts: 684 us -> 127 us
  Pallas kernels: 0 us -> 262 us
  waiting for transfers between devices: 235 us -> 42 us
  matrix products: 101 us -> 1.66 us
  blocking collectives: 40.6 us -> 9.79 us
  loops' own time: 19 us -> 0 us
    reduce_sum x789 -> x6, other arithmetic: 428 us -> 2.67 us  [the longest x1 0.93 us: layer_grads(): vec = jnp.sum(gvec, axis=1)]
    pallas_call x0 -> x1, Pallas kernels: none -> 262 us  [run_layer(): pl.pallas_call(functools.partial(layer_kernel, chunks), grid=(windows, 2,...]
    rev x4 -> x1, local copies, waits for them, and re-layouts: 165 us -> 0.03 us  [run_layer(): flip = jnp.stack([jnp.eye(CHUNK, dtype=BF), jnp.eye(CHUNK, dtype=BF)[::-1]])]
    dynamic_update_slice x81 -> x0, other arithmetic: 156 us -> none  [the longest x80 156 us: scan_piece(): lax.scan(run_block, start, tuple((to_blocks(value) for value in (delta, a...]
    unnamed x6 -> x0, waiting for transfers between devices: 148 us -> none
    dot_general x15 -> x2, matrix products: 101 us -> 1.66 us  [the longest x1 1.25 us: dot(): return jnp.dot(a, b, preferred_element_type=F32)]
    squeeze x82 -> x3, local copies, waits for them, and re-layouts: 99.3 us -> 4.96 us  [the longest x1 2.7 us: layer_grads(): gwin[1]]
    mul x385 -> x2, other arithmetic: 82.7 us -> 2.17 us  [the longest x1 1.56 us: on_device(): upstream = cotangent * loss_mask.astype(BF)[..., None]]
  transfers between devices with their start and end apart: 5 -> 9, of which waited for: 3 -> 6; matrix products, arithmetic and copies ran while one was open for 6% -> 4% of each run, Pallas kernels for 0% -> 0%
where the time goes in v1:
time: 499 us; the launch traced here: 491 us
  Pallas kernels  262 us (53%)
  local copies, waits for them, and re-layouts  127 us (25%)
  waiting for transfers between devices  42 us (8%)
  other arithmetic  23.9 us (5%)
  starting transfers between devices  23.5 us (5%)
  blocking collectives  9.79 us (2%)
    pallas_call x1, Pallas kernels, run_layer(): pl.pallas_call(functools.partial(layer_kernel, chunks), grid=(windows, 2,...  262 us
    slice x13, local copies, waits for them, and re-layouts, high_of(): return theta[edges[index]:edges[index + 1]].reshape(shapes[index])  83.5 us
    ppermute x7, waiting for transfers between devices, swap(): return lax.ppermute(value, axis, [(i, i ^ bit) for i in range(size)])  23.3 us
    all_to_all x1, waiting for transfers between devices, on_device(): lax.all_to_all(padded[source], 'dp', split_axis=0, concat_axis=0, tiled=T...  18.6 us
    ppermute x7, starting transfers between devices, swap(): return lax.ppermute(value, axis, [(i, i ^ bit) for i in range(size)])  14 us
    unnamed x70, local copies, waits for them, and re-layouts  11.7 us
  transfers between devices with their start and end apart: 9, of which 6 were waited for; matrix products, arithmetic and copies ran while one was open for 4% of the time, Pallas kernels for 0%

profile of v1, /device:TPU:1, one launch (start us, length us, event | category | flops | bytes accessed | tf_op | source)
XLA Modules:
  0.0 491.3 jit_solution(15313604473300465850)
XLA Ops:
  0.6 1.7 constant_dynamic-update-slice_fusion.4
  7.2 3.2 collective-permute-start
  11.1 1.6 broadcast_multiply_fusion
  14.2 4.8 all-to-all-start
  23.3 1.7 copy.62
  28.5 5.1 %collective-permute-done.1 = bf16[12,6848]{1,0:T(8,128)(2,1)S(1)} collective-permute-done((bf16[12,6848]{1,0:T(8,128)(2,1)S(1)}, bf16[12,6848]{1,0:T(8,128)(2,1)S(1)}, u32[]{:S(2)}, u32[]{:S(2)}) %collective-permute-start.1) | collective-permute-done | bytes 164384 | tf_op jit(solution)/shard_map/ppermute | solution.py:537
  37.5 6.6 %collective-permute-done.2 = bf16[20,6848]{1,0:T(8,128)(2,1)S(1)} collective-permute-done((bf16[20,6848]{1,0:T(8,128)(2,1)S(1)}, bf16[20,6848]{1,0:T(8,128)(2,1)S(1)}, u32[]{:S(2)}, u32[]{:S(2)}) %collective-permute-start.2) | collective-permute-done | bytes 273952 | tf_op jit(solution)/shard_map/ppermute | solution.py:537
  48.4 10.3 %collective-permute-done.3 = bf16[36,6848]{1,0:T(8,128)(2,1)S(1)} collective-permute-done((bf16[36,6848]{1,0:T(8,128)(2,1)S(1)}, bf16[36,6848]{1,0:T(8,128)(2,1)S(1)}, u32[]{:S(2)}, u32[]{:S(2)}) %collective-permute-start.3) | collective-permute-done | bytes 493088 | tf_op jit(solution)/shard_map/ppermute | solution.py:537
  60.6 1.6 reshape.272
  64.1 2.7 collective-permute-start.4
  69.0 6.4 %slice.201 = bf16[27392,16]{1,0:T(8,128)(2,1)} reshape(bf16[32,13696]{1,0:T(8,128)(2,1)S(1)} %fusion.2) | data formatting | bytes 1753088 | tf_op jit(solution)/shard_map/slice | solution.py:618
  76.8 72.5 %slice.192 = bf16[109568,4]{1,0:T(8,128)(2,1)} reshape(bf16[32,13696]{1,0:T(8,128)(2,1)S(1)} %fusion.2) | data formatting | bytes 1753088 | tf_op jit(solution)/shard_map/slice | solution.py:618
  149.6 2.3 slice.184
  151.9 2.2 slice.181
  162.9 262.0 %shard_map.128 = (bf16[2,1024,256]{2,1,0:T(8,128)(2,1)}, f32[2,1024,256]{2,1,0:T(8,128)}, f32[2,256,1024]{2,1,0:T(8,128)}, f32[2,512,256]{2,1,0:T(8,128)}, f32[8...) custom-call(bf16[2,1024,256]{2,1,0:T(8,128)(2,1)} %get-tuple-element.24.x_ref, ...), custom_call_target="tpu_custom_call" | custom-call | tf_op jit(solution)/shard_map/pallas_call | solution.py:446
  428.1 2.7 slice_bitcast_fusion
  434.2 2.1 slice_bitcast_fusion.2
  446.9 4.7 all-to-all-start.3
  451.7 18.6 %all-to-all-done.3 = bf16[16,4,6848]{2,1,0:T(4,128)(2,1)S(1)} async-done(((bf16[16,4,6848]{2,1,0:T(4,128)(2,1)}), bf16[16,4,6848]{2,1,0:T(4,128)(2,1)S(1)}, u32[]{:S(2)}, u32[]{:S(2)}) %all-to-all-start.3) | async-done | bytes 876576 | tf_op jit(solution)/shard_map/all_to_all | solution.py:654
  470.7 3.7 collective-permute-start.6
  474.4 1.6 copy.70
  476.0 5.1 %all_to_all.63 = f32[2,1024,256]{2,0,1:T(2,128)S(1)} all-to-all(f32[2,1024,256]{2,0,1:T(2,128)S(1)} %copy.70), channel_id=1, replica_groups=mesh['dp'=16,'seq'=2] {'seq'}, dimensions={1} | all-to-all | bytes 4194304 | tf_op jit(solution)/shard_map/all_to_all | solution.py:641
  481.1 1.5 copy.71
  483.7 4.7 all_to_all.64
  (210 shorter events, 60.0 us)
Async XLA Ops:
  0.6 12.1 %copy-start.7 = (bf16[4,512,256]{2,1,0:T(8,128)(2,1)S(1)}, bf16[4,512,256]{2,1,0:T(8,128)(2,1)}, u32[]{:S(2)}) copy-start(bf16[4,512,256]{2,1,0:T(8,128)(2,1)} %param.9) | copy-start | bytes 3145732
  4.3 14.8 %copy-start.21 = (s32[32]{0:T(128)}, s32[32]{0:T(128)S(1)}, u32[]{:S(2)}) copy-start(s32[32]{0:T(128)S(1)} %convert_reduce_fusion.1) | copy-start | bytes 388
  7.2 19.0 %collective-permute-start = (bf16[8,6848]{1,0:T(8,128)(2,1)S(1)}, bf16[8,6848]{1,0:T(8,128)(2,1)S(1)}, u32[]{:S(2)}, u32[]{:S(2)}) collective-permute-start(bf16[8,6848]{1,0:T(8,128)(2,1)S(1)} %pad_maximum_fusion.9), channel_id=1, source_target_pairs={{0,16},{2,18},{4,20},{6,22},{8,24},{10,26},{12,28},{14,30},{16,0},... | collective-permute-start | bytes 328712 | tf_op jit(solution)/shard_map/ppermute | solution.py:537
  14.2 4.9 copy-start.23
  14.2 5.4 %copy-start.15 = (s32[256]{0:T(256)S(1)}, s32[256]{0:T(256)}, u32[]{:S(2)}) copy-start(s32[256]{0:T(256)} %param.12) | copy-start | bytes 3076
  14.2 7.7 %all-to-all-start = ((bf16[4,512,512]{2,1,0:T(8,128)(2,1)}), bf16[4,512,512]{2,1,0:T(8,128)(2,1)S(1)}, u32[]{:S(2)}, u32[]{:S(2)}) async-start(bf16[4,512,512]{2,1,0:T(8,128)(2,1)} %pad_maximum_fusion), calls=%async_computation | async-start | bytes 4194304 | tf_op jit(solution)/shard_map/all_to_all | solution.py:603
  26.5 7.1 %collective-permute-start.1 = (bf16[12,6848]{1,0:T(8,128)(2,1)S(1)}, bf16[12,6848]{1,0:T(8,128)(2,1)S(1)}, u32[]{:S(2)}, u32[]{:S(2)}) collective-permute-start(bf16[12,6848]{1,0:T(8,128)(2,1)S(1)} %pad_maximum_fusion.7), channel_id=1, source_target_pairs={{0,8},{2,10},{4,12},{6,14},{8,0},{10,2},{12,4},{14,6},{16,24},{18,... | collective-permute-start | bytes 493064 | tf_op jit(solution)/shard_map/ppermute | solution.py:537
  35.5 8.6 %collective-permute-start.2 = (bf16[20,6848]{1,0:T(8,128)(2,1)S(1)}, bf16[20,6848]{1,0:T(8,128)(2,1)S(1)}, u32[]{:S(2)}, u32[]{:S(2)}) collective-permute-start(bf16[20,6848]{1,0:T(8,128)(2,1)S(1)} %pad_maximum_fusion.6), channel_id=1, source_target_pairs={{0,4},{2,6},{4,0},{6,2},{8,12},{10,14},{12,8},{14,10},{16,20},{18,... | collective-permute-start | bytes 821768 | tf_op jit(solution)/shard_map/ppermute | solution.py:537
  46.4 12.4 %collective-permute-start.3 = (bf16[36,6848]{1,0:T(8,128)(2,1)S(1)}, bf16[36,6848]{1,0:T(8,128)(2,1)S(1)}, u32[]{:S(2)}, u32[]{:S(2)}) collective-permute-start(bf16[36,6848]{1,0:T(8,128)(2,1)S(1)} %pad_maximum_fusion.2), channel_id=1, source_target_pairs={{0,2},{2,0},{4,6},{6,4},{8,10},{10,8},{12,14},{14,12},{16,18},{18,... | collective-permute-start | bytes 1479176 | tf_op jit(solution)/shard_map/ppermute | solution.py:537
  64.1 4.3 collective-permute-start.4
  76.7 78.2 %copy-start.2 = (bf16[438272]{0:T(1024)(128)(2,1)}, bf16[438272]{0:T(1024)(128)(2,1)S(1)}, u32[]{:S(2)}) copy-start(bf16[438272]{0:T(1024)(128)(2,1)S(1)} %reshape.273) | copy-start | bytes 2629636
  151.9 2.5 slice-start
  154.5 3.3 copy-start.4
  159.5 2.7 copy-start.3
  441.8 2.5 collective-permute-start.5
  445.7 5.8 %copy-start.22 = (s32[32]{0:T(128)S(1)}, s32[32]{0:T(128)}, u32[]{:S(2)}) copy-start(s32[32]{0:T(128)} %copy-done.21) | copy-start | bytes 388
  445.7 5.8 %copy-start.25 = (pred[32]{0:T(512)(128)(4,1)S(1)}, pred[32]{0:T(512)(128)(4,1)}, u32[]{:S(2)}) copy-start(pred[32]{0:T(512)(128)(4,1)} %copy-done.24) | copy-start | bytes 100
  446.9 27.5 %copy-start.5 = (f32[2,1024,256]{2,1,0:T(8,128)S(1)}, f32[2,1024,256]{2,1,0:T(8,128)}, u32[]{:S(2)}) copy-start(f32[2,1024,256]{2,1,0:T(8,128)} %get-tuple-element.13) | copy-start | bytes 6291460
  446.9 23.4 %all-to-all-start.3 = ((bf16[16,4,6848]{2,1,0:T(4,128)(2,1)}), bf16[16,4,6848]{2,1,0:T(4,128)(2,1)S(1)}, u32[]{:S(2)}, u32[]{:S(2)}) async-start(bf16[16,4,6848]{2,1,0:T(4,128)(2,1)} %all_to_all.57), calls=%async_computation.3 | async-start | bytes 1769472 | tf_op jit(solution)/shard_map/all_to_all | solution.py:654
  470.7 18.9 %collective-permute-start.6 = (f32[4,6848]{1,0:T(4,128)S(1)}, f32[4,6848]{1,0:T(4,128)S(1)}, u32[]{:S(2)}, u32[]{:S(2)}) collective-permute-start(f32[4,6848]{1,0:T(4,128)S(1)} %convert_reduce_fusion), channel_id=1, source_target_pairs={{0,1},{1,0},{2,3},{3,2},{4,5},{5,4},{6,7},{7,6},{8,9},{9,8},{10,11... | collective-permute-start | bytes 328712 | tf_op jit(solution)/shard_map/ppermute | solution.py:537
  483.7 5.9 %copy-start.8 = (f32[4,13696]{1,0:T(4,128)S(1)}, f32[4,13696]{1,0:T(4,128)}, u32[]{:S(2)}) copy-start(f32[4,13696]{1,0:T(4,128)} %param.14) | copy-start | bytes 657412
  483.7 5.9 %copy-start.11 = (f32[4,13696]{1,0:T(4,128)S(1)}, f32[4,13696]{1,0:T(4,128)}, u32[]{:S(2)}) copy-start(f32[4,13696]{1,0:T(4,128)} %param.16) | copy-start | bytes 657412
  483.7 5.9 %copy-start.12 = (f32[4,13696]{1,0:T(4,128)S(1)}, f32[4,13696]{1,0:T(4,128)}, u32[]{:S(2)}) copy-start(f32[4,13696]{1,0:T(4,128)} %param.15) | copy-start | bytes 657412
  483.7 5.8 %copy-start.20 = (pred[4]{0:T(512)(128)(4,1)S(1)}, pred[4]{0:T(512)(128)(4,1)}, u32[]{:S(2)}) copy-start(pred[4]{0:T(512)(128)(4,1)} %get-tuple-element.50) | copy-start | bytes 16
  (14 other events, 17.3 us)

commit v2 on v1

--- a/solution.py
+++ b/solution.py
@@ -181,14 +181,12 @@
             gslope_s[a : a + block, :] = dgated * gsig * (1.0 + gate * (1.0 - gsig))
         halo_s[0:8, :] = halo_s[CHUNK : CHUNK + 8, :]
         act_high, act_low = split_low(act_s[here, :])
-        proj = dot(act_high, wx_ref[0]) + dot(act_low, wx_ref[0]) + dot(act_high, wx_ref[1])
+        proj = dot(act_high, wx_ref[...]) + dot(act_low, wx_ref[...])
         proj_s[here, :] = proj
         columns = jnp.transpose(proj)
         projt_s[chunk] = columns[: 3 * STATE]
         proj_high, proj_low = split_low(proj)
-        pre_all = (
-            dot(proj_high, wdt_ref[0]) + dot(proj_low, wdt_ref[0]) + dot(proj_high, wdt_ref[1])
-        )
+        pre_all = dot(proj_high, wdt_ref[...]) + dot(proj_low, wdt_ref[...])
         for a in pieces:
             pre = pre_all[a : a + block] + vec_ref[5:6, :]
             small = jnp.exp(-jnp.abs(pre))
@@ -332,9 +330,8 @@
             gvec_ref[6] += row_sum(dscan * act_s[here_a, :])
         dpre_high, dpre_low = split_low(gsilu_s[...])
         dproj = (
-            dot(dpre_high, wdt_ref[0], NT)
-            + dot(dpre_low, wdt_ref[0], NT)
-            + dot(dpre_high, wdt_ref[1], NT)
+            dot(dpre_high, wdt_ref[...], NT)
+            + dot(dpre_low, wdt_ref[...], NT)
             + dot(wide_s[...], fold_ref[0])
             + dread_s[here, :]
         )
@@ -342,11 +339,7 @@
         gsmall_ref[STATE : 2 * STATE, :] += dot(columns[:RANK].astype(BF), dpre_high)
         turned = jnp.transpose(dproj)[: 3 * STATE].astype(BF)
         gsmall_ref[2 * STATE : 5 * STATE, :] += dot(turned, act_s[here, :].astype(BF))
-        extra = (
-            dot(dproj_high, wx_ref[0], NT)
-            + dot(dproj_low, wx_ref[0], NT)
-            + dot(dproj_high, wx_ref[1], NT)
-        )
+        extra = dot(dproj_high, wx_ref[...], NT) + dot(dproj_low, wx_ref[...], NT)
         for a in pieces:
             dconv_s[a : a + block, :] = (
                 y_s[a : a + block, :] + extra[a : a + block]
@@ -389,8 +382,8 @@
     chunks = length // CHUNK
     w_in_pair = jnp.stack([w_in, dot(perm, w_in, TN).astype(BF)])
     w_out_pair = jnp.stack([w_out, dot(w_out, perm).astype(BF)])
-    wx_pair = jnp.pad(jnp.stack(w_x), ((0, 0), (0, 0), (0, LANES - w_x[0].shape[1])))
-    wdt_pair = jnp.pad(jnp.stack(w_dt), ((0, 0), (0, LANES - RANK), (0, 0)))
+    wx_wide = jnp.pad(w_x, ((0, 0), (0, LANES - w_x.shape[1])))
+    wdt_wide = jnp.pad(w_dt, ((0, LANES - RANK), (0, 0)))
     vec = jnp.concatenate(
         [conv_w.T, conv_b[None], dt_bias[None], d_skip[None], jnp.zeros((1, INNER), F32)], axis=0
     )
@@ -425,7 +418,7 @@
 
     piece = (1, CHUNK, D)
     operands = (
-        x, up, flip, w_in_pair, w_out_pair, wx_pair, wdt_pair, vec, rate, gain[None], tile, sums, fold, mask,
+        x, up, flip, w_in_pair, w_out_pair, wx_wide, wdt_wide, vec, rate, gain[None], tile, sums, fold, mask,
     )
     in_specs = [
         pl.BlockSpec(piece, of_chunk),
@@ -533,60 +526,110 @@
     return jnp.sum(same.astype(jnp.int32), axis=1)
 
 
-def swap(value, axis, bit, size):
+def swap(value, axis, bit):
+    size = lax.axis_size(axis)
     return lax.ppermute(value, axis, [(i, i ^ bit) for i in range(size)])
 
 
-def fine_blocks(block_len):
-    edges = bounds()
-    wanted = []
-    for begin, end in ((edges[1], edges[3]), (edges[4], edges[10])):
-        wanted.extend(range(begin // block_len, (end - 1) // block_len + 1))
-    return sorted(set(wanted))
+def up_to(value, multiple):
+    return -(-value // multiple) * multiple
+
+
+def pad_rows(value, rows, axis):
+    widths = [(0, 0)] * value.ndim
+    widths[axis] = (0, rows - value.shape[axis])
+    return jnp.pad(value, widths)
 
 
 def gather_params(weights, owners, rank, matches):
     size = lax.axis_size("dp")
     me = lax.axis_index("dp")
     core = lax.axis_index("seq")
-    block_len = weights.shape[1]
-    half = block_len // 2
-    mine = lax.dynamic_slice_in_dim(weights, core * half, half, 1)
-    high, low = split_low(mine)
-    special = fine_blocks(block_len)
-    fine = jnp.sum(
-        jnp.where(
-            matches[:, special].T[:, :, None], low.astype(F32)[None], 0.0
-        ),
-        axis=1,
-    ).astype(BF)
-    many = high[None]
+    blocks, block_len = owners.shape[0], weights.shape[1]
+    rows = block_len // LANES
+    padded = up_to(rows, 16)
+    near = min(4, size)
+    tiles = weights.reshape(SLOTS, rows, LANES)
+    rounded = lax.reduce_precision(tiles, 8, 7)
+    pair = SLOTS // 2
+    mine = lax.dynamic_slice_in_dim(rounded, core * pair, pair, 0).astype(BF)
+    many = pad_rows(mine, padded, 1).reshape(pair * padded, LANES)
+    first = MATRIX_END // block_len
+    last = (PARAMS - 1) // block_len + 1
+    here = matches[:, first:last].T[:, :, None, None]
+    fine = jnp.sum(jnp.where(here, (tiles - rounded)[None], 0.0), axis=1).astype(BF)
+    fine_rows = (last - first) * rows
+    fine_half = up_to(fine_rows, 32) // 2
+    fine = pad_rows(fine.reshape(fine_rows, LANES), 2 * fine_half, 0)
+    fine = lax.dynamic_slice_in_dim(fine, core * fine_half, fine_half, 0)
+    away = owners ^ me
     spot = jnp.zeros_like(owners)
-    bit = size // 2
-    step = 0
-    while bit:
-        both = jnp.concatenate([many.reshape(-1, half), fine], axis=0)
-        got = swap(both, "dp", bit, size)
+    bit, step = size // 2, 0
+    while bit >= near:
+        got = swap(jnp.concatenate([many, fine], axis=0), "dp", bit)
         count = many.shape[0]
-        many = jnp.concatenate([many, got[: count * SLOTS].reshape(count, SLOTS, half)], axis=0)
-        fine = fine + got[count * SLOTS :]
-        spot = spot + jnp.where(((owners ^ me) & bit) != 0, 1 << step, 0)
-        step += 1
-        bit //= 2
-    rows = many.reshape(-1, half)[spot * SLOTS + rank]
-    both = jnp.concatenate([rows, fine], axis=0)
-    other = swap(both, "seq", 1, 2)
-    first = jnp.where(core == 0, both, other)
-    second = jnp.where(core == 0, other, both)
-    full = jnp.concatenate([first, second], axis=1)
-    blocks = owners.shape[0]
-    return full[:blocks].reshape(-1), full[blocks:], special
-
-
-def fine_range(table, special, block_len, begin, end):
-    first, last = begin // block_len, (end - 1) // block_len
-    rows = table[special.index(first) : special.index(last) + 1].reshape(-1)
-    return rows[begin - first * block_len : end - first * block_len]
+        many = jnp.concatenate([many, got[:count]], axis=0)
+        fine = fine + got[count:]
+        spot = spot + jnp.where((away & bit) != 0, 1 << step, 0)
+        bit, step = bit // 2, step + 1
+    count = many.shape[0]
+    sent = jnp.concatenate([many, fine], axis=0)
+    others = [swap(sent, "dp", k) for k in range(1, near)]
+    many = jnp.stack([many] + [item[:count] for item in others])
+    for item in others:
+        fine = fine + item[count:]
+    spot = (spot + (away & (near - 1)) * (size // near)) * pair + rank % pair
+    chosen = many.reshape(size * pair, padded, LANES)[spot]
+    sent = jnp.concatenate([chosen.reshape(blocks * padded, LANES), fine], axis=0)
+    got = swap(sent, "seq", 1)
+    theirs = got[: blocks * padded].reshape(blocks, padded, LANES)
+    local = (rank // pair == core)[:, None, None]
+    theta = jnp.where(local, chosen, theirs)[:, :rows].reshape(blocks * rows, LANES)
+    fine_got = got[blocks * padded :]
+    fine = jnp.concatenate(
+        [jnp.where(core == 0, fine, fine_got), jnp.where(core == 0, fine_got, fine)], axis=0
+    )
+    begin = (MATRIX_END - first * block_len) // LANES
+    fine = fine[begin : begin + (PARAMS - MATRIX_END) // LANES]
+    return lax.optimization_barrier((theta, fine))
+
+
+def scatter_sum(value, size):
+    me = lax.axis_index("dp")
+    stride = 1
+    total = value
+    while stride < size:
+        radix = min(4, size // stride)
+        total = total.reshape((size // (stride * radix), radix) + value.shape[1:])
+        digit = (me // stride) % radix
+        low = total.astype(BF)
+        kept = lax.dynamic_index_in_dim(total, digit, 1, keepdims=False).astype(F32)
+        for k in range(1, radix):
+            given = lax.dynamic_index_in_dim(low, digit ^ k, 1, keepdims=False)
+            kept = kept + swap(given, "dp", k * stride).astype(F32)
+        total = kept
+        stride *= radix
+    return total[0]
+
+
+def trade(value, core):
+    half = value.shape[1] // 2
+    kept = lax.dynamic_slice_in_dim(value, core * half, half, 1)
+    given = lax.dynamic_slice_in_dim(value, (1 - core) * half, half, 1)
+    got = swap(given, "seq", 1)
+    return jnp.concatenate(
+        [jnp.where(core == 0, kept, got), jnp.where(core == 0, got, kept)], axis=0
+    )
+
+
+def untrade(value, core):
+    count = value.shape[0] // 2
+    kept = lax.dynamic_slice_in_dim(value, core * count, count, 0)
+    given = lax.dynamic_slice_in_dim(value, (1 - core) * count, count, 0)
+    got = swap(given, "seq", 1)
+    return jnp.concatenate(
+        [jnp.where(core == 0, kept, got), jnp.where(core == 0, got, kept)], axis=1
+    )
 
 
 def on_device(
@@ -595,70 +638,57 @@
     size = lax.axis_size("dp")
     me = lax.axis_index("dp")
     core = lax.axis_index("seq")
-    blocks_count = owners.shape[0]
-    block_len = weights.shape[1]
-    half = block_len // 2
-    upstream = cotangent * loss_mask.astype(BF)[..., None]
-    sent = jnp.concatenate([inputs, upstream], axis=2)
-    held = lax.all_to_all(sent, "seq", split_axis=0, concat_axis=1, tiled=True)
-    x, up = held[:, :, :D], held[:, :, D:]
-
+    blocks, block_len = owners.shape[0], weights.shape[1]
+    rows = block_len // LANES
+    pair = SLOTS // 2
     rank = slot_index(owners)
-    order = jnp.arange(blocks_count, dtype=jnp.int32)
+    order = jnp.arange(blocks, dtype=jnp.int32)
     matches = (owners[None, :] == me) & (
         rank[None, :] == jnp.arange(SLOTS, dtype=jnp.int32)[:, None]
     )
     occupied = jnp.any(matches, axis=1)
     block_of = jnp.sum(jnp.where(matches, order[None, :], 0), axis=1)
-    theta, fine, special = gather_params(weights, owners, rank, matches)
-    edges = bounds()
+    theta, fine = gather_params(weights, owners, rank, matches)
+    x = untrade(inputs, core)
+    up = untrade(cotangent * loss_mask.astype(BF)[..., None], core)
+
+    edges = [edge // LANES for edge in bounds()]
     shapes = param_shapes()
+    tail = edges[4]
 
     def high_of(index):
         return theta[edges[index] : edges[index + 1]].reshape(shapes[index])
 
-    def low_of(index):
-        return fine_range(fine, special, block_len, edges[index], edges[index + 1]).reshape(
-            shapes[index]
-        )
-
     def full_of(index):
-        return high_of(index).astype(F32) + low_of(index).astype(F32)
+        part = theta[edges[index] : edges[index + 1]].astype(F32)
+        part = part + fine[edges[index] - tail : edges[index + 1] - tail].astype(F32)
+        return part.reshape(shapes[index])
 
     perm = (complement_map[:, None] == jnp.arange(D, dtype=jnp.int32)[None, :]).astype(BF)
     results = run_layer(
-        x,
-        up,
-        high_of(0),
-        (high_of(1), low_of(1)),
-        (high_of(2), low_of(2)),
-        high_of(3),
-        *[full_of(index) for index in range(4, 10)],
-        perm,
-    )
-    output, grad_input = results[:2]
-    output = lax.all_to_all(output, "seq", split_axis=1, concat_axis=0, tiled=True)
-    grad_input = lax.all_to_all(grad_input, "seq", split_axis=1, concat_axis=0, tiled=True)
-
+        x, up, *[high_of(index) for index in range(4)], *[full_of(index) for index in range(4, 10)], perm
+    )
     pieces = layer_grads(results[2:], complement_map)
     flat_grad = jnp.concatenate([item.reshape(-1) for item in pieces])
-    grad_blocks = jnp.pad(flat_grad, (0, blocks_count * block_len - PARAMS)).reshape(
-        blocks_count, block_len
-    )
-    given = lax.dynamic_slice_in_dim(grad_blocks, (1 - core) * half, half, 1)
-    kept = lax.dynamic_slice_in_dim(grad_blocks, core * half, half, 1)
-    chip = kept + swap(given, "seq", 1, 2)
-    slot_of = owners * SLOTS + rank
-    source = jnp.full((size * SLOTS,), blocks_count, jnp.int32).at[slot_of].set(order)
-    padded = jnp.concatenate([chip.astype(BF), jnp.zeros((1, half), BF)], axis=0)
-    routed = lax.all_to_all(padded[source], "dp", split_axis=0, concat_axis=0, tiled=True)
-    owned_half = jnp.sum(routed.reshape(size, SLOTS, half).astype(F32), axis=0)
-    other_half = swap(owned_half, "seq", 1, 2)
-    owned = jnp.where(
-        core == 0,
-        jnp.concatenate([owned_half, other_half], axis=1),
-        jnp.concatenate([other_half, owned_half], axis=1),
-    )
+    flat_grad = jnp.pad(flat_grad, (0, (blocks + 1) * block_len - PARAMS))
+    grad_blocks = flat_grad.reshape(blocks + 1, rows, LANES)
+    source = jnp.full((size * SLOTS,), blocks, jnp.int32).at[owners * SLOTS + rank].set(order)
+    source = source.reshape(size, 2, pair)
+
+    def for_core(which):
+        index = lax.dynamic_index_in_dim(source, which, 1, keepdims=False)
+        return grad_blocks[index.reshape(-1)].reshape(size, pair, rows, LANES)
+
+    got = swap(for_core(1 - core).astype(BF), "seq", 1)
+    chip = (for_core(core) + got.astype(F32)).astype(BF)
+    chip = pad_rows(chip, up_to(rows, 16), 2).reshape(size, -1, LANES)
+    summed = scatter_sum(chip, size).reshape(pair, -1, LANES)[:, :rows]
+    other = swap(summed, "seq", 1)
+    owned = jnp.concatenate(
+        [jnp.where(core == 0, summed, other), jnp.where(core == 0, other, summed)], axis=0
+    ).reshape(SLOTS, block_len)
+    output = trade(results[0], core)
+    grad_input = trade(results[1], core)
     new_first = BETA_ONE * first_moment + (1.0 - BETA_ONE) * owned
     new_second = BETA_TWO * second_moment + (1.0 - BETA_TWO) * owned * owned
     position = block_of[:, None] * block_len + jnp.arange(block_len, dtype=jnp.int32)[None, :]

time: 499 us -> 373 us (0.75); the launches traced: 491 us -> 372 us
  local copies, waits for them, and re-layouts: 127 us -> 37.4 us
  waiting for transfers between devices: 42 us -> 23 us
  blocking collectives: 9.79 us -> 0 us
  other arithmetic: 23.9 us -> 31.1 us
    slice x13 -> x6, local copies, waits for them, and re-layouts: 83.5 us -> 0.07 us  [high_of(): return theta[edges[index]:edges[index + 1]].reshape(shapes[index])]
    all_to_all x2 -> x0, waiting for transfers between devices: 18.6 us -> none  [the longest x1 18.6 us: on_device(): lax.all_to_all(padded[source], 'dp', split_axis=0, concat_axis=0, tiled=T...]
    all_to_all x2 -> x0, blocking collectives: 9.79 us -> none  [the longest x1 5.08 us: on_device(): lax.all_to_all(grad_input, 'seq', split_axis=1, concat_axis=0, tiled=True)]
    all_to_all x2 -> x0, starting transfers between devices: 9.52 us -> none  [the longest x1 4.84 us: on_device(): held = lax.all_to_all(sent, 'seq', split_axis=0, concat_axis=1, tiled=True)]
    all_to_all x4 -> x0, local copies, waits for them, and re-layouts: 5.47 us -> none  [the longest x1 1.73 us: on_device(): held = lax.all_to_all(sent, 'seq', split_axis=0, concat_axis=1, tiled=True)]
    unnamed x70 -> x76, local copies, waits for them, and re-layouts: 11.7 us -> 6.24 us
    ppermute x7 -> x18, starting transfers between devices: 14 us -> 19.4 us  [swap(): return lax.ppermute(value, axis, [(i, i ^ bit) for i in range(size)])]
    ppermute x7 -> x18, waiting for transfers between devices: 23.3 us -> 23 us  [swap(): return lax.ppermute(value, axis, [(i, i ^ bit) for i in range(size)])]
  transfers between devices with their start and end apart: 9 -> 18, of which waited for: 6 -> 7; matrix products, arithmetic and copies ran while one was open for 4% -> 8% of each run, Pallas kernels for 0% -> 0%
where the time goes in v2:
time: 373 us; the launch traced here: 372 us
  Pallas kernels  259 us (69%)
  local copies, waits for them, and re-layouts  37.4 us (10%)
  other arithmetic  31.1 us (8%)
  waiting for transfers between devices  23 us (6%)
  starting transfers between devices  19.4 us (5%)
    pallas_call x1, Pallas kernels, run_layer(): pl.pallas_call(functools.partial(layer_kernel, chunks), grid=(windows, 2,...  259 us
    ppermute x18, waiting for transfers between devices, swap(): return lax.ppermute(value, axis, [(i, i ^ bit) for i in range(size)])  23 us
    ppermute x18, starting transfers between devices, swap(): return lax.ppermute(value, axis, [(i, i ^ bit) for i in range(size)])  19.4 us
  transfers between devices with their start and end apart: 18, of which 7 were waited for; matrix products, arithmetic and copies ran while one was open for 8% of the time, Pallas kernels for 0%

profile of v2, /device:TPU:1, one launch (start us, length us, event | category | flops | bytes accessed | tf_op | source)
XLA Modules:
  0.0 371.7 jit_solution(3132801108720170042)
XLA Ops:
  5.3 3.2 collective-permute-start.2
  9.2 1.6 broadcast_multiply_fusion
  17.7 1.4 collective-permute-start.3
  19.7 2.6 collective-permute-done.3
  22.3 2.2 collective-permute-start.6
  26.4 3.0 collective-permute-done.6
  30.1 6.0 %collective-permute-done.5 = bf16[960,128]{1,0:T(8,128)(2,1)S(1)} collective-permute-done((bf16[960,128]{1,0:T(8,128)(2,1)S(1)}, bf16[960,128]{1,0:T(8,128)(2,1)S(1)}, u32[]{:S(2)}, u32[]{:S(2)}) %collective-permute-start.5) | collective-permute-done | bytes 245792 | tf_op jit(solution)/shard_map/ppermute | solution.py:531
  41.7 1.7 copy.73.tile_ref
  43.3 1.4 rev.3
  44.7 1.4 pad_maximum_fusion.11.flip_ref
  60.6 258.5 %shard_map.119 = (bf16[2,1024,256]{2,1,0:T(8,128)(2,1)}, f32[2,1024,256]{2,1,0:T(8,128)}, f32[2,256,1024]{2,1,0:T(8,128)}, f32[2,512,256]{2,1,0:T(8,128)}, f32[8...) custom-call(bf16[2,1024,256]{2,1,0:T(8,128)(2,1)} %pad_maximum_fusion.1.x_ref, ...), custom_call_target="tpu_custom_call" | custom-call | tf_op jit(solution)/shard_map/pallas_call | solution.py:439
  322.3 2.7 slice_bitcast_fusion
  328.5 2.1 slice_bitcast_fusion.2
  335.1 1.4 pad.28
  336.5 1.7 reshape.353
  340.5 1.9 gather_fusion.3
  344.6 1.4 add_convert_fusion
  350.2 2.8 collective-permute-done.11
  353.9 5.0 %collective-permute-done.13 = bf16[4,224,128]{2,1,0:T(8,128)(2,1)S(1)} collective-permute-done((bf16[4,224,128]{2,1,0:T(8,128)(2,1)S(1)}, bf16[4,224,128]{2,1,0:T(8,128)(2,1)S(1)}, u32[]{:S(2)}, u32[]{:S(2)}) %collective-permute-start.13) | collective-permute-done | bytes 229408 | tf_op jit(solution)/shard_map/ppermute | solution.py:531
  360.5 2.2 collective-permute-start.16
  362.9 2.6 collective-permute-done.15
  365.6 3.2 collective-permute-start.17
  368.8 1.5 pad_maximum_fusion
  370.4 1.4 broadcast_select_fusion.7
  (228 shorter events, 57.3 us)
Async XLA Ops:
  1.5 11.9 %copy-start.26 = (s32[32]{0:T(128)}, s32[32]{0:T(128)S(1)}, u32[]{:S(2)}) copy-start(s32[32]{0:T(128)S(1)} %convert_reduce_fusion) | copy-start | bytes 388
  5.2 7.4 %copy-start.5 = (bf16[4,512,256]{2,1,0:T(8,128)(2,1)S(1)}, bf16[4,512,256]{2,1,0:T(8,128)(2,1)}, u32[]{:S(2)}) copy-start(bf16[4,512,256]{2,1,0:T(8,128)(2,1)} %param.8) | copy-start | bytes 3145732
  5.3 12.3 %collective-permute-start.2 = (bf16[288,128]{1,0:T(8,128)(2,1)S(1)}, bf16[288,128]{1,0:T(8,128)(2,1)S(1)}, u32[]{:S(2)}, u32[]{:S(2)}) collective-permute-start(bf16[288,128]{1,0:T(8,128)(2,1)S(1)} %pad_maximum_fusion.10), channel_id=1, source_target_pairs={{0,16},{2,18},{4,20},{6,22},{8,24},{10,26},{12,28},{14,30},{16,0},... | collective-permute-start | bytes 221192 | tf_op jit(solution)/shard_map/ppermute | solution.py:531
  9.2 4.2 %copy-start.29 = (s32[32]{0:T(128)S(1)}, s32[32]{0:T(128)}, u32[]{:S(2)}) copy-start(s32[32]{0:T(128)} %param.12) | copy-start | bytes 388
  9.2 5.4 %copy-start.15 = (s32[256]{0:T(256)S(1)}, s32[256]{0:T(256)}, u32[]{:S(2)}) copy-start(s32[256]{0:T(256)} %param.11) | copy-start | bytes 3076
  11.6 35.7 %collective-permute-start.1 = (bf16[2,512,256]{2,1,0:T(8,128)(2,1)}, bf16[2,512,256]{2,1,0:T(8,128)(2,1)S(1)}, u32[]{:S(2)}, u32[]{:S(2)}) collective-permute-start(bf16[2,512,256]{2,1,0:T(8,128)(2,1)} %constant_dynamic-slice_fusion.5), channel_id=1, source_target_pairs={{0,1},{1,0},{2,3},{3,2},{4,5},{5,4},{6,7},{7,6},{8,9},{9,8},{10,11... | collective-permute-start | bytes 1572872 | tf_op jit(solution)/shard_map/ppermute | solution.py:531
  13.4 33.9 %collective-permute-start = (bf16[2,512,256]{2,1,0:T(8,128)(2,1)}, bf16[2,512,256]{2,1,0:T(8,128)(2,1)}, u32[]{:S(2)}, u32[]{:S(2)}) collective-permute-start(bf16[2,512,256]{2,1,0:T(8,128)(2,1)} %constant_dynamic-slice_fusion.6), channel_id=1, source_target_pairs={{0,1},{1,0},{2,3},{3,2},{4,5},{5,4},{6,7},{7,6},{8,9},{9,8},{10,11... | collective-permute-start | bytes 1572872 | tf_op jit(solution)/shard_map/ppermute | solution.py:531
  17.7 4.6 %collective-permute-start.3 = (bf16[512,128]{1,0:T(8,128)(2,1)S(1)}, bf16[512,128]{1,0:T(8,128)(2,1)S(1)}, u32[]{:S(2)}, u32[]{:S(2)}) collective-permute-start(bf16[512,128]{1,0:T(8,128)(2,1)S(1)} %pad_maximum_fusion.9), channel_id=1, source_target_pairs={{0,8},{2,10},{4,12},{6,14},{8,0},{10,2},{12,4},{14,6},{16,24},{18,... | collective-permute-start | bytes 393224 | tf_op jit(solution)/shard_map/ppermute | solution.py:531
  22.3 7.1 %collective-permute-start.6 = (bf16[960,128]{1,0:T(8,128)(2,1)S(1)}, bf16[960,128]{1,0:T(8,128)(2,1)S(1)}, u32[]{:S(2)}, u32[]{:S(2)}) collective-permute-start(bf16[960,128]{1,0:T(8,128)(2,1)S(1)} %pad_maximum_fusion.8), channel_id=1, source_target_pairs={{0,6},{2,4},{4,2},{6,0},{8,14},{10,12},{12,10},{14,8},{16,22},{18,... | collective-permute-start | bytes 737288 | tf_op jit(solution)/shard_map/ppermute | solution.py:531
  25.9 10.2 %collective-permute-start.5 = (bf16[960,128]{1,0:T(8,128)(2,1)S(1)}, bf16[960,128]{1,0:T(8,128)(2,1)S(1)}, u32[]{:S(2)}, u32[]{:S(2)}) collective-permute-start(bf16[960,128]{1,0:T(8,128)(2,1)S(1)} %pad_maximum_fusion.8), channel_id=1, source_target_pairs={{0,4},{2,6},{4,0},{6,2},{8,12},{10,14},{12,8},{14,10},{16,20},{18,... | collective-permute-start | bytes 737288 | tf_op jit(solution)/shard_map/ppermute | solution.py:531
  26.1 10.0 %collective-permute-start.4 = (bf16[960,128]{1,0:T(8,128)(2,1)S(1)}, bf16[960,128]{1,0:T(8,128)(2,1)S(1)}, u32[]{:S(2)}, u32[]{:S(2)}) collective-permute-start(bf16[960,128]{1,0:T(8,128)(2,1)S(1)} %pad_maximum_fusion.8), channel_id=1, source_target_pairs={{0,2},{2,0},{4,6},{6,4},{8,10},{10,8},{12,14},{14,12},{16,18},{18,... | collective-permute-start | bytes 737288 | tf_op jit(solution)/shard_map/ppermute | solution.py:531
  38.3 9.0 %copy-start.6 = (bf16[4,512,256]{2,1,0:T(8,128)(2,1)S(1)}, bf16[4,512,256]{2,1,0:T(8,128)(2,1)}, u32[]{:S(2)}) copy-start(bf16[4,512,256]{2,1,0:T(8,128)(2,1)} %param.8) | copy-start | bytes 3145732
  40.2 10.4 %collective-permute-start.7 = (bf16[3648,128]{1,0:T(8,128)(2,1)}, bf16[3648,128]{1,0:T(8,128)(2,1)}, u32[]{:S(2)}, u32[]{:S(2)}) collective-permute-start(bf16[3648,128]{1,0:T(8,128)(2,1)} %pad_maximum_fusion.5), channel_id=1, source_target_pairs={{0,1},{1,0},{2,3},{3,2},{4,5},{5,4},{6,7},{7,6},{8,9},{9,8},{10,11... | collective-permute-start | bytes 2801672 | tf_op jit(solution)/shard_map/ppermute | solution.py:531
  340.4 4.2 %collective-permute-start.10 = (bf16[16,2,107,128]{3,0,2,1:T(8,128)(2,1)}, bf16[16,2,107,128]{3,0,2,1:T(8,128)(2,1)}, u32[]{:S(2)}, u32[]{:S(2)}) collective-permute-start(bf16[16,2,107,128]{3,0,2,1:T(8,128)(2,1)} %copy.80), channel_id=1, source_target_pairs={{0,1},{1,0},{2,3},{3,2},{4,5},{5,4},{6,7},{7,6},{8,9},{9,8},{10,11... | collective-permute-start | bytes 2629640 | tf_op jit(solution)/shard_map/ppermute | solution.py:531
  342.5 6.4 %collective-permute-start.8 = (bf16[2,512,256]{2,1,0:T(8,128)(2,1)S(1)}, bf16[2,512,256]{2,1,0:T(8,128)(2,1)S(1)}, u32[]{:S(2)}, u32[]{:S(2)}) collective-permute-start(bf16[2,512,256]{2,1,0:T(8,128)(2,1)S(1)} %constant_dynamic-slice_fusion.4), channel_id=1, source_target_pairs={{0,1},{1,0},{2,3},{3,2},{4,5},{5,4},{6,7},{7,6},{8,9},{9,8},{10,11... | collective-permute-start | bytes 1572872 | tf_op jit(solution)/shard_map/ppermute | solution.py:531
  344.3 18.4 %collective-permute-start.9 = (f32[2,512,256]{2,1,0:T(8,128)S(1)}, f32[2,512,256]{2,1,0:T(8,128)S(1)}, u32[]{:S(2)}, u32[]{:S(2)}) collective-permute-start(f32[2,512,256]{2,1,0:T(8,128)S(1)} %constant_dynamic-slice_fusion.3), channel_id=1, source_target_pairs={{0,1},{1,0},{2,3},{3,2},{4,5},{5,4},{6,7},{7,6},{8,9},{9,8},{10,11... | collective-permute-start | bytes 3145736 | tf_op jit(solution)/shard_map/ppermute | solution.py:531
  346.1 6.9 %collective-permute-start.11 = (bf16[4,224,128]{2,1,0:T(8,128)(2,1)S(1)}, bf16[4,224,128]{2,1,0:T(8,128)(2,1)S(1)}, u32[]{:S(2)}, u32[]{:S(2)}) collective-permute-start(bf16[4,224,128]{2,1,0:T(8,128)(2,1)S(1)} %get-tuple-element.41), channel_id=1, source_target_pairs={{0,2},{2,0},{4,6},{6,4},{8,10},{10,8},{12,14},{14,12},{16,18},{18,... | collective-permute-start | bytes 688136 | tf_op jit(solution)/shard_map/ppermute | solution.py:531
  347.4 6.5 %collective-permute-start.12 = (bf16[4,224,128]{2,1,0:T(8,128)(2,1)S(1)}, bf16[4,224,128]{2,1,0:T(8,128)(2,1)S(1)}, u32[]{:S(2)}, u32[]{:S(2)}) collective-permute-start(bf16[4,224,128]{2,1,0:T(8,128)(2,1)S(1)} %get-tuple-element.43), channel_id=1, source_target_pairs={{0,4},{2,6},{4,0},{6,2},{8,12},{10,14},{12,8},{14,10},{16,20},{18,... | collective-permute-start | bytes 688136 | tf_op jit(solution)/shard_map/ppermute | solution.py:531
  348.6 10.3 %collective-permute-start.13 = (bf16[4,224,128]{2,1,0:T(8,128)(2,1)S(1)}, bf16[4,224,128]{2,1,0:T(8,128)(2,1)S(1)}, u32[]{:S(2)}, u32[]{:S(2)}) collective-permute-start(bf16[4,224,128]{2,1,0:T(8,128)(2,1)S(1)} %get-tuple-element.42), channel_id=1, source_target_pairs={{0,6},{2,4},{4,2},{6,0},{8,14},{10,12},{12,10},{14,8},{16,22},{18,... | collective-permute-start | bytes 688136 | tf_op jit(solution)/shard_map/ppermute | solution.py:531
  349.1 13.6 %copy-start.3 = (f32[2,1024,256]{2,1,0:T(8,128)S(1)}, f32[2,1024,256]{2,1,0:T(8,128)}, u32[]{:S(2)}) copy-start(f32[2,1024,256]{2,1,0:T(8,128)} %get-tuple-element.17) | copy-start | bytes 6291460
  359.1 3.8 %collective-permute-start.14 = (bf16[1,224,128]{2,1,0:T(8,128)(2,1)S(1)}, bf16[1,224,128]{2,1,0:T(8,128)(2,1)S(1)}, u32[]{:S(2)}, u32[]{:S(2)}) collective-permute-start(bf16[1,224,128]{2,1,0:T(8,128)(2,1)S(1)} %get-tuple-element.52), channel_id=1, source_target_pairs={{0,8},{2,10},{4,12},{6,14},{8,0},{10,2},{12,4},{14,6},{16,24},{18,... | collective-permute-start | bytes 172040 | tf_op jit(solution)/shard_map/ppermute | solution.py:531
  360.5 5.1 %collective-permute-start.15 = (bf16[1,224,128]{2,1,0:T(8,128)(2,1)S(1)}, bf16[1,224,128]{2,1,0:T(8,128)(2,1)S(1)}, u32[]{:S(2)}, u32[]{:S(2)}) collective-permute-start(bf16[1,224,128]{2,1,0:T(8,128)(2,1)S(1)} %get-tuple-element.54), channel_id=1, source_target_pairs={{0,16},{2,18},{4,20},{6,22},{8,24},{10,26},{12,28},{14,30},{16,0},... | collective-permute-start | bytes 172040 | tf_op jit(solution)/shard_map/ppermute | solution.py:531
  360.5 5.0 %collective-permute-start.16 = (bf16[1,224,128]{2,1,0:T(8,128)(2,1)S(1)}, bf16[1,224,128]{2,1,0:T(8,128)(2,1)S(1)}, u32[]{:S(2)}, u32[]{:S(2)}) collective-permute-start(bf16[1,224,128]{2,1,0:T(8,128)(2,1)S(1)} %get-tuple-element.53), channel_id=1, source_target_pairs={{0,24},{2,26},{4,28},{6,30},{8,16},{10,18},{12,20},{14,22},{16,8},... | collective-permute-start | bytes 172040 | tf_op jit(solution)/shard_map/ppermute | solution.py:531
  365.6 4.7 %collective-permute-start.17 = (f32[2,107,128]{2,1,0:T(8,128)S(1)}, f32[2,107,128]{2,1,0:T(8,128)S(1)}, u32[]{:S(2)}, u32[]{:S(2)}) collective-permute-start(f32[2,107,128]{2,1,0:T(8,128)S(1)} %bitcast.111), channel_id=1, source_target_pairs={{0,1},{1,0},{2,3},{3,2},{4,5},{5,4},{6,7},{7,6},{8,9},{9,8},{10,11... | collective-permute-start | bytes 328712 | tf_op jit(solution)/shard_map/ppermute | solution.py:531
  (28 other events, 44.8 us)

commit v3 on v2

v3 whole, which is shorter than its diff:
```python
import functools
import math

import jax
import jax.numpy as jnp
from jax import lax
from jax.experimental import pallas as pl
from jax.experimental.pallas import tpu as pltpu
from jax.sharding import PartitionSpec as P

D = 256
INNER = 512
STATE = 16
RANK = 16
KERNEL = 4
SLOTS = 4
STEP_COUNT = 10
PARAMS = 438016
MATRIX_END = 425984
BETA_ONE = 0.9
BETA_TWO = 0.95
ADAM_EPSILON = 1e-08
RATE_MATRIX = 0.1
RATE_VECTOR = 0.5
WEIGHT_DECAY = 0.1
NORM_EPSILON = 1e-05
LOG2E = 1.4426950408889634
LN2 = 0.6931471805599453
CHUNK = 128
GROUP = 16
SLAB = 512
BLOCK = 32
LANES = 128
WIDE = GROUP * STATE
BF = jnp.bfloat16
F32 = jnp.float32
NT = (((1,), (1,)), ((), ()))
TN = (((0,), (0,)), ((), ()))


def split_low(value):
    high = value.astype(BF)
    return high, (value - high.astype(F32)).astype(BF)


def dot(a, b, dims=None):
    if dims is None:
        return jnp.dot(a, b, preferred_element_type=F32)
    return lax.dot_general(a, b, dims, preferred_element_type=F32)


def row_sum(value):
    return jnp.sum(value.reshape(value.shape[0] // 8, 8, value.shape[1]), axis=0)


def span(start, count, step=None):
    return pl.ds(pl.multiple_of(start, step or count), count)


def iota(shape, axis):
    return lax.broadcasted_iota(jnp.int32, shape, axis)


def spread(value, index):
    return jnp.broadcast_to(value[index : index + 1, :], (8, LANES))


def each(count, body):
    lax.fori_loop(0, count, lambda i, c: (body(i), c)[1], 0)


def layer_kernel(
    core_ref,
    x_kept_ref,
    x_got_ref,
    up_kept_ref,
    up_got_ref,
    perm_ref,
    w_in_ref,
    w_out_ref,
    wx_ref,
    wdt_ref,
    vec_ref,
    rate_ref,
    gain_ref,
    out_ref,
    gin_ref,
    gwin_ref,
    gwout_ref,
    gsmall_ref,
    gvec_ref,
    ggain_ref,
    states,
    act_s,
    slope_s,
    delta_s,
    ratio_s,
    dscan_s,
    u_s,
    y_s,
    gsilu_s,
    gslope_s,
    inner_s,
    proj_s,
    dread_s,
    projt_s,
    dproj_s,
    gated_s,
    copy_s,
    dmix_s,
    x_s,
    up_s,
    mixed_s,
    dnorm_s,
    wide_s,
    read_s,
    entry_s,
    w_in_s,
    w_out_s,
    flip_s,
    tile_s,
    fold_s,
    sums_s,
    mask_s,
    near_s,
):
    window = pl.program_id(0)
    natural = pl.program_id(1)
    core = core_ref[0]
    length = x_s.shape[0]
    half = length // 2
    chunks = length // CHUNK
    slabs = length // SLAB
    groups = CHUNK // GROUP
    pieces = range(0, SLAB, BLOCK)

    @pl.when((window == 0) & (natural == 0))
    def _():
        gwin_ref[...] = jnp.zeros_like(gwin_ref)
        gwout_ref[...] = jnp.zeros_like(gwout_ref)
        gsmall_ref[...] = jnp.zeros_like(gsmall_ref)
        gvec_ref[...] = jnp.zeros_like(gvec_ref)
        ggain_ref[...] = jnp.zeros_like(ggain_ref)
        inner_s[0:8, :] = jnp.zeros((8, INNER), F32)
        gsilu_s[length : length + 8, :] = jnp.zeros((8, INNER), F32)
        rows, lanes = iota((CHUNK, CHUNK), 0), iota((CHUNK, CHUNK), 1)
        flip_s[1] = jnp.where(rows == lanes, 1.0, 0.0).astype(BF)
        flip_s[0] = jnp.where(rows + lanes == CHUNK - 1, 1.0, 0.0).astype(BF)
        rows, lanes = iota((LANES, WIDE), 0), iota((LANES, WIDE), 1)
        for k in range(2):
            tile_s[k] = jnp.where(rows == STATE * (k + 1) + lanes % STATE, 1.0, 0.0).astype(BF)
        rows, lanes = iota((WIDE, LANES), 0), iota((WIDE, LANES), 1)
        for k in range(2):
            fold_s[k] = jnp.where(lanes == STATE * (k + 1) + rows % STATE, 1.0, 0.0).astype(BF)
        rows, lanes = iota((GROUP, WIDE), 0), iota((GROUP, WIDE), 1)
        mask = jnp.where(rows == lanes // STATE, 1.0, 0.0)
        mask_s[...] = mask
        sums_s[:GROUP, :] = mask.astype(BF)
        sums_s[GROUP:, :] = jnp.where(rows == lanes % STATE, 1.0, 0.0).astype(BF)

    @pl.when(natural == 0)
    def _():
        kept, got = span(core * half, half), span((1 - core) * half, half)
        x_s[kept, :] = x_kept_ref[0]
        x_s[got, :] = x_got_ref[0]
        up_s[kept, :] = up_kept_ref[0]
        up_s[got, :] = up_got_ref[0]
        w_in_s[...] = dot(perm_ref[...], w_in_ref[...], TN).astype(BF)
        w_out_s[...] = dot(w_out_ref[...], perm_ref[...]).astype(BF)

    @pl.when(natural == 1)
    def _():
        w_in_s[...] = w_in_ref[...]
        w_out_s[...] = w_out_ref[...]

    def place_of(chunk):
        return jnp.where(natural == 1, chunk, chunks - 1 - chunk) * CHUNK

    def norm_parts(rows):
        xf = x_s[rows, :].astype(F32)
        inv = lax.rsqrt(jnp.mean(xf * xf, axis=-1, keepdims=True) + NORM_EPSILON)
        return xf, inv

    def load_copies(chunk):
        there = span(place_of(chunk), CHUNK)
        xf, inv = norm_parts(there)
        normed = (xf * inv * gain_ref[...]).astype(BF)
        copy_s[span(chunk * CHUNK, CHUNK), :] = dot(flip_s[natural], normed).astype(BF)
        dmix_s[span(chunk * CHUNK, CHUNK), :] = dot(flip_s[natural], up_s[there, :]).astype(BF)

    each(chunks, load_copies)

    def project(slab):
        row = slab * SLAB
        copy = copy_s[span(row, SLAB), :]
        inner_s[span(row + 8, SLAB, 8), :] = (
            dot(copy, w_in_s[:, :INNER]).astype(BF).astype(F32)
        )
        gate_all = dot(copy, w_in_s[:, INNER:])
        dgated_all = dot(dmix_s[span(row, SLAB), :], w_out_s[...], NT)
        for a in pieces:
            rows = span(row + a, BLOCK)
            gate = gate_all[a : a + BLOCK].astype(BF).astype(F32)
            dgated = dgated_all[a : a + BLOCK].astype(BF).astype(F32)
            sig = 1.0 / (1.0 + jnp.exp(-gate))
            silu = gate * sig
            gsilu_s[rows, :] = silu
            dscan_s[rows, :] = dgated * silu
            gslope_s[rows, :] = dgated * (sig + silu * (1.0 - sig))

    each(slabs, project)

    def convolve(slab):
        row = slab * SLAB
        near_s[...] = inner_s[span(row, SLAB + 8, 8), :]
        for a in pieces:
            rows = span(row + a, BLOCK)
            conv = vec_ref[4:5, :]
            for j in range(KERNEL):
                conv = conv + vec_ref[j : j + 1, :] * near_s[a + 5 + j : a + 5 + j + BLOCK, :]
            sig = 1.0 / (1.0 + jnp.exp(-conv))
            act = conv * sig
            act_s[rows, :] = act
            slope_s[rows, :] = sig + act * (1.0 - sig)
        act_high, act_low = split_low(act_s[span(row, SLAB), :])
        proj = dot(act_high, wx_ref[...]) + dot(act_low, wx_ref[...])
        proj_s[span(row, SLAB), :] = proj
        for k in range(SLAB // CHUNK):
            turned = jnp.transpose(proj[k * CHUNK : (k + 1) * CHUNK])
            projt_s[slab * (SLAB // CHUNK) + k] = turned[: 3 * STATE]
        proj_high, proj_low = split_low(proj)
        for kind, target in ((0, entry_s), (1, read_s)):
            wide = dot(proj_high, tile_s[kind])
            for g in range(SLAB // GROUP):
                part = wide[g * GROUP : (g + 1) * GROUP] * mask_s[...]
                target[span(row + g * GROUP, GROUP), :] = part.astype(BF)
        pre_all = dot(proj_high, wdt_ref[...]) + dot(proj_low, wdt_ref[...])
        for a in pieces:
            rows = span(row + a, BLOCK)
            pre = pre_all[a : a + BLOCK] + vec_ref[5:6, :]
            small = jnp.exp(-jnp.abs(pre))
            delta = jnp.maximum(pre, 0.0) + jnp.log1p(small)
            sig = jnp.where(pre >= 0.0, 1.0, small) / (1.0 + small)
            delta_s[rows, :] = delta
            ratio_s[rows, :] = jnp.where(delta > 1e-30, sig / delta, 1.0)
            u_s[rows, :] = delta * act_s[rows, :]

    each(slabs, convolve)

    zero = jnp.zeros((8, LANES), F32)
    ones = jnp.ones((GROUP, LANES), BF)
    lane_sets = [slice(LANES * e, LANES * (e + 1)) for e in range(4)]

    def pack(top, bottom):
        return jnp.concatenate([top, bottom], axis=0).astype(BF)

    def scan_chunk(chunk, carry):
        state = [list(carry[0:4]), list(carry[4:8])]
        last = list(carry[8:])
        columns = projt_s[chunk]
        for g in range(groups):
            base = chunk * CHUNK + g * GROUP
            rows = span(base, GROUP)
            steps = delta_s[rows, :]
            feeds = u_s[rows, :]
            pulls = dscan_s[rows, :]
            held, sums = [], []
            for t in range(GROUP):
                at = g * GROUP + t
                entry = [
                    jnp.broadcast_to(
                        columns[STATE + 8 * h : STATE + 8 * h + 8, at : at + 1], (8, LANES)
                    )
                    for h in range(2)
                ]
                place = span((base + t) * STATE, STATE)
                total = [None, None]
                for e, lanes in enumerate(lane_sets):
                    step = spread(steps[:, lanes], t)
                    feed = spread(feeds[:, lanes], t)
                    pull = spread(pulls[:, lanes], t)
                    for h in range(2):
                        decay = jnp.exp2(step * rate_ref[8 * h : 8 * h + 8, lanes])
                        state[h][e] = decay * state[h][e] + feed * entry[h]
                        part = pull * state[h][e]
                        total[h] = part if e == 0 else total[h] + part
                    states[place, lanes] = last[e]
                    last[e] = pack(state[0][e], state[1][e])
                held.append(jnp.concatenate(last, axis=1))
                sums.append(pack(*total))
            y_s[rows, :] = dot(read_s[rows, :], jnp.concatenate(held, axis=0))
            found = dot(ones, jnp.concatenate(sums, axis=0), NT)
            wide_s[rows, :] = (found * mask_s[...]).astype(BF)
        return tuple(state[0] + state[1] + last)

    lax.fori_loop(0, chunks, scan_chunk, (zero,) * 8 + (pack(zero, zero),) * 4)

    def finish(slab):
        row = slab * SLAB
        dread_s[span(row, SLAB), :] = dot(wide_s[span(row, SLAB), :], fold_s[1])
        for a in pieces:
            rows = span(row + a, BLOCK)
            scanned = y_s[rows, :] + vec_ref[6:7, :] * act_s[rows, :]
            gated_s[rows, :] = (scanned * gsilu_s[rows, :]).astype(BF)
            dproj_s[rows, INNER:] = (scanned * gslope_s[rows, :]).astype(BF)

    each(slabs, finish)

    def mirror_mixed(slab):
        mixed_all = dot(gated_s[span(slab * SLAB, SLAB), :], w_out_s[...])
        for k in range(SLAB // CHUNK):
            high, low = split_low(mixed_all[k * CHUNK : (k + 1) * CHUNK])
            there = span(place_of(slab * (SLAB // CHUNK) + k), CHUNK)
            mixed_s[there, :] = dot(flip_s[0], high) + dot(flip_s[0], low)

    def natural_mixed(slab):
        rows = span(slab * SLAB, SLAB)
        mixed = dot(gated_s[rows, :], w_out_s[...])
        total = x_s[rows, :].astype(F32) + (mixed + mixed_s[rows, :])
        out_ref[jnp.where(slab == core, 0, 1), 0] = total.astype(BF)

    @pl.when(natural == 0)
    def _():
        each(slabs, mirror_mixed)
        dmix_s[...] = dot(dmix_s[...], perm_ref[...], NT).astype(BF)

    @pl.when(natural == 1)
    def _():
        each(slabs, natural_mixed)

    gwout_ref[...] += dot(gated_s[...], dmix_s[...], TN)

    def back_chunk(step_index, carry_all):
        chunk = chunks - 1 - step_index
        carry = [list(carry_all[0:4]), list(carry_all[4:8])]
        rate_sum = carry_all[8]
        columns = projt_s[chunk]
        for g in reversed(range(groups)):
            base = chunk * CHUNK + g * GROUP
            rows = span(base, GROUP)
            steps = delta_s[rows, :]
            feeds = dscan_s[rows, :]
            pulls = u_s[rows, :]
            held, prods, sums = [], [], []
            for t in reversed(range(GROUP)):
                at = g * GROUP + t
                read = [
                    jnp.broadcast_to(
                        columns[2 * STATE + 8 * h : 2 * STATE + 8 * h + 8, at : at + 1], (8, LANES)
                    )
                    for h in range(2)
                ]
                place = span((base + t) * STATE, STATE)
                held_row, prod_row = [], []
                total = [None, None]
                for e, lanes in enumerate(lane_sets):
                    step = spread(steps[:, lanes], t)
                    feed = spread(feeds[:, lanes], t)
                    pull = spread(pulls[:, lanes], t)
                    before = states[place, lanes].astype(F32)
                    lams, both = [], []
                    for h in range(2):
                        power = step * rate_ref[8 * h : 8 * h + 8, lanes]
                        lam = feed * read[h] + carry[h][e]
                        carry[h][e] = jnp.exp2(power) * lam
                        lams.append(lam)
                        part = pull * lam
                        total[h] = part if e == 0 else total[h] + part
                        both.append(power * (carry[h][e] * before[8 * h : 8 * h + 8]))
                    held_row.append(pack(*lams))
                    prod_row.append(pack(*both))
                held.insert(0, jnp.concatenate(held_row, axis=1))
                prods.insert(0, jnp.concatenate(prod_row, axis=1))
                sums.insert(0, pack(*total))
            y_s[rows, :] = dot(entry_s[rows, :], jnp.concatenate(held, axis=0))
            both = dot(sums_s[...], jnp.concatenate(prods, axis=0))
            gslope_s[rows, :] = both[:GROUP]
            rate_sum = rate_sum + both[GROUP:]
            found = dot(ones, jnp.concatenate(sums, axis=0), NT)
            wide_s[rows, :] = (found * mask_s[...]).astype(BF)
        return tuple(carry[0] + carry[1]) + (rate_sum,)

    done = lax.fori_loop(
        0, chunks, back_chunk, (zero,) * 8 + (jnp.zeros((STATE, INNER), F32),)
    )
    gsmall_ref[0:STATE, :] += done[8] * LN2

    def gradients(slab):
        row = slab * SLAB
        sum_pre = sum_skip = None
        for a in pieces:
            rows = span(row + a, BLOCK)
            dfeed = y_s[rows, :]
            dpre = ratio_s[rows, :] * (gslope_s[rows, :] * LN2 + dfeed * u_s[rows, :])
            gsilu_s[rows, :] = dpre
            dscan = dscan_s[rows, :]
            y_s[rows, :] = dscan * vec_ref[6:7, :] + dfeed * delta_s[rows, :]
            one, two = row_sum(dpre), row_sum(dscan * act_s[rows, :])
            sum_pre = one if sum_pre is None else sum_pre + one
            sum_skip = two if sum_skip is None else sum_skip + two
        gvec_ref[5] += sum_pre
        gvec_ref[6] += sum_skip
        dpre_all = gsilu_s[span(row, SLAB), :].astype(BF)
        dproj = (
            dot(dpre_all, wdt_ref[...], NT)
            + dot(wide_s[span(row, SLAB), :], fold_s[0])
            + dread_s[span(row, SLAB), :]
        )
        extra = dot(dproj.astype(BF), wx_ref[...], NT)
        low = proj_s[span(row, SLAB), :].astype(BF)
        gsmall_ref[STATE : 2 * STATE, :] += dot(low, dpre_all, TN)[:RANK]
        gsmall_ref[2 * STATE : 5 * STATE, :] += dot(
            dproj.astype(BF), act_s[span(row, SLAB), :].astype(BF), TN
        )[: 3 * STATE]
        for a in pieces:
            rows = span(row + a, BLOCK)
            gsilu_s[rows, :] = (y_s[rows, :] + extra[a : a + BLOCK]) * slope_s[rows, :]

    each(slabs, gradients)

    def unconvolve(slab):
        row = slab * SLAB
        totals = [None] * 5
        near_s[...] = gsilu_s[span(row, SLAB + 8, 8), :]
        for a in pieces:
            rows = span(row + a, BLOCK)
            inner = inner_s[span(row + a + 8, BLOCK, 8), :]
            dinner = None
            for j in range(KERNEL):
                moved = near_s[a + 3 - j : a + 3 - j + BLOCK, :]
                term = vec_ref[j : j + 1, :] * moved
                dinner = term if dinner is None else dinner + term
                part = row_sum(moved * inner)
                totals[j] = part if totals[j] is None else totals[j] + part
            part = row_sum(near_s[a : a + BLOCK, :])
            totals[4] = part if totals[4] is None else totals[4] + part
            dproj_s[rows, :INNER] = dinner.astype(BF)
        for j in range(5):
            gvec_ref[j] += totals[j]

    each(slabs, unconvolve)

    def mirror_dnorm(slab):
        dnorm_all = dot(dproj_s[span(slab * SLAB, SLAB), :], w_in_s[...], NT)
        for k in range(SLAB // CHUNK):
            high, low = split_low(dnorm_all[k * CHUNK : (k + 1) * CHUNK])
            there = span(place_of(slab * (SLAB // CHUNK) + k), CHUNK)
            dnorm_s[there, :] = dot(flip_s[0], high) + dot(flip_s[0], low)

    def natural_dnorm(slab):
        rows = span(slab * SLAB, SLAB)
        total = dot(dproj_s[rows, :], w_in_s[...], NT) + dnorm_s[rows, :]
        xf, inv = norm_parts(rows)
        scaled = total * gain_ref[...]
        hat = xf * inv
        ggain_ref[...] += row_sum(total * hat)
        mean = jnp.mean(scaled * hat, axis=-1, keepdims=True)
        gin_ref[jnp.where(slab == core, 0, 1), 0] = up_s[rows, :].astype(F32) + inv * (
            scaled - hat * mean
        )

    @pl.when(natural == 0)
    def _():
        each(slabs, mirror_dnorm)
        copy_s[...] = dot(copy_s[...], perm_ref[...], NT).astype(BF)

    @pl.when(natural == 1)
    def _():
        each(slabs, natural_dnorm)

    gwin_ref[...] += dot(copy_s[...], dproj_s[...], TN)


def run_layer(
    core, x, x_got, up, up_got, perm, w_in, w_x, w_dt, w_out, conv_w, conv_b, dt_bias, a_log, d_skip, gain
):
    windows, half, _ = x_got.shape
    length = 2 * half
    wx_wide = jnp.pad(w_x, ((0, 0), (0, LANES - w_x.shape[1])))
    wdt_wide = jnp.pad(w_dt, ((0, LANES - RANK), (0, 0)))
    vec = jnp.concatenate(
        [conv_w.T, conv_b[None], dt_bias[None], d_skip[None], jnp.zeros((1, INNER), F32)], axis=0
    )
    rate = (-LOG2E) * jnp.exp(a_log).T

    def whole(shape):
        return pl.BlockSpec(shape, lambda w, q, core: (0,) * len(shape))

    kept = pl.BlockSpec((1, half, D), lambda w, q, core: (windows * core[0] + w, 0, 0))
    got = pl.BlockSpec((1, half, D), lambda w, q, core: (w, 0, 0))
    both = pl.BlockSpec((2, 1, half, D), lambda w, q, core: (0, w, 0, 0))
    fixed = (perm, w_in, w_out, wx_wide, wdt_wide, vec, rate, gain[None])
    grads = [
        jax.ShapeDtypeStruct((D, 2 * INNER), F32),
        jax.ShapeDtypeStruct((INNER, D), F32),
        jax.ShapeDtypeStruct((5 * STATE, INNER), F32),
        jax.ShapeDtypeStruct((7, 8, INNER), F32),
        jax.ShapeDtypeStruct((8, D), F32),
    ]
    inner_f32 = [pltpu.VMEM((length, INNER), F32)]
    outer_bf = [pltpu.VMEM((length, D), BF)]
    outer_f32 = [pltpu.VMEM((length, D), F32)]
    halo_f32 = [pltpu.VMEM((length + 8, INNER), F32)]
    scratch = (
        [pltpu.VMEM((length * STATE, INNER), BF)]
        + inner_f32 * 7
        + halo_f32
        + inner_f32
        + halo_f32
        + [pltpu.VMEM((length, LANES), F32)] * 2
        + [
            pltpu.VMEM((length // CHUNK, 3 * STATE, CHUNK), F32),
            pltpu.VMEM((length, 2 * INNER), BF),
            pltpu.VMEM((length, INNER), BF),
        ]
        + outer_bf * 4
        + outer_f32 * 2
        + [pltpu.VMEM((length, WIDE), BF)] * 3
        + [
            pltpu.VMEM((D, 2 * INNER), BF),
            pltpu.VMEM((INNER, D), BF),
            pltpu.VMEM((2, CHUNK, CHUNK), BF),
            pltpu.VMEM((2, LANES, WIDE), BF),
            pltpu.VMEM((2, WIDE, LANES), BF),
            pltpu.VMEM((2 * GROUP, WIDE), BF),
            pltpu.VMEM((GROUP, WIDE), F32),
            pltpu.VMEM((SLAB + 8, INNER), F32),
        ]
    )
    return pl.pallas_call(
        layer_kernel,
        grid_spec=pltpu.PrefetchScalarGridSpec(
            num_scalar_prefetch=1,
            grid=(windows, 2),
            in_specs=[kept, got, kept, got] + [whole(item.shape) for item in fixed],
            out_specs=[both, both] + [whole(item.shape) for item in grads],
            scratch_shapes=scratch,
        ),
        out_shape=[
            jax.ShapeDtypeStruct((2, windows, half, D), BF),
            jax.ShapeDtypeStruct((2, windows, half, D), F32),
        ]
        + grads,
        compiler_params=pltpu.CompilerParams(vmem_limit_bytes=63 * 2**20),
    )(core.reshape(1).astype(jnp.int32), x, x_got, up, up_got, *fixed)


def layer_grads(results):
    gwin, gwout, gsmall, gvec, ggain = results
    vec = jnp.sum(gvec, axis=1)
    return [
        gwin,
        gsmall[2 * STATE :].T,
        gsmall[STATE : 2 * STATE],
        gwout,
        vec[:KERNEL].T,
        vec[4],
        vec[5],
        gsmall[:STATE].T,
        vec[6],
        jnp.sum(ggain, axis=0),
    ]


def param_shapes():
    return [
        (D, 2 * INNER),
        (INNER, RANK + 2 * STATE),
        (RANK, INNER),
        (INNER, D),
        (INNER, KERNEL),
        (INNER,),
        (INNER,),
        (INNER, STATE),
        (INNER,),
        (D,),
    ]


def bounds():
    edges = [0]
    for shape in param_shapes():
        edges.append(edges[-1] + math.prod(shape))
    return edges


def slot_index(owners):
    count = owners.shape[0]
    order = jnp.arange(count, dtype=jnp.int32)
    same = (owners[None, :] == owners[:, None]) & (order[None, :] < order[:, None])
    return jnp.sum(same.astype(jnp.int32), axis=1)


def swap(value, axis, bit):
    size = lax.axis_size(axis)
    return lax.ppermute(value, axis, [(i, i ^ bit) for i in range(size)])


def up_to(value, multiple):
    return -(-value // multiple) * multiple


def pad_rows(value, rows, axis):
    widths = [(0, 0)] * value.ndim
    widths[axis] = (0, rows - value.shape[axis])
    return jnp.pad(value, widths)


def gather_params(weights, owners, rank, matches):
    size = lax.axis_size("dp")
    me = lax.axis_index("dp")
    core = lax.axis_index("seq")
    blocks, block_len = owners.shape[0], weights.shape[1]
    rows = block_len // LANES
    padded = up_to(rows, 16)
    near = min(4, size)
    tiles = weights.reshape(SLOTS, rows, LANES)
    rounded = lax.reduce_precision(tiles, 8, 7)
    pair = SLOTS // 2
    mine = lax.dynamic_slice_in_dim(rounded, core * pair, pair, 0).astype(BF)
    many = pad_rows(mine, padded, 1).reshape(pair * padded, LANES)
    first = MATRIX_END // block_len
    last = (PARAMS - 1) // block_len + 1
    here = matches[:, first:last].T[:, :, None, None]
    fine = jnp.sum(jnp.where(here, (tiles - rounded)[None], 0.0), axis=1).astype(BF)
    fine_rows = (last - first) * rows
    fine_half = up_to(fine_rows, 32) // 2
    fine = pad_rows(fine.reshape(fine_rows, LANES), 2 * fine_half, 0)
    fine = lax.dynamic_slice_in_dim(fine, core * fine_half, fine_half, 0)
    away = owners ^ me
    spot = jnp.zeros_like(owners)
    bit, step = size // 2, 0
    while bit >= near:
        got = swap(jnp.concatenate([many, fine], axis=0), "dp", bit)
        count = many.shape[0]
        many = jnp.concatenate([many, got[:count]], axis=0)
        fine = fine + got[count:]
        spot = spot + jnp.where((away & bit) != 0, 1 << step, 0)
        bit, step = bit // 2, step + 1
    count = many.shape[0]
    sent = jnp.concatenate([many, fine], axis=0)
    others = [swap(sent, "dp", k) for k in range(1, near)]
    many = jnp.stack([many] + [item[:count] for item in others])
    for item in others:
        fine = fine + item[count:]
    spot = (spot + (away & (near - 1)) * (size // near)) * pair + rank % pair
    chosen = many.reshape(size * pair, padded, LANES)[spot]
    sent = jnp.concatenate([chosen.reshape(blocks * padded, LANES), fine], axis=0)
    got = swap(sent, "seq", 1)
    theirs = got[: blocks * padded].reshape(blocks, padded, LANES)
    local = (rank // pair == core)[:, None, None]
    theta = jnp.where(local, chosen, theirs)[:, :rows].reshape(blocks * rows, LANES)
    fine_got = got[blocks * padded :]
    fine = jnp.concatenate(
        [jnp.where(core == 0, fine, fine_got), jnp.where(core == 0, fine_got, fine)], axis=0
    )
    begin = (MATRIX_END - first * block_len) // LANES
    fine = fine[begin : begin + (PARAMS - MATRIX_END) // LANES]
    return lax.optimization_barrier((theta, fine))


def scatter_sum(value, size):
    me = lax.axis_index("dp")
    stride = 1
    total = value
    while stride < size:
        radix = min(4, size // stride)
        total = total.reshape((size // (stride * radix), radix) + value.shape[1:])
        digit = (me // stride) % radix
        low = total.astype(BF)
        kept = lax.dynamic_index_in_dim(total, digit, 1, keepdims=False).astype(F32)
        for k in range(1, radix):
            given = lax.dynamic_index_in_dim(low, digit ^ k, 1, keepdims=False)
            kept = kept + swap(given, "dp", k * stride).astype(F32)
        total = kept
        stride *= radix
    return total[0]


def other_half(value, core):
    count = value.shape[0] // 2
    return swap(lax.dynamic_slice_in_dim(value, (1 - core) * count, count, 0), "seq", 1)


def by_position(pair, core):
    kept, got = pair[0], swap(pair[1], "seq", 1)
    return jnp.concatenate(
        [jnp.where(core == 0, kept, got), jnp.where(core == 0, got, kept)], axis=0
    )


def on_device(
    inputs, cotangent, loss_mask, complement_map, owners, weights, first_moment, second_moment
):
    size = lax.axis_size("dp")
    me = lax.axis_index("dp")
    core = lax.axis_index("seq")
    blocks, block_len = owners.shape[0], weights.shape[1]
    rows = block_len // LANES
    pair = SLOTS // 2
    rank = slot_index(owners)
    order = jnp.arange(blocks, dtype=jnp.int32)
    matches = (owners[None, :] == me) & (
        rank[None, :] == jnp.arange(SLOTS, dtype=jnp.int32)[:, None]
    )
    occupied = jnp.any(matches, axis=1)
    block_of = jnp.sum(jnp.where(matches, order[None, :], 0), axis=1)
    theta, fine = gather_params(weights, owners, rank, matches)
    upstream = cotangent * loss_mask.astype(BF)[..., None]
    x_got = other_half(inputs, core)
    up_got = other_half(upstream, core)

    edges = [edge // LANES for edge in bounds()]
    shapes = param_shapes()
    tail = edges[4]

    def high_of(index):
        return theta[edges[index] : edges[index + 1]].reshape(shapes[index])

    def full_of(index):
        part = theta[edges[index] : edges[index + 1]].astype(F32)
        part = part + fine[edges[index] - tail : edges[index + 1] - tail].astype(F32)
        return part.reshape(shapes[index])

    perm = (complement_map[:, None] == jnp.arange(D, dtype=jnp.int32)[None, :]).astype(BF)
    results = run_layer(
        core,
        inputs,
        x_got,
        upstream,
        up_got,
        perm,
        *[high_of(index) for index in range(4)],
        *[full_of(index) for index in range(4, 10)],
    )
    pieces = layer_grads(results[2:])
    flat_grad = jnp.concatenate([item.reshape(-1) for item in pieces])
    flat_grad = jnp.pad(flat_grad, (0, (blocks + 1) * block_len - PARAMS))
    grad_blocks = flat_grad.reshape(blocks + 1, rows, LANES)
    source = jnp.full((size * SLOTS,), blocks, jnp.int32).at[owners * SLOTS + rank].set(order)
    source = source.reshape(size, 2, pair)

    def for_core(which):
        index = lax.dynamic_index_in_dim(source, which, 1, keepdims=False)
        return grad_blocks[index.reshape(-1)].reshape(size, pair, rows, LANES)

    got = swap(for_core(1 - core).astype(BF), "seq", 1)
    chip = (for_core(core) + got.astype(F32)).astype(BF)
    chip = pad_rows(chip, up_to(rows, 16), 2).reshape(size, -1, LANES)
    summed = scatter_sum(chip, size).reshape(pair, -1, LANES)[:, :rows]
    other = swap(summed, "seq", 1)
    owned = jnp.concatenate(
        [jnp.where(core == 0, summed, other), jnp.where(core == 0, other, summed)], axis=0
    ).reshape(SLOTS, block_len)
    output = by_position(results[0], core)
    grad_input = by_position(results[1], core)
    new_first = BETA_ONE * first_moment + (1.0 - BETA_ONE) * owned
    new_second = BETA_TWO * second_moment + (1.0 - BETA_TWO) * owned * owned
    position = block_of[:, None] * block_len + jnp.arange(block_len, dtype=jnp.int32)[None, :]
    is_matrix = position < MATRIX_END
    rate = jnp.where(is_matrix, RATE_MATRIX, RATE_VECTOR)
    decay = jnp.where(is_matrix, WEIGHT_DECAY, 0.0)
    corrected = (
        new_first
        / (1.0 - BETA_ONE**STEP_COUNT)
        / (jnp.sqrt(new_second / (1.0 - BETA_TWO**STEP_COUNT)) + ADAM_EPSILON)
    )
    new_theta = weights - rate * (corrected + decay * weights)
    keep = occupied[:, None]
    return (
        output,
        grad_input,
        jnp.where(keep, new_theta, 0.0),
        jnp.where(keep, new_first, 0.0),
        jnp.where(keep, new_second, 0.0),
    )


def solution(mesh):
    in_specs = (
        P("dp", "seq", None),
        P("dp", "seq", None),
        P("dp", "seq"),
        P(),
        P(),
        P("dp", None),
        P("dp", None),
        P("dp", None),
    )
    out_specs = (
        P("dp", "seq", None),
        P("dp", "seq", None),
        P("dp", None),
        P("dp", None),
        P("dp", None),
    )
    return jax.shard_map(
        on_device, mesh=mesh, in_specs=in_specs, out_specs=out_specs, check_vma=False
    )
```

time: 373 us -> 289 us (0.77)
  Pallas kernels: 259 us -> 194 us
  other arithmetic: 31.1 us -> 18 us
  local copies, waits for them, and re-layouts: 37.4 us -> 26.6 us
  starting transfers between devices: 19.4 us -> 23.2 us
    pallas_call x1, Pallas kernels: 259 us -> 194 us  [run_layer(): pl.pallas_call(layer_kernel, grid_spec=pltpu.PrefetchScalarGridSpec(num_s...]
    ppermute x18, starting transfers between devices: 19.4 us -> 23.2 us  [swap(): return lax.ppermute(value, axis, [(i, i ^ bit) for i in range(size)])]
  transfers between devices with their start and end apart: 18 -> 18, of which waited for: 7 -> 9; matrix products, arithmetic and copies ran while one was open for 8% -> 8% of each run, Pallas kernels for 0% -> 0%
where the time goes in v3:
time: 289 us
  Pallas kernels  194 us (67%)
  local copies, waits for them, and re-layouts  26.6 us (9%)
  waiting for transfers between devices  25.6 us (9%)
  starting transfers between devices  23.2 us (8%)
  other arithmetic  18 us (6%)
    pallas_call x1, Pallas kernels, run_layer(): pl.pallas_call(layer_kernel, grid_spec=pltpu.PrefetchScalarGridSpec(num_s...  194 us
    ppermute x18, waiting for transfers between devices, swap(): return lax.ppermute(value, axis, [(i, i ^ bit) for i in range(size)])  25.6 us
    ppermute x18, starting transfers between devices, swap(): return lax.ppermute(value, axis, [(i, i ^ bit) for i in range(size)])  23.2 us
  transfers between devices with their start and end apart: 18, of which 9 were waited for; matrix products, arithmetic and copies ran while one was open for 8% of the time, Pallas kernels for 0%

profile of v3, /device:TPU:1, one launch (start us, length us, event | category | flops | bytes accessed | tf_op | source)
XLA Modules:
  0.0 288.6 jit_solution(3093660720982392534)
XLA Ops:
  5.3 3.2 %collective-permute-start.2 = (bf16[288,128]{1,0:T(8,128)(2,1)S(1)}, bf16[288,128]{1,0:T(8,128)(2,1)S(1)}, u32[]{:S(2)}, u32[]{:S(2)}) collective-permute-start(bf16[288,128]{1,0:T(8,128)(2,1)S(1)} %pad_maximum_fusion.6), channel_id=1, source_target_pairs={{0,16},{2,18},{4,20},{6,22},{8,24},{10,26},{12,28},{14,30},{16,0},... | collective-permute-start | bytes 221192 | tf_op jit(solution)/shard_map/ppermute | solution.py:596
  10.3 2.8 collective-permute-start.3
  13.5 2.0 collective-permute-done.3
  15.6 2.2 collective-permute-start.6
  18.8 2.8 collective-permute-done.6
  21.7 6.1 %collective-permute-done.5 = bf16[960,128]{1,0:T(8,128)(2,1)S(1)} collective-permute-done((bf16[960,128]{1,0:T(8,128)(2,1)S(1)}, bf16[960,128]{1,0:T(8,128)(2,1)S(1)}, u32[]{:S(2)}, u32[]{:S(2)}) %collective-permute-start.5) | collective-permute-done | bytes 245792 | tf_op jit(solution)/shard_map/ppermute | solution.py:596
  31.2 2.5 collective-permute-start.7
  46.5 193.7 %shard_map.119 = (bf16[2,2,512,256]{3,2,1,0:T(8,128)(2,1)}, f32[2,2,512,256]{3,2,1,0:T(8,128)}, f32[256,1024]{1,0:T(8,128)}, f32[512,256]{1,0:T(8,128)}, f32[80,...) custom-call(s32[1]{0:T(128)} %bitcast.core_ref, bf16[4,512,256]{2,1,0:T(8,128)(2,1)} %x_kept_ref.1, ...), custom_call_target="tpu_custom_call" | custom-call | tf_op jit(solution)/shard_map/pallas_call | solution.py:530
  242.8 1.4 copy.59
  246.3 1.4 pad.28
  247.7 1.5 reshape.216
  252.9 2.3 slice_bitcast_fusion
  255.2 1.9 gather_fusion.1
  257.4 2.0 add_convert_fusion
  259.5 1.3 collective-permute-start.11
  263.4 3.2 %collective-permute-done.11 = bf16[4,224,128]{2,1,0:T(8,128)(2,1)S(1)} collective-permute-done((bf16[4,224,128]{2,1,0:T(8,128)(2,1)S(1)}, bf16[4,224,128]{2,1,0:T(8,128)(2,1)S(1)}, u32[]{:S(2)}, u32[]{:S(2)}) %collective-permute-start.11) | collective-permute-done | bytes 229408 | tf_op jit(solution)/shard_map/ppermute | solution.py:596
  267.5 4.9 %collective-permute-done.13 = bf16[4,224,128]{2,1,0:T(8,128)(2,1)S(1)} collective-permute-done((bf16[4,224,128]{2,1,0:T(8,128)(2,1)S(1)}, bf16[4,224,128]{2,1,0:T(8,128)(2,1)S(1)}, u32[]{:S(2)}, u32[]{:S(2)}) %collective-permute-start.13) | collective-permute-done | bytes 229408 | tf_op jit(solution)/shard_map/ppermute | solution.py:596
  272.5 2.0 collective-permute-start.14
  274.6 3.1 %collective-permute-start.15 = (bf16[1,224,128]{2,1,0:T(8,128)(2,1)S(1)}, bf16[1,224,128]{2,1,0:T(8,128)(2,1)S(1)}, u32[]{:S(2)}, u32[]{:S(2)}) collective-permute-start(bf16[1,224,128]{2,1,0:T(8,128)(2,1)S(1)} %get-tuple-element.46), channel_id=1, source_target_pairs={{0,16},{2,18},{4,20},{6,22},{8,24},{10,26},{12,28},{14,30},{16,0},... | collective-permute-start | bytes 172040 | tf_op jit(solution)/shard_map/ppermute | solution.py:596
  277.9 1.3 collective-permute-done.15
  279.2 3.3 %collective-permute-done.16 = bf16[1,224,128]{2,1,0:T(8,128)(2,1)S(1)} collective-permute-done((bf16[1,224,128]{2,1,0:T(8,128)(2,1)S(1)}, bf16[1,224,128]{2,1,0:T(8,128)(2,1)S(1)}, u32[]{:S(2)}, u32[]{:S(2)}) %collective-permute-start.16) | collective-permute-done | bytes 57376 | tf_op jit(solution)/shard_map/ppermute | solution.py:596
  282.5 3.1 %collective-permute-start.17 = (f32[2,107,128]{2,1,0:T(8,128)S(1)}, f32[2,107,128]{2,1,0:T(8,128)S(1)}, u32[]{:S(2)}, u32[]{:S(2)}) collective-permute-start(f32[2,107,128]{2,1,0:T(8,128)S(1)} %bitcast.99), channel_id=1, source_target_pairs={{0,1},{1,0},{2,3},{3,2},{4,5},{5,4},{6,7},{7,6},{8,9},{9,8},{10,11... | collective-permute-start | bytes 328712 | tf_op jit(solution)/shard_map/ppermute | solution.py:596
  285.6 1.5 pad_maximum_fusion
  287.2 1.4 broadcast_select_fusion.1
  (174 shorter events, 36.3 us)
Async XLA Ops:
  0.6 12.5 %copy-start.5 = (bf16[4,512,256]{2,1,0:T(8,128)(2,1)S(1)}, bf16[4,512,256]{2,1,0:T(8,128)(2,1)}, u32[]{:S(2)}) copy-start(bf16[4,512,256]{2,1,0:T(8,128)(2,1)} %param.9) | copy-start | bytes 3145732
  1.6 16.2 %copy-start.16 = (s32[32]{0:T(128)}, s32[32]{0:T(128)S(1)}, u32[]{:S(2)}) copy-start(s32[32]{0:T(128)S(1)} %convert_reduce_fusion) | copy-start | bytes 388
  5.3 12.5 %copy-start.20 = (s32[32]{0:T(128)S(1)}, s32[32]{0:T(128)}, u32[]{:S(2)}) copy-start(s32[32]{0:T(128)} %param.12) | copy-start | bytes 388
  5.3 4.9 %collective-permute-start.2 = (bf16[288,128]{1,0:T(8,128)(2,1)S(1)}, bf16[288,128]{1,0:T(8,128)(2,1)S(1)}, u32[]{:S(2)}, u32[]{:S(2)}) collective-permute-start(bf16[288,128]{1,0:T(8,128)(2,1)S(1)} %pad_maximum_fusion.6), channel_id=1, source_target_pairs={{0,16},{2,18},{4,20},{6,22},{8,24},{10,26},{12,28},{14,30},{16,0},... | collective-permute-start | bytes 221192 | tf_op jit(solution)/shard_map/ppermute | solution.py:596
  10.3 5.2 %collective-permute-start.3 = (bf16[512,128]{1,0:T(8,128)(2,1)S(1)}, bf16[512,128]{1,0:T(8,128)(2,1)S(1)}, u32[]{:S(2)}, u32[]{:S(2)}) collective-permute-start(bf16[512,128]{1,0:T(8,128)(2,1)S(1)} %pad_maximum_fusion.5), channel_id=1, source_target_pairs={{0,8},{2,10},{4,12},{6,14},{8,0},{10,2},{12,4},{14,6},{16,24},{18,... | collective-permute-start | bytes 393224 | tf_op jit(solution)/shard_map/ppermute | solution.py:596
  13.5 20.2 %copy-start = (bf16[4,512,256]{2,1,0:T(8,128)(2,1)}, bf16[4,512,256]{2,1,0:T(8,128)(2,1)S(1)}, u32[]{:S(2)}) copy-start(bf16[4,512,256]{2,1,0:T(8,128)(2,1)S(1)} %broadcast_multiply_fusion.up_kept_ref) | copy-start | bytes 3145732
  15.6 6.1 %collective-permute-start.6 = (bf16[960,128]{1,0:T(8,128)(2,1)S(1)}, bf16[960,128]{1,0:T(8,128)(2,1)S(1)}, u32[]{:S(2)}, u32[]{:S(2)}) collective-permute-start(bf16[960,128]{1,0:T(8,128)(2,1)S(1)} %pad_maximum_fusion.4), channel_id=1, source_target_pairs={{0,6},{2,4},{4,2},{6,0},{8,14},{10,12},{12,10},{14,8},{16,22},{18,... | collective-permute-start | bytes 737288 | tf_op jit(solution)/shard_map/ppermute | solution.py:596
  18.3 9.5 %collective-permute-start.5 = (bf16[960,128]{1,0:T(8,128)(2,1)S(1)}, bf16[960,128]{1,0:T(8,128)(2,1)S(1)}, u32[]{:S(2)}, u32[]{:S(2)}) collective-permute-start(bf16[960,128]{1,0:T(8,128)(2,1)S(1)} %pad_maximum_fusion.4), channel_id=1, source_target_pairs={{0,4},{2,6},{4,0},{6,2},{8,12},{10,14},{12,8},{14,10},{16,20},{18,... | collective-permute-start | bytes 737288 | tf_op jit(solution)/shard_map/ppermute | solution.py:596
  18.5 9.3 %collective-permute-start.4 = (bf16[960,128]{1,0:T(8,128)(2,1)S(1)}, bf16[960,128]{1,0:T(8,128)(2,1)S(1)}, u32[]{:S(2)}, u32[]{:S(2)}) collective-permute-start(bf16[960,128]{1,0:T(8,128)(2,1)S(1)} %pad_maximum_fusion.4), channel_id=1, source_target_pairs={{0,2},{2,0},{4,6},{6,4},{8,10},{10,8},{12,14},{14,12},{16,18},{18,... | collective-permute-start | bytes 737288 | tf_op jit(solution)/shard_map/ppermute | solution.py:596
  30.2 8.0 %copy-start.19 = (s32[256]{0:T(256)S(1)}, s32[256]{0:T(256)}, u32[]{:S(2)}) copy-start(s32[256]{0:T(256)} %param.11) | copy-start | bytes 3076
  31.2 7.8 %collective-permute-start.7 = (bf16[3648,128]{1,0:T(8,128)(2,1)}, bf16[3648,128]{1,0:T(8,128)(2,1)S(1)}, u32[]{:S(2)}, u32[]{:S(2)}) collective-permute-start(bf16[3648,128]{1,0:T(8,128)(2,1)} %pad_maximum_fusion.2), channel_id=1, source_target_pairs={{0,1},{1,0},{2,3},{3,2},{4,5},{5,4},{6,7},{7,6},{8,9},{9,8},{10,11... | collective-permute-start | bytes 2801672 | tf_op jit(solution)/shard_map/ppermute | solution.py:596
  34.6 11.2 %collective-permute-start.1 = (bf16[2,512,256]{2,1,0:T(8,128)(2,1)}, bf16[2,512,256]{2,1,0:T(8,128)(2,1)S(1)}, u32[]{:S(2)}, u32[]{:S(2)}) collective-permute-start(bf16[2,512,256]{2,1,0:T(8,128)(2,1)} %constant_dynamic-slice_fusion.3), channel_id=1, source_target_pairs={{0,1},{1,0},{2,3},{3,2},{4,5},{5,4},{6,7},{7,6},{8,9},{9,8},{10,11... | collective-permute-start | bytes 1572872 | tf_op jit(solution)/shard_map/ppermute | solution.py:596
  35.4 10.3 %collective-permute-start = (bf16[2,512,256]{2,1,0:T(8,128)(2,1)}, bf16[2,512,256]{2,1,0:T(8,128)(2,1)}, u32[]{:S(2)}, u32[]{:S(2)}) collective-permute-start(bf16[2,512,256]{2,1,0:T(8,128)(2,1)} %constant_dynamic-slice_fusion.4), channel_id=1, source_target_pairs={{0,1},{1,0},{2,3},{3,2},{4,5},{5,4},{6,7},{7,6},{8,9},{9,8},{10,11... | collective-permute-start | bytes 1572872 | tf_op jit(solution)/shard_map/ppermute | solution.py:596
  251.3 6.0 %collective-permute-start.10 = (bf16[16,2,107,128]{3,0,2,1:T(8,128)(2,1)}, bf16[16,2,107,128]{3,0,2,1:T(8,128)(2,1)}, u32[]{:S(2)}, u32[]{:S(2)}) collective-permute-start(bf16[16,2,107,128]{3,0,2,1:T(8,128)(2,1)} %copy.57), channel_id=1, source_target_pairs={{0,1},{1,0},{2,3},{3,2},{4,5},{5,4},{6,7},{7,6},{8,9},{9,8},{10,11... | collective-permute-start | bytes 2629640 | tf_op jit(solution)/shard_map/ppermute | solution.py:596
  252.7 9.6 %collective-permute-start.8 = (bf16[2,512,256]{2,1,0:T(8,128)(2,1)}, bf16[2,512,256]{2,1,0:T(8,128)(2,1)S(1)}, u32[]{:S(2)}, u32[]{:S(2)}) collective-permute-start(bf16[2,512,256]{2,1,0:T(8,128)(2,1)} %slice_bitcast_fusion.1), channel_id=1, source_target_pairs={{0,1},{1,0},{2,3},{3,2},{4,5},{5,4},{6,7},{7,6},{8,9},{9,8},{10,11... | collective-permute-start | bytes 1572872 | tf_op jit(solution)/shard_map/ppermute | solution.py:596
  257.1 20.6 %collective-permute-start.9 = (f32[2,512,256]{2,1,0:T(8,128)}, f32[2,512,256]{2,1,0:T(8,128)S(1)}, u32[]{:S(2)}, u32[]{:S(2)}) collective-permute-start(f32[2,512,256]{2,1,0:T(8,128)} %slice_bitcast_fusion), channel_id=1, source_target_pairs={{0,1},{1,0},{2,3},{3,2},{4,5},{5,4},{6,7},{7,6},{8,9},{9,8},{10,11... | collective-permute-start | bytes 3145736 | tf_op jit(solution)/shard_map/ppermute | solution.py:596
  259.5 7.1 %collective-permute-start.11 = (bf16[4,224,128]{2,1,0:T(8,128)(2,1)S(1)}, bf16[4,224,128]{2,1,0:T(8,128)(2,1)S(1)}, u32[]{:S(2)}, u32[]{:S(2)}) collective-permute-start(bf16[4,224,128]{2,1,0:T(8,128)(2,1)S(1)} %get-tuple-element.33), channel_id=1, source_target_pairs={{0,2},{2,0},{4,6},{6,4},{8,10},{10,8},{12,14},{14,12},{16,18},{18,... | collective-permute-start | bytes 688136 | tf_op jit(solution)/shard_map/ppermute | solution.py:596
  260.8 6.7 %collective-permute-start.12 = (bf16[4,224,128]{2,1,0:T(8,128)(2,1)S(1)}, bf16[4,224,128]{2,1,0:T(8,128)(2,1)S(1)}, u32[]{:S(2)}, u32[]{:S(2)}) collective-permute-start(bf16[4,224,128]{2,1,0:T(8,128)(2,1)S(1)} %get-tuple-element.35), channel_id=1, source_target_pairs={{0,4},{2,6},{4,0},{6,2},{8,12},{10,14},{12,8},{14,10},{16,20},{18,... | collective-permute-start | bytes 688136 | tf_op jit(solution)/shard_map/ppermute | solution.py:596
  261.8 10.6 %collective-permute-start.13 = (bf16[4,224,128]{2,1,0:T(8,128)(2,1)S(1)}, bf16[4,224,128]{2,1,0:T(8,128)(2,1)S(1)}, u32[]{:S(2)}, u32[]{:S(2)}) collective-permute-start(bf16[4,224,128]{2,1,0:T(8,128)(2,1)S(1)} %get-tuple-element.34), channel_id=1, source_target_pairs={{0,6},{2,4},{4,2},{6,0},{8,14},{10,12},{12,10},{14,8},{16,22},{18,... | collective-permute-start | bytes 688136 | tf_op jit(solution)/shard_map/ppermute | solution.py:596
  262.3 15.4 %copy-start.2 = (f32[2,2,512,256]{3,2,1,0:T(8,128)S(1)}, f32[2,2,512,256]{3,2,1,0:T(8,128)}, u32[]{:S(2)}) copy-start(f32[2,2,512,256]{3,2,1,0:T(8,128)} %get-tuple-element.17) | copy-start | bytes 6291460
  272.5 5.3 %collective-permute-start.14 = (bf16[1,224,128]{2,1,0:T(8,128)(2,1)S(1)}, bf16[1,224,128]{2,1,0:T(8,128)(2,1)S(1)}, u32[]{:S(2)}, u32[]{:S(2)}) collective-permute-start(bf16[1,224,128]{2,1,0:T(8,128)(2,1)S(1)} %get-tuple-element.44), channel_id=1, source_target_pairs={{0,8},{2,10},{4,12},{6,14},{8,0},{10,2},{12,4},{14,6},{16,24},{18,... | collective-permute-start | bytes 172040 | tf_op jit(solution)/shard_map/ppermute | solution.py:596
  274.6 4.6 %collective-permute-start.15 = (bf16[1,224,128]{2,1,0:T(8,128)(2,1)S(1)}, bf16[1,224,128]{2,1,0:T(8,128)(2,1)S(1)}, u32[]{:S(2)}, u32[]{:S(2)}) collective-permute-start(bf16[1,224,128]{2,1,0:T(8,128)(2,1)S(1)} %get-tuple-element.46), channel_id=1, source_target_pairs={{0,16},{2,18},{4,20},{6,22},{8,24},{10,26},{12,28},{14,30},{16,0},... | collective-permute-start | bytes 172040 | tf_op jit(solution)/shard_map/ppermute | solution.py:596
  277.6 4.8 %collective-permute-start.16 = (bf16[1,224,128]{2,1,0:T(8,128)(2,1)S(1)}, bf16[1,224,128]{2,1,0:T(8,128)(2,1)S(1)}, u32[]{:S(2)}, u32[]{:S(2)}) collective-permute-start(bf16[1,224,128]{2,1,0:T(8,128)(2,1)S(1)} %get-tuple-element.45), channel_id=1, source_target_pairs={{0,24},{2,26},{4,28},{6,30},{8,16},{10,18},{12,20},{14,22},{16,8},... | collective-permute-start | bytes 172040 | tf_op jit(solution)/shard_map/ppermute | solution.py:596
  282.5 4.6 %collective-permute-start.17 = (f32[2,107,128]{2,1,0:T(8,128)S(1)}, f32[2,107,128]{2,1,0:T(8,128)S(1)}, u32[]{:S(2)}, u32[]{:S(2)}) collective-permute-start(f32[2,107,128]{2,1,0:T(8,128)S(1)} %bitcast.99), channel_id=1, source_target_pairs={{0,1},{1,0},{2,3},{3,2},{4,5},{5,4},{6,7},{7,6},{8,9},{9,8},{10,11... | collective-permute-start | bytes 328712 | tf_op jit(solution)/shard_map/ppermute | solution.py:596
  (17 other events, 35.9 us)

commit v4 on v3

--- a/solution.py
+++ b/solution.py
@@ -29,6 +29,7 @@
 CHUNK = 128
 GROUP = 16
 SLAB = 512
+REACH = 256
 BLOCK = 32
 LANES = 128
 WIDE = GROUP * STATE
@@ -83,8 +84,10 @@
     vec_ref,
     rate_ref,
     gain_ref,
-    out_ref,
-    gin_ref,
+    out_kept_ref,
+    out_given_ref,
+    gin_kept_ref,
+    gin_given_ref,
     gwin_ref,
     gwout_ref,
     gsmall_ref,
@@ -110,7 +113,6 @@
     dmix_s,
     x_s,
     up_s,
-    mixed_s,
     dnorm_s,
     wide_s,
     read_s,
@@ -123,6 +125,8 @@
     sums_s,
     mask_s,
     near_s,
+    wx_s,
+    wdt_s,
 ):
     window = pl.program_id(0)
     natural = pl.program_id(1)
@@ -131,7 +135,7 @@
     half = length // 2
     chunks = length // CHUNK
     slabs = length // SLAB
-    groups = CHUNK // GROUP
+    groups = REACH // GROUP
     pieces = range(0, SLAB, BLOCK)
 
     @pl.when((window == 0) & (natural == 0))
@@ -141,7 +145,11 @@
         gsmall_ref[...] = jnp.zeros_like(gsmall_ref)
         gvec_ref[...] = jnp.zeros_like(gvec_ref)
         ggain_ref[...] = jnp.zeros_like(ggain_ref)
-        inner_s[0:8, :] = jnp.zeros((8, INNER), F32)
+        wx_s[...] = jnp.zeros_like(wx_s)
+        wx_s[:, : 3 * STATE] = wx_ref[...]
+        wdt_s[...] = jnp.zeros_like(wdt_s)
+        wdt_s[:RANK, :] = wdt_ref[...]
+        inner_s[0:16, :] = jnp.zeros((16, INNER), BF)
         gsilu_s[length : length + 8, :] = jnp.zeros((8, INNER), F32)
         rows, lanes = iota((CHUNK, CHUNK), 0), iota((CHUNK, CHUNK), 1)
         flip_s[1] = jnp.where(rows == lanes, 1.0, 0.0).astype(BF)
@@ -193,15 +201,13 @@
     def project(slab):
         row = slab * SLAB
         copy = copy_s[span(row, SLAB), :]
-        inner_s[span(row + 8, SLAB, 8), :] = (
-            dot(copy, w_in_s[:, :INNER]).astype(BF).astype(F32)
-        )
-        gate_all = dot(copy, w_in_s[:, INNER:])
-        dgated_all = dot(dmix_s[span(row, SLAB), :], w_out_s[...], NT)
+        inner_s[span(row + 16, SLAB, 16), :] = dot(copy, w_in_s[:, :INNER]).astype(BF)
+        gate_all = dot(copy, w_in_s[:, INNER:]).astype(BF)
+        dgated_all = dot(dmix_s[span(row, SLAB), :], w_out_s[...], NT).astype(BF)
         for a in pieces:
             rows = span(row + a, BLOCK)
-            gate = gate_all[a : a + BLOCK].astype(BF).astype(F32)
-            dgated = dgated_all[a : a + BLOCK].astype(BF).astype(F32)
+            gate = gate_all[a : a + BLOCK].astype(F32)
+            dgated = dgated_all[a : a + BLOCK].astype(F32)
             sig = 1.0 / (1.0 + jnp.exp(-gate))
             silu = gate * sig
             gsilu_s[rows, :] = silu
@@ -212,19 +218,19 @@
 
     def convolve(slab):
         row = slab * SLAB
-        near_s[...] = inner_s[span(row, SLAB + 8, 8), :]
+        near_s[...] = inner_s[span(row, SLAB + 16, 16), :].astype(F32)
         for a in pieces:
             rows = span(row + a, BLOCK)
             conv = vec_ref[4:5, :]
             for j in range(KERNEL):
-                conv = conv + vec_ref[j : j + 1, :] * near_s[a + 5 + j : a + 5 + j + BLOCK, :]
+                conv = conv + vec_ref[j : j + 1, :] * near_s[a + 13 + j : a + 13 + j + BLOCK, :]
             sig = 1.0 / (1.0 + jnp.exp(-conv))
             act = conv * sig
             act_s[rows, :] = act
             slope_s[rows, :] = sig + act * (1.0 - sig)
         act_high, act_low = split_low(act_s[span(row, SLAB), :])
-        proj = dot(act_high, wx_ref[...]) + dot(act_low, wx_ref[...])
-        proj_s[span(row, SLAB), :] = proj
+        proj = dot(act_high, wx_s[...]) + dot(act_low, wx_s[...])
+        proj_s[span(row, SLAB), :] = proj.astype(BF)
         for k in range(SLAB // CHUNK):
             turned = jnp.transpose(proj[k * CHUNK : (k + 1) * CHUNK])
             projt_s[slab * (SLAB // CHUNK) + k] = turned[: 3 * STATE]
@@ -234,15 +240,15 @@
             for g in range(SLAB // GROUP):
                 part = wide[g * GROUP : (g + 1) * GROUP] * mask_s[...]
                 target[span(row + g * GROUP, GROUP), :] = part.astype(BF)
-        pre_all = dot(proj_high, wdt_ref[...]) + dot(proj_low, wdt_ref[...])
+        pre_all = dot(proj_high, wdt_s[...]) + dot(proj_low, wdt_s[...])
         for a in pieces:
             rows = span(row + a, BLOCK)
             pre = pre_all[a : a + BLOCK] + vec_ref[5:6, :]
             small = jnp.exp(-jnp.abs(pre))
             delta = jnp.maximum(pre, 0.0) + jnp.log1p(small)
-            sig = jnp.where(pre >= 0.0, 1.0, small) / (1.0 + small)
+            scaled = jnp.where(pre >= 0.0, 1.0, small) / ((1.0 + small) * delta)
             delta_s[rows, :] = delta
-            ratio_s[rows, :] = jnp.where(delta > 1e-30, sig / delta, 1.0)
+            ratio_s[rows, :] = jnp.where(delta > 1e-30, scaled, 1.0)
             u_s[rows, :] = delta * act_s[rows, :]
 
     each(slabs, convolve)
@@ -254,19 +260,24 @@
     def pack(top, bottom):
         return jnp.concatenate([top, bottom], axis=0).astype(BF)
 
-    def scan_chunk(chunk, carry):
+    def turned_of(index):
+        each_chunk = REACH // CHUNK
+        return [projt_s[index * each_chunk + k] for k in range(each_chunk)]
+
+    def scan_chunk(index, carry):
         state = [list(carry[0:4]), list(carry[4:8])]
         last = list(carry[8:])
-        columns = projt_s[chunk]
+        turned = turned_of(index)
         for g in range(groups):
-            base = chunk * CHUNK + g * GROUP
+            base = index * REACH + g * GROUP
+            columns = turned[g * GROUP // CHUNK]
             rows = span(base, GROUP)
             steps = delta_s[rows, :]
             feeds = u_s[rows, :]
             pulls = dscan_s[rows, :]
             held, sums = [], []
             for t in range(GROUP):
-                at = g * GROUP + t
+                at = (g * GROUP + t) % CHUNK
                 entry = [
                     jnp.broadcast_to(
                         columns[STATE + 8 * h : STATE + 8 * h + 8, at : at + 1], (8, LANES)
@@ -293,11 +304,11 @@
             wide_s[rows, :] = (found * mask_s[...]).astype(BF)
         return tuple(state[0] + state[1] + last)
 
-    lax.fori_loop(0, chunks, scan_chunk, (zero,) * 8 + (pack(zero, zero),) * 4)
+    lax.fori_loop(0, length // REACH, scan_chunk, (zero,) * 8 + (pack(zero, zero),) * 4)
 
     def finish(slab):
         row = slab * SLAB
-        dread_s[span(row, SLAB), :] = dot(wide_s[span(row, SLAB), :], fold_s[1])
+        dread_s[span(row, SLAB), :] = dot(wide_s[span(row, SLAB), :], fold_s[1]).astype(BF)
         for a in pieces:
             rows = span(row + a, BLOCK)
             scanned = y_s[rows, :] + vec_ref[6:7, :] * act_s[rows, :]
@@ -306,18 +317,35 @@
 
     each(slabs, finish)
 
+    def store_half(kept_ref, given_ref, which, rows, value):
+        @pl.when(which == core)
+        def _():
+            kept_ref[0, rows, :] = value
+
+        @pl.when(which != core)
+        def _():
+            given_ref[0, rows, :] = value
+
     def mirror_mixed(slab):
         mixed_all = dot(gated_s[span(slab * SLAB, SLAB), :], w_out_s[...])
         for k in range(SLAB // CHUNK):
             high, low = split_low(mixed_all[k * CHUNK : (k + 1) * CHUNK])
-            there = span(place_of(slab * (SLAB // CHUNK) + k), CHUNK)
-            mixed_s[there, :] = dot(flip_s[0], high) + dot(flip_s[0], low)
+            place = place_of(slab * (SLAB // CHUNK) + k)
+            mixed = dot(flip_s[0], high) + dot(flip_s[0], low)
+            store_half(gin_kept_ref, gin_given_ref, place // half, span(place % half, CHUNK), mixed)
 
     def natural_mixed(slab):
         rows = span(slab * SLAB, SLAB)
         mixed = dot(gated_s[rows, :], w_out_s[...])
-        total = x_s[rows, :].astype(F32) + (mixed + mixed_s[rows, :])
-        out_ref[jnp.where(slab == core, 0, 1), 0] = total.astype(BF)
+        total = x_s[rows, :].astype(F32) + mixed
+
+        @pl.when(slab == core)
+        def _():
+            out_kept_ref[0] = (total + gin_kept_ref[0]).astype(BF)
+
+        @pl.when(slab != core)
+        def _():
+            out_given_ref[0] = (total + gin_given_ref[0]).astype(BF)
 
     @pl.when(natural == 0)
     def _():
@@ -331,19 +359,20 @@
     gwout_ref[...] += dot(gated_s[...], dmix_s[...], TN)
 
     def back_chunk(step_index, carry_all):
-        chunk = chunks - 1 - step_index
+        index = length // REACH - 1 - step_index
         carry = [list(carry_all[0:4]), list(carry_all[4:8])]
         rate_sum = carry_all[8]
-        columns = projt_s[chunk]
+        turned = turned_of(index)
         for g in reversed(range(groups)):
-            base = chunk * CHUNK + g * GROUP
+            base = index * REACH + g * GROUP
+            columns = turned[g * GROUP // CHUNK]
             rows = span(base, GROUP)
             steps = delta_s[rows, :]
             feeds = dscan_s[rows, :]
             pulls = u_s[rows, :]
             held, prods, sums = [], [], []
             for t in reversed(range(GROUP)):
-                at = g * GROUP + t
+                at = (g * GROUP + t) % CHUNK
                 read = [
                     jnp.broadcast_to(
                         columns[2 * STATE + 8 * h : 2 * STATE + 8 * h + 8, at : at + 1], (8, LANES)
@@ -357,7 +386,7 @@
                     step = spread(steps[:, lanes], t)
                     feed = spread(feeds[:, lanes], t)
                     pull = spread(pulls[:, lanes], t)
-                    before = states[place, lanes].astype(F32)
+                    before = states[place, lanes]
                     lams, both = [], []
                     for h in range(2):
                         power = step * rate_ref[8 * h : 8 * h + 8, lanes]
@@ -366,9 +395,9 @@
                         lams.append(lam)
                         part = pull * lam
                         total[h] = part if e == 0 else total[h] + part
-                        both.append(power * (carry[h][e] * before[8 * h : 8 * h + 8]))
+                        both.append(power * carry[h][e])
                     held_row.append(pack(*lams))
-                    prod_row.append(pack(*both))
+                    prod_row.append(pack(*both) * before)
                 held.insert(0, jnp.concatenate(held_row, axis=1))
                 prods.insert(0, jnp.concatenate(prod_row, axis=1))
                 sums.insert(0, pack(*total))
@@ -381,7 +410,7 @@
         return tuple(carry[0] + carry[1]) + (rate_sum,)
 
     done = lax.fori_loop(
-        0, chunks, back_chunk, (zero,) * 8 + (jnp.zeros((STATE, INNER), F32),)
+        0, length // REACH, back_chunk, (zero,) * 8 + (jnp.zeros((STATE, INNER), F32),)
     )
     gsmall_ref[0:STATE, :] += done[8] * LN2
 
@@ -402,12 +431,12 @@
         gvec_ref[6] += sum_skip
         dpre_all = gsilu_s[span(row, SLAB), :].astype(BF)
         dproj = (
-            dot(dpre_all, wdt_ref[...], NT)
+            dot(dpre_all, wdt_s[...], NT)
             + dot(wide_s[span(row, SLAB), :], fold_s[0])
-            + dread_s[span(row, SLAB), :]
+            + dread_s[span(row, SLAB), :].astype(F32)
         )
-        extra = dot(dproj.astype(BF), wx_ref[...], NT)
-        low = proj_s[span(row, SLAB), :].astype(BF)
+        extra = dot(dproj.astype(BF), wx_s[...], NT)
+        low = proj_s[span(row, SLAB), :]
         gsmall_ref[STATE : 2 * STATE, :] += dot(low, dpre_all, TN)[:RANK]
         gsmall_ref[2 * STATE : 5 * STATE, :] += dot(
             dproj.astype(BF), act_s[span(row, SLAB), :].astype(BF), TN
@@ -421,10 +450,10 @@
     def unconvolve(slab):
         row = slab * SLAB
         totals = [None] * 5
-        near_s[...] = gsilu_s[span(row, SLAB + 8, 8), :]
+        near_s[: SLAB + 8, :] = gsilu_s[span(row, SLAB + 8, 8), :]
         for a in pieces:
             rows = span(row + a, BLOCK)
-            inner = inner_s[span(row + a + 8, BLOCK, 8), :]
+            inner = inner_s[span(row + a + 16, BLOCK, 16), :].astype(F32)
             dinner = None
             for j in range(KERNEL):
                 moved = near_s[a + 3 - j : a + 3 - j + BLOCK, :]
@@ -455,9 +484,8 @@
         hat = xf * inv
         ggain_ref[...] += row_sum(total * hat)
         mean = jnp.mean(scaled * hat, axis=-1, keepdims=True)
-        gin_ref[jnp.where(slab == core, 0, 1), 0] = up_s[rows, :].astype(F32) + inv * (
-            scaled - hat * mean
-        )
+        result = up_s[rows, :].astype(F32) + inv * (scaled - hat * mean)
+        store_half(gin_kept_ref, gin_given_ref, slab, slice(None), result)
 
     @pl.when(natural == 0)
     def _():
@@ -476,8 +504,6 @@
 ):
     windows, half, _ = x_got.shape
     length = 2 * half
-    wx_wide = jnp.pad(w_x, ((0, 0), (0, LANES - w_x.shape[1])))
-    wdt_wide = jnp.pad(w_dt, ((0, LANES - RANK), (0, 0)))
     vec = jnp.concatenate(
         [conv_w.T, conv_b[None], dt_bias[None], d_skip[None], jnp.zeros((1, INNER), F32)], axis=0
     )
@@ -488,8 +514,7 @@
 
     kept = pl.BlockSpec((1, half, D), lambda w, q, core: (windows * core[0] + w, 0, 0))
     got = pl.BlockSpec((1, half, D), lambda w, q, core: (w, 0, 0))
-    both = pl.BlockSpec((2, 1, half, D), lambda w, q, core: (0, w, 0, 0))
-    fixed = (perm, w_in, w_out, wx_wide, wdt_wide, vec, rate, gain[None])
+    fixed = (perm, w_in, w_out, w_x, w_dt, vec, rate, gain[None])
     grads = [
         jax.ShapeDtypeStruct((D, 2 * INNER), F32),
         jax.ShapeDtypeStruct((INNER, D), F32),
@@ -506,15 +531,15 @@
         + inner_f32 * 7
         + halo_f32
         + inner_f32
-        + halo_f32
-        + [pltpu.VMEM((length, LANES), F32)] * 2
+        + [pltpu.VMEM((length + 16, INNER), BF)]
+        + [pltpu.VMEM((length, LANES), BF)] * 2
         + [
             pltpu.VMEM((length // CHUNK, 3 * STATE, CHUNK), F32),
             pltpu.VMEM((length, 2 * INNER), BF),
             pltpu.VMEM((length, INNER), BF),
         ]
         + outer_bf * 4
-        + outer_f32 * 2
+        + outer_f32
         + [pltpu.VMEM((length, WIDE), BF)] * 3
         + [
             pltpu.VMEM((D, 2 * INNER), BF),
@@ -524,7 +549,9 @@
             pltpu.VMEM((2, WIDE, LANES), BF),
             pltpu.VMEM((2 * GROUP, WIDE), BF),
             pltpu.VMEM((GROUP, WIDE), F32),
-            pltpu.VMEM((SLAB + 8, INNER), F32),
+            pltpu.VMEM((SLAB + 16, INNER), F32),
+            pltpu.VMEM((INNER, LANES), BF),
+            pltpu.VMEM((LANES, INNER), BF),
         ]
     )
     return pl.pallas_call(
@@ -533,15 +560,14 @@
             num_scalar_prefetch=1,
             grid=(windows, 2),
             in_specs=[kept, got, kept, got] + [whole(item.shape) for item in fixed],
-            out_specs=[both, both] + [whole(item.shape) for item in grads],
+            out_specs=[got] * 4 + [whole(item.shape) for item in grads],
             scratch_shapes=scratch,
         ),
         out_shape=[
-            jax.ShapeDtypeStruct((2, windows, half, D), BF),
-            jax.ShapeDtypeStruct((2, windows, half, D), F32),
+            jax.ShapeDtypeStruct((windows, half, D), kind) for kind in (BF, BF, F32, F32)
         ]
         + grads,
-        compiler_params=pltpu.CompilerParams(vmem_limit_bytes=63 * 2**20),
+        compiler_params=pltpu.CompilerParams(vmem_limit_bytes=64 * 2**20 - 65536),
     )(core.reshape(1).astype(jnp.int32), x, x_got, up, up_got, *fixed)
 
 
@@ -682,8 +708,8 @@
     return swap(lax.dynamic_slice_in_dim(value, (1 - core) * count, count, 0), "seq", 1)
 
 
-def by_position(pair, core):
-    kept, got = pair[0], swap(pair[1], "seq", 1)
+def by_position(kept, given, core):
+    got = swap(given, "seq", 1)
     return jnp.concatenate(
         [jnp.where(core == 0, kept, got), jnp.where(core == 0, got, kept)], axis=0
     )
@@ -733,27 +759,29 @@
         *[high_of(index) for index in range(4)],
         *[full_of(index) for index in range(4, 10)],
     )
-    pieces = layer_grads(results[2:])
-    flat_grad = jnp.concatenate([item.reshape(-1) for item in pieces])
-    flat_grad = jnp.pad(flat_grad, (0, (blocks + 1) * block_len - PARAMS))
-    grad_blocks = flat_grad.reshape(blocks + 1, rows, LANES)
+    pieces = layer_grads(results[4:])
+    padded = up_to(rows, 16)
+    spare = jnp.zeros(((blocks + 1) * rows - PARAMS // LANES, LANES), BF)
+    tiles = [item.astype(BF).reshape(-1, LANES) for item in pieces] + [spare]
+    grad_blocks = jnp.concatenate(tiles, axis=0).reshape(blocks + 1, rows, LANES)
+    grad_blocks = pad_rows(grad_blocks, padded, 1)
     source = jnp.full((size * SLOTS,), blocks, jnp.int32).at[owners * SLOTS + rank].set(order)
     source = source.reshape(size, 2, pair)
 
     def for_core(which):
         index = lax.dynamic_index_in_dim(source, which, 1, keepdims=False)
-        return grad_blocks[index.reshape(-1)].reshape(size, pair, rows, LANES)
-
-    got = swap(for_core(1 - core).astype(BF), "seq", 1)
-    chip = (for_core(core) + got.astype(F32)).astype(BF)
-    chip = pad_rows(chip, up_to(rows, 16), 2).reshape(size, -1, LANES)
+        return grad_blocks[index.reshape(-1)].reshape(size * pair * padded, LANES)
+
+    got = swap(for_core(1 - core), "seq", 1)
+    chip = (for_core(core).astype(F32) + got.astype(F32)).astype(BF)
+    chip = chip.reshape(size, pair * padded, LANES)
     summed = scatter_sum(chip, size).reshape(pair, -1, LANES)[:, :rows]
     other = swap(summed, "seq", 1)
     owned = jnp.concatenate(
         [jnp.where(core == 0, summed, other), jnp.where(core == 0, other, summed)], axis=0
     ).reshape(SLOTS, block_len)
-    output = by_position(results[0], core)
-    grad_input = by_position(results[1], core)
+    output = by_position(results[0], results[1], core)
+    grad_input = by_position(results[2], results[3], core)
     new_first = BETA_ONE * first_moment + (1.0 - BETA_ONE) * owned
     new_second = BETA_TWO * second_moment + (1.0 - BETA_TWO) * owned * owned
     position = block_of[:, None] * block_len + jnp.arange(block_len, dtype=jnp.int32)[None, :]

time: 289 us -> 273 us (0.945)
  local copies, waits for them, and re-layouts: 26.6 us -> 13.4 us
  Pallas kernels: 194 us -> 188 us
    pallas_call x1, Pallas kernels: 194 us -> 188 us  [run_layer(): pl.pallas_call(layer_kernel, grid_spec=pltpu.PrefetchScalarGridSpec(num_s...]
    unnamed x58 -> x38, local copies, waits for them, and re-layouts: 4.59 us -> 0.08 us
    squeeze x2 -> x0, local copies, waits for them, and re-layouts: 3.1 us -> none  [by_position(): kept, got = (pair[0], swap(pair[1], 'seq', 1))]
  transfers between devices with their start and end apart: 18 -> 18, of which waited for: 9 -> 10; matrix products, arithmetic and copies ran while one was open for 8% -> 6% of each run, Pallas kernels for 0% -> 0%
where the time goes in v4:
time: 273 us; the launch traced here: 272 us
  Pallas kernels  188 us (69%)
  waiting for transfers between devices  27.2 us (10%)
  starting transfers between devices  23.3 us (9%)
  other arithmetic  19.3 us (7%)
  local copies, waits for them, and re-layouts  13.4 us (5%)
    pallas_call x1, Pallas kernels, run_layer(): pl.pallas_call(layer_kernel, grid_spec=pltpu.PrefetchScalarGridSpec(num_s...  188 us
    ppermute x18, waiting for transfers between devices, swap(): return lax.ppermute(value, axis, [(i, i ^ bit) for i in range(size)])  27.2 us
    ppermute x18, starting transfers between devices, swap(): return lax.ppermute(value, axis, [(i, i ^ bit) for i in range(size)])  23.3 us
  transfers between devices with their start and end apart: 18, of which 10 were waited for; matrix products, arithmetic and copies ran while one was open for 6% of the time, Pallas kernels for 0%

profile of v4, /device:TPU:1, one launch (start us, length us, event | category | flops | bytes accessed | tf_op | source)
XLA Modules:
  0.0 272.4 jit_solution(17445266829541075672)
XLA Ops:
  3.9 1.2 select_reduce_fusion
  5.3 3.2 %collective-permute-start.2 = (bf16[288,128]{1,0:T(8,128)(2,1)S(1)}, bf16[288,128]{1,0:T(8,128)(2,1)S(1)}, u32[]{:S(2)}, u32[]{:S(2)}) collective-permute-start(bf16[288,128]{1,0:T(8,128)(2,1)S(1)} %pad_maximum_fusion.6), channel_id=1, source_target_pairs={{0,16},{2,18},{4,20},{6,22},{8,24},{10,26},{12,28},{14,30},{16,0},... | collective-permute-start | bytes 221192 | tf_op jit(solution)/shard_map/ppermute | solution.py:622
  9.2 1.0 collective-permute-done.2
  10.3 2.8 %collective-permute-start.3 = (bf16[512,128]{1,0:T(8,128)(2,1)S(1)}, bf16[512,128]{1,0:T(8,128)(2,1)S(1)}, u32[]{:S(2)}, u32[]{:S(2)}) collective-permute-start(bf16[512,128]{1,0:T(8,128)(2,1)S(1)} %pad_maximum_fusion.5), channel_id=1, source_target_pairs={{0,8},{2,10},{4,12},{6,14},{8,0},{10,2},{12,4},{14,6},{16,24},{18,... | collective-permute-start | bytes 393224 | tf_op jit(solution)/shard_map/ppermute | solution.py:622
  13.5 2.0 collective-permute-done.3
  15.6 2.2 collective-permute-start.6
  18.4 3.3 %collective-permute-done.6 = bf16[960,128]{1,0:T(8,128)(2,1)S(1)} collective-permute-done((bf16[960,128]{1,0:T(8,128)(2,1)S(1)}, bf16[960,128]{1,0:T(8,128)(2,1)S(1)}, u32[]{:S(2)}, u32[]{:S(2)}) %collective-permute-start.6) | collective-permute-done | bytes 245792 | tf_op jit(solution)/shard_map/ppermute | solution.py:622
  21.7 6.3 %collective-permute-done.5 = bf16[960,128]{1,0:T(8,128)(2,1)S(1)} collective-permute-done((bf16[960,128]{1,0:T(8,128)(2,1)S(1)}, bf16[960,128]{1,0:T(8,128)(2,1)S(1)}, u32[]{:S(2)}, u32[]{:S(2)}) %collective-permute-start.5) | collective-permute-done | bytes 245792 | tf_op jit(solution)/shard_map/ppermute | solution.py:622
  31.7 2.3 collective-permute-start.7
  44.9 187.7 %shard_map.119 = (bf16[2,512,256]{2,1,0:T(8,128)(2,1)}, bf16[2,512,256]{2,1,0:T(8,128)(2,1)}, f32[2,512,256]{2,1,0:T(8,128)}, f32[2,512,256]{2,1,0:T(8,128)}, f3...) custom-call(s32[1]{0:T(128)} %bitcast.core_ref, ...), custom_call_target="tpu_custom_call" | custom-call | tf_op jit(solution)/shard_map/pallas_call | solution.py:557
  234.6 1.3 convert_element_type.162
  241.9 1.4 fusion
  243.4 1.3 collective-permute-start.11
  246.2 1.1 pad_maximum_fusion.1
  247.2 3.3 %collective-permute-done.11 = bf16[4,224,128]{2,1,0:T(8,128)(2,1)S(1)} collective-permute-done((bf16[4,224,128]{2,1,0:T(8,128)(2,1)S(1)}, bf16[4,224,128]{2,1,0:T(8,128)(2,1)S(1)}, u32[]{:S(2)}, u32[]{:S(2)}) %collective-permute-start.11) | collective-permute-done | bytes 229408 | tf_op jit(solution)/shard_map/ppermute | solution.py:622
  250.5 1.0 collective-permute-done.12
  251.5 4.7 %collective-permute-done.13 = bf16[4,224,128]{2,1,0:T(8,128)(2,1)S(1)} collective-permute-done((bf16[4,224,128]{2,1,0:T(8,128)(2,1)S(1)}, bf16[4,224,128]{2,1,0:T(8,128)(2,1)S(1)}, u32[]{:S(2)}, u32[]{:S(2)}) %collective-permute-start.13) | collective-permute-done | bytes 229408 | tf_op jit(solution)/shard_map/ppermute | solution.py:622
  256.4 2.0 collective-permute-start.14
  258.4 3.1 %collective-permute-start.15 = (bf16[1,224,128]{2,1,0:T(8,128)(2,1)S(1)}, bf16[1,224,128]{2,1,0:T(8,128)(2,1)S(1)}, u32[]{:S(2)}, u32[]{:S(2)}) collective-permute-start(bf16[1,224,128]{2,1,0:T(8,128)(2,1)S(1)} %get-tuple-element.53), channel_id=1, source_target_pairs={{0,16},{2,18},{4,20},{6,22},{8,24},{10,26},{12,28},{14,30},{16,0},... | collective-permute-start | bytes 172040 | tf_op jit(solution)/shard_map/ppermute | solution.py:622
  261.7 1.3 collective-permute-done.15
  263.0 3.3 %collective-permute-done.16 = bf16[1,224,128]{2,1,0:T(8,128)(2,1)S(1)} collective-permute-done((bf16[1,224,128]{2,1,0:T(8,128)(2,1)S(1)}, bf16[1,224,128]{2,1,0:T(8,128)(2,1)S(1)}, u32[]{:S(2)}, u32[]{:S(2)}) %collective-permute-start.16) | collective-permute-done | bytes 57376 | tf_op jit(solution)/shard_map/ppermute | solution.py:622
  266.3 3.1 %collective-permute-start.17 = (f32[2,107,128]{2,1,0:T(8,128)S(1)}, f32[2,107,128]{2,1,0:T(8,128)S(1)}, u32[]{:S(2)}, u32[]{:S(2)}) collective-permute-start(f32[2,107,128]{2,1,0:T(8,128)S(1)} %bitcast.82), channel_id=1, source_target_pairs={{0,1},{1,0},{2,3},{3,2},{4,5},{5,4},{6,7},{7,6},{8,9},{9,8},{10,11... | collective-permute-start | bytes 328712 | tf_op jit(solution)/shard_map/ppermute | solution.py:622
  269.4 1.5 pad_maximum_fusion
  271.0 1.4 broadcast_select_fusion.5
  (155 shorter events, 29.1 us)
Async XLA Ops:
  0.6 12.5 %copy-start.4 = (bf16[4,512,256]{2,1,0:T(8,128)(2,1)S(1)}, bf16[4,512,256]{2,1,0:T(8,128)(2,1)}, u32[]{:S(2)}) copy-start(bf16[4,512,256]{2,1,0:T(8,128)(2,1)} %param.9) | copy-start | bytes 3145732
  1.6 36.1 %copy-start.12 = (s32[32]{0:T(128)}, s32[32]{0:T(128)S(1)}, u32[]{:S(2)}) copy-start(s32[32]{0:T(128)S(1)} %convert_reduce_fusion) | copy-start | bytes 388
  2.3 11.3 %copy-start.16 = (pred[32]{0:T(512)(128)(4,1)}, pred[32]{0:T(512)(128)(4,1)S(1)}, u32[]{:S(2)}) copy-start(pred[32]{0:T(512)(128)(4,1)S(1)} %broadcast_compare_fusion) | copy-start | bytes 100
  5.2 12.6 %copy-start.15 = (s32[32]{0:T(128)S(1)}, s32[32]{0:T(128)}, u32[]{:S(2)}) copy-start(s32[32]{0:T(128)} %param.12) | copy-start | bytes 388
  5.3 4.9 %collective-permute-start.2 = (bf16[288,128]{1,0:T(8,128)(2,1)S(1)}, bf16[288,128]{1,0:T(8,128)(2,1)S(1)}, u32[]{:S(2)}, u32[]{:S(2)}) collective-permute-start(bf16[288,128]{1,0:T(8,128)(2,1)S(1)} %pad_maximum_fusion.6), channel_id=1, source_target_pairs={{0,16},{2,18},{4,20},{6,22},{8,24},{10,26},{12,28},{14,30},{16,0},... | collective-permute-start | bytes 221192 | tf_op jit(solution)/shard_map/ppermute | solution.py:622
  10.3 5.2 %collective-permute-start.3 = (bf16[512,128]{1,0:T(8,128)(2,1)S(1)}, bf16[512,128]{1,0:T(8,128)(2,1)S(1)}, u32[]{:S(2)}, u32[]{:S(2)}) collective-permute-start(bf16[512,128]{1,0:T(8,128)(2,1)S(1)} %pad_maximum_fusion.5), channel_id=1, source_target_pairs={{0,8},{2,10},{4,12},{6,14},{8,0},{10,2},{12,4},{14,6},{16,24},{18,... | collective-permute-start | bytes 393224 | tf_op jit(solution)/shard_map/ppermute | solution.py:622
  13.5 20.5 %copy-start = (bf16[4,512,256]{2,1,0:T(8,128)(2,1)}, bf16[4,512,256]{2,1,0:T(8,128)(2,1)S(1)}, u32[]{:S(2)}) copy-start(bf16[4,512,256]{2,1,0:T(8,128)(2,1)S(1)} %broadcast_multiply_fusion.up_kept_ref) | copy-start | bytes 3145732
  15.6 6.1 %collective-permute-start.6 = (bf16[960,128]{1,0:T(8,128)(2,1)S(1)}, bf16[960,128]{1,0:T(8,128)(2,1)S(1)}, u32[]{:S(2)}, u32[]{:S(2)}) collective-permute-start(bf16[960,128]{1,0:T(8,128)(2,1)S(1)} %pad_maximum_fusion.4), channel_id=1, source_target_pairs={{0,6},{2,4},{4,2},{6,0},{8,14},{10,12},{12,10},{14,8},{16,22},{18,... | collective-permute-start | bytes 737288 | tf_op jit(solution)/shard_map/ppermute | solution.py:622
  17.8 10.2 %collective-permute-start.5 = (bf16[960,128]{1,0:T(8,128)(2,1)S(1)}, bf16[960,128]{1,0:T(8,128)(2,1)S(1)}, u32[]{:S(2)}, u32[]{:S(2)}) collective-permute-start(bf16[960,128]{1,0:T(8,128)(2,1)S(1)} %pad_maximum_fusion.4), channel_id=1, source_target_pairs={{0,4},{2,6},{4,0},{6,2},{8,12},{10,14},{12,8},{14,10},{16,20},{18,... | collective-permute-start | bytes 737288 | tf_op jit(solution)/shard_map/ppermute | solution.py:622
  18.1 9.9 %collective-permute-start.4 = (bf16[960,128]{1,0:T(8,128)(2,1)S(1)}, bf16[960,128]{1,0:T(8,128)(2,1)}, u32[]{:S(2)}, u32[]{:S(2)}) collective-permute-start(bf16[960,128]{1,0:T(8,128)(2,1)S(1)} %pad_maximum_fusion.4), channel_id=1, source_target_pairs={{0,2},{2,0},{4,6},{6,4},{8,10},{10,8},{12,14},{14,12},{16,18},{18,... | collective-permute-start | bytes 737288 | tf_op jit(solution)/shard_map/ppermute | solution.py:622
  31.7 6.8 %collective-permute-start.7 = (bf16[3648,128]{1,0:T(8,128)(2,1)}, bf16[3648,128]{1,0:T(8,128)(2,1)S(1)}, u32[]{:S(2)}, u32[]{:S(2)}) collective-permute-start(bf16[3648,128]{1,0:T(8,128)(2,1)} %pad_maximum_fusion.2), channel_id=1, source_target_pairs={{0,1},{1,0},{2,3},{3,2},{4,5},{5,4},{6,7},{7,6},{8,9},{9,8},{10,11... | collective-permute-start | bytes 2801672 | tf_op jit(solution)/shard_map/ppermute | solution.py:622
  34.1 10.8 %collective-permute-start.1 = (bf16[2,512,256]{2,1,0:T(8,128)(2,1)S(1)}, bf16[2,512,256]{2,1,0:T(8,128)(2,1)}, u32[]{:S(2)}, u32[]{:S(2)}) collective-permute-start(bf16[2,512,256]{2,1,0:T(8,128)(2,1)S(1)} %constant_dynamic-slice_fusion.3), channel_id=1, source_target_pairs={{0,1},{1,0},{2,3},{3,2},{4,5},{5,4},{6,7},{7,6},{8,9},{9,8},{10,11... | collective-permute-start | bytes 1572872 | tf_op jit(solution)/shard_map/ppermute | solution.py:622
  35.0 9.8 %collective-permute-start = (bf16[2,512,256]{2,1,0:T(8,128)(2,1)}, bf16[2,512,256]{2,1,0:T(8,128)(2,1)}, u32[]{:S(2)}, u32[]{:S(2)}) collective-permute-start(bf16[2,512,256]{2,1,0:T(8,128)(2,1)} %constant_dynamic-slice_fusion.4), channel_id=1, source_target_pairs={{0,1},{1,0},{2,3},{3,2},{4,5},{5,4},{6,7},{7,6},{8,9},{9,8},{10,11... | collective-permute-start | bytes 1572872 | tf_op jit(solution)/shard_map/ppermute | solution.py:622
  239.2 2.7 collective-permute-start.10
  240.3 21.2 %collective-permute-start.9 = (f32[2,512,256]{2,1,0:T(8,128)}, f32[2,512,256]{2,1,0:T(8,128)S(1)}, u32[]{:S(2)}, u32[]{:S(2)}) collective-permute-start(f32[2,512,256]{2,1,0:T(8,128)} %get-tuple-element.21), channel_id=1, source_target_pairs={{0,1},{1,0},{2,3},{3,2},{4,5},{5,4},{6,7},{7,6},{8,9},{9,8},{10,11... | collective-permute-start | bytes 3145736 | tf_op jit(solution)/shard_map/ppermute | solution.py:622
  240.8 5.3 %collective-permute-start.8 = (bf16[2,512,256]{2,1,0:T(8,128)(2,1)S(1)}, bf16[2,512,256]{2,1,0:T(8,128)(2,1)S(1)}, u32[]{:S(2)}, u32[]{:S(2)}) collective-permute-start(bf16[2,512,256]{2,1,0:T(8,128)(2,1)S(1)} %copy-done.18), channel_id=1, source_target_pairs={{0,1},{1,0},{2,3},{3,2},{4,5},{5,4},{6,7},{7,6},{8,9},{9,8},{10,11... | collective-permute-start | bytes 1572872 | tf_op jit(solution)/shard_map/ppermute | solution.py:622
  243.4 7.1 %collective-permute-start.11 = (bf16[4,224,128]{2,1,0:T(8,128)(2,1)S(1)}, bf16[4,224,128]{2,1,0:T(8,128)(2,1)S(1)}, u32[]{:S(2)}, u32[]{:S(2)}) collective-permute-start(bf16[4,224,128]{2,1,0:T(8,128)(2,1)S(1)} %get-tuple-element.40), channel_id=1, source_target_pairs={{0,2},{2,0},{4,6},{6,4},{8,10},{10,8},{12,14},{14,12},{16,18},{18,... | collective-permute-start | bytes 688136 | tf_op jit(solution)/shard_map/ppermute | solution.py:622
  244.6 6.9 %collective-permute-start.12 = (bf16[4,224,128]{2,1,0:T(8,128)(2,1)S(1)}, bf16[4,224,128]{2,1,0:T(8,128)(2,1)S(1)}, u32[]{:S(2)}, u32[]{:S(2)}) collective-permute-start(bf16[4,224,128]{2,1,0:T(8,128)(2,1)S(1)} %get-tuple-element.42), channel_id=1, source_target_pairs={{0,4},{2,6},{4,0},{6,2},{8,12},{10,14},{12,8},{14,10},{16,20},{18,... | collective-permute-start | bytes 688136 | tf_op jit(solution)/shard_map/ppermute | solution.py:622
  245.1 11.1 %collective-permute-start.13 = (bf16[4,224,128]{2,1,0:T(8,128)(2,1)S(1)}, bf16[4,224,128]{2,1,0:T(8,128)(2,1)S(1)}, u32[]{:S(2)}, u32[]{:S(2)}) collective-permute-start(bf16[4,224,128]{2,1,0:T(8,128)(2,1)S(1)} %get-tuple-element.41), channel_id=1, source_target_pairs={{0,6},{2,4},{4,2},{6,0},{8,14},{10,12},{12,10},{14,8},{16,22},{18,... | collective-permute-start | bytes 688136 | tf_op jit(solution)/shard_map/ppermute | solution.py:622
  246.2 15.3 %copy-start.3 = (f32[2,512,256]{2,1,0:T(8,128)S(1)}, f32[2,512,256]{2,1,0:T(8,128)}, u32[]{:S(2)}) copy-start(f32[2,512,256]{2,1,0:T(8,128)} %get-tuple-element.20) | copy-start | bytes 3145732
  256.4 5.3 %collective-permute-start.14 = (bf16[1,224,128]{2,1,0:T(8,128)(2,1)S(1)}, bf16[1,224,128]{2,1,0:T(8,128)(2,1)S(1)}, u32[]{:S(2)}, u32[]{:S(2)}) collective-permute-start(bf16[1,224,128]{2,1,0:T(8,128)(2,1)S(1)} %get-tuple-element.51), channel_id=1, source_target_pairs={{0,8},{2,10},{4,12},{6,14},{8,0},{10,2},{12,4},{14,6},{16,24},{18,... | collective-permute-start | bytes 172040 | tf_op jit(solution)/shard_map/ppermute | solution.py:622
  258.4 4.7 %collective-permute-start.15 = (bf16[1,224,128]{2,1,0:T(8,128)(2,1)S(1)}, bf16[1,224,128]{2,1,0:T(8,128)(2,1)S(1)}, u32[]{:S(2)}, u32[]{:S(2)}) collective-permute-start(bf16[1,224,128]{2,1,0:T(8,128)(2,1)S(1)} %get-tuple-element.53), channel_id=1, source_target_pairs={{0,16},{2,18},{4,20},{6,22},{8,24},{10,26},{12,28},{14,30},{16,0},... | collective-permute-start | bytes 172040 | tf_op jit(solution)/shard_map/ppermute | solution.py:622
  261.5 4.8 %collective-permute-start.16 = (bf16[1,224,128]{2,1,0:T(8,128)(2,1)S(1)}, bf16[1,224,128]{2,1,0:T(8,128)(2,1)S(1)}, u32[]{:S(2)}, u32[]{:S(2)}) collective-permute-start(bf16[1,224,128]{2,1,0:T(8,128)(2,1)S(1)} %get-tuple-element.52), channel_id=1, source_target_pairs={{0,24},{2,26},{4,28},{6,30},{8,16},{10,18},{12,20},{14,22},{16,8},... | collective-permute-start | bytes 172040 | tf_op jit(solution)/shard_map/ppermute | solution.py:622
  266.3 4.6 %collective-permute-start.17 = (f32[2,107,128]{2,1,0:T(8,128)S(1)}, f32[2,107,128]{2,1,0:T(8,128)S(1)}, u32[]{:S(2)}, u32[]{:S(2)}) collective-permute-start(f32[2,107,128]{2,1,0:T(8,128)S(1)} %bitcast.82), channel_id=1, source_target_pairs={{0,1},{1,0},{2,3},{3,2},{4,5},{5,4},{6,7},{7,6},{8,9},{9,8},{10,11... | collective-permute-start | bytes 328712 | tf_op jit(solution)/shard_map/ppermute | solution.py:622
  (13 other events, 32.6 us)

commit v5 on v4

--- a/solution.py
+++ b/solution.py
@@ -88,11 +88,11 @@
     out_given_ref,
     gin_kept_ref,
     gin_given_ref,
-    gwin_ref,
-    gwout_ref,
-    gsmall_ref,
-    gvec_ref,
-    ggain_ref,
+    gwin_out,
+    gwout_out,
+    gsmall_out,
+    gvec_out,
+    ggain_out,
     states,
     act_s,
     slope_s,
@@ -127,6 +127,11 @@
     near_s,
     wx_s,
     wdt_s,
+    gwin_ref,
+    gwout_ref,
+    gsmall_ref,
+    gvec_ref,
+    ggain_ref,
 ):
     window = pl.program_id(0)
     natural = pl.program_id(1)
@@ -161,9 +166,9 @@
         for k in range(2):
             fold_s[k] = jnp.where(lanes == STATE * (k + 1) + rows % STATE, 1.0, 0.0).astype(BF)
         rows, lanes = iota((GROUP, WIDE), 0), iota((GROUP, WIDE), 1)
-        mask = jnp.where(rows == lanes // STATE, 1.0, 0.0)
-        mask_s[...] = mask
-        sums_s[:GROUP, :] = mask.astype(BF)
+        mask_s[0] = jnp.where(GROUP - 1 - rows == lanes // STATE, 1.0, 0.0)
+        mask_s[1] = jnp.where(rows == lanes // STATE, 1.0, 0.0)
+        sums_s[:GROUP, :] = mask_s[0].astype(BF)
         sums_s[GROUP:, :] = jnp.where(rows == lanes % STATE, 1.0, 0.0).astype(BF)
 
     @pl.when(natural == 0)
@@ -189,14 +194,18 @@
         inv = lax.rsqrt(jnp.mean(xf * xf, axis=-1, keepdims=True) + NORM_EPSILON)
         return xf, inv
 
-    def load_copies(chunk):
-        there = span(place_of(chunk), CHUNK)
-        xf, inv = norm_parts(there)
+    def load_copies(slab):
+        rows = span(slab * SLAB, SLAB)
+        xf, inv = norm_parts(rows)
         normed = (xf * inv * gain_ref[...]).astype(BF)
-        copy_s[span(chunk * CHUNK, CHUNK), :] = dot(flip_s[natural], normed).astype(BF)
-        dmix_s[span(chunk * CHUNK, CHUNK), :] = dot(flip_s[natural], up_s[there, :]).astype(BF)
-
-    each(chunks, load_copies)
+        upstream = up_s[rows, :]
+        for k in range(SLAB // CHUNK):
+            part = slice(k * CHUNK, (k + 1) * CHUNK)
+            there = span(place_of(slab * (SLAB // CHUNK) + k), CHUNK)
+            copy_s[there, :] = dot(flip_s[natural], normed[part]).astype(BF)
+            dmix_s[there, :] = dot(flip_s[natural], upstream[part]).astype(BF)
+
+    each(slabs, load_copies)
 
     def project(slab):
         row = slab * SLAB
@@ -208,7 +217,7 @@
             rows = span(row + a, BLOCK)
             gate = gate_all[a : a + BLOCK].astype(F32)
             dgated = dgated_all[a : a + BLOCK].astype(F32)
-            sig = 1.0 / (1.0 + jnp.exp(-gate))
+            sig = 0.5 + 0.5 * jnp.tanh(0.5 * gate)
             silu = gate * sig
             gsilu_s[rows, :] = silu
             dscan_s[rows, :] = dgated * silu
@@ -224,7 +233,7 @@
             conv = vec_ref[4:5, :]
             for j in range(KERNEL):
                 conv = conv + vec_ref[j : j + 1, :] * near_s[a + 13 + j : a + 13 + j + BLOCK, :]
-            sig = 1.0 / (1.0 + jnp.exp(-conv))
+            sig = 0.5 + 0.5 * jnp.tanh(0.5 * conv)
             act = conv * sig
             act_s[rows, :] = act
             slope_s[rows, :] = sig + act * (1.0 - sig)
@@ -238,15 +247,18 @@
         for kind, target in ((0, entry_s), (1, read_s)):
             wide = dot(proj_high, tile_s[kind])
             for g in range(SLAB // GROUP):
-                part = wide[g * GROUP : (g + 1) * GROUP] * mask_s[...]
+                part = wide[g * GROUP : (g + 1) * GROUP] * mask_s[kind]
                 target[span(row + g * GROUP, GROUP), :] = part.astype(BF)
         pre_all = dot(proj_high, wdt_s[...]) + dot(proj_low, wdt_s[...])
         for a in pieces:
             rows = span(row + a, BLOCK)
             pre = pre_all[a : a + BLOCK] + vec_ref[5:6, :]
             small = jnp.exp(-jnp.abs(pre))
-            delta = jnp.maximum(pre, 0.0) + jnp.log1p(small)
-            scaled = jnp.where(pre >= 0.0, 1.0, small) / ((1.0 + small) * delta)
+            whole = 1.0 + small
+            share = 1.0 / whole
+            log_part = jnp.log(whole) + (small - (whole - 1.0)) * share
+            delta = jnp.maximum(pre, 0.0) + log_part
+            scaled = jnp.where(pre >= 0.0, share, small * share) / delta
             delta_s[rows, :] = delta
             ratio_s[rows, :] = jnp.where(delta > 1e-30, scaled, 1.0)
             u_s[rows, :] = delta * act_s[rows, :]
@@ -301,7 +313,7 @@
                 sums.append(pack(*total))
             y_s[rows, :] = dot(read_s[rows, :], jnp.concatenate(held, axis=0))
             found = dot(ones, jnp.concatenate(sums, axis=0), NT)
-            wide_s[rows, :] = (found * mask_s[...]).astype(BF)
+            wide_s[rows, :] = (found * mask_s[1]).astype(BF)
         return tuple(state[0] + state[1] + last)
 
     lax.fori_loop(0, length // REACH, scan_chunk, (zero,) * 8 + (pack(zero, zero),) * 4)
@@ -398,15 +410,15 @@
                         both.append(power * carry[h][e])
                     held_row.append(pack(*lams))
                     prod_row.append(pack(*both) * before)
-                held.insert(0, jnp.concatenate(held_row, axis=1))
-                prods.insert(0, jnp.concatenate(prod_row, axis=1))
-                sums.insert(0, pack(*total))
+                held.append(jnp.concatenate(held_row, axis=1))
+                prods.append(jnp.concatenate(prod_row, axis=1))
+                sums.append(pack(*total))
             y_s[rows, :] = dot(entry_s[rows, :], jnp.concatenate(held, axis=0))
             both = dot(sums_s[...], jnp.concatenate(prods, axis=0))
             gslope_s[rows, :] = both[:GROUP]
             rate_sum = rate_sum + both[GROUP:]
             found = dot(ones, jnp.concatenate(sums, axis=0), NT)
-            wide_s[rows, :] = (found * mask_s[...]).astype(BF)
+            wide_s[rows, :] = (found * mask_s[0]).astype(BF)
         return tuple(carry[0] + carry[1]) + (rate_sum,)
 
     done = lax.fori_loop(
@@ -498,6 +510,17 @@
 
     gwin_ref[...] += dot(copy_s[...], dproj_s[...], TN)
 
+    @pl.when((window == pl.num_programs(0) - 1) & (natural == 1))
+    def _():
+        gwin_out[...] = gwin_ref[...].astype(BF)
+        gwout_out[...] = gwout_ref[...].astype(BF)
+        gsmall_out[...] = gsmall_ref[...].astype(BF)
+        vectors = [jnp.sum(gvec_ref[j], axis=0, keepdims=True) for j in range(7)]
+        vectors.append(jnp.zeros((9, INNER), F32))
+        gvec_out[...] = jnp.concatenate(vectors, axis=0).astype(BF)
+        gain = jnp.sum(ggain_ref[...], axis=0, keepdims=True)
+        ggain_out[...] = jnp.broadcast_to(gain, (16, D)).astype(BF)
+
 
 def run_layer(
     core, x, x_got, up, up_got, perm, w_in, w_x, w_dt, w_out, conv_w, conv_b, dt_bias, a_log, d_skip, gain
@@ -516,11 +539,11 @@
     got = pl.BlockSpec((1, half, D), lambda w, q, core: (w, 0, 0))
     fixed = (perm, w_in, w_out, w_x, w_dt, vec, rate, gain[None])
     grads = [
-        jax.ShapeDtypeStruct((D, 2 * INNER), F32),
-        jax.ShapeDtypeStruct((INNER, D), F32),
-        jax.ShapeDtypeStruct((5 * STATE, INNER), F32),
-        jax.ShapeDtypeStruct((7, 8, INNER), F32),
-        jax.ShapeDtypeStruct((8, D), F32),
+        jax.ShapeDtypeStruct((D, 2 * INNER), BF),
+        jax.ShapeDtypeStruct((INNER, D), BF),
+        jax.ShapeDtypeStruct((5 * STATE, INNER), BF),
+        jax.ShapeDtypeStruct((16, INNER), BF),
+        jax.ShapeDtypeStruct((16, D), BF),
     ]
     inner_f32 = [pltpu.VMEM((length, INNER), F32)]
     outer_bf = [pltpu.VMEM((length, D), BF)]
@@ -548,10 +571,15 @@
             pltpu.VMEM((2, LANES, WIDE), BF),
             pltpu.VMEM((2, WIDE, LANES), BF),
             pltpu.VMEM((2 * GROUP, WIDE), BF),
-            pltpu.VMEM((GROUP, WIDE), F32),
+            pltpu.VMEM((2, GROUP, WIDE), F32),
             pltpu.VMEM((SLAB + 16, INNER), F32),
             pltpu.VMEM((INNER, LANES), BF),
             pltpu.VMEM((LANES, INNER), BF),
+            pltpu.VMEM((D, 2 * INNER), F32),
+            pltpu.VMEM((INNER, D), F32),
+            pltpu.VMEM((5 * STATE, INNER), F32),
+            pltpu.VMEM((7, 8, INNER), F32),
+            pltpu.VMEM((8, D), F32),
         ]
     )
     return pl.pallas_call(
@@ -573,18 +601,17 @@
 
 def layer_grads(results):
     gwin, gwout, gsmall, gvec, ggain = results
-    vec = jnp.sum(gvec, axis=1)
     return [
         gwin,
         gsmall[2 * STATE :].T,
         gsmall[STATE : 2 * STATE],
         gwout,
-        vec[:KERNEL].T,
-        vec[4],
-        vec[5],
+        gvec[:KERNEL].T,
+        gvec[4],
+        gvec[5],
         gsmall[:STATE].T,
-        vec[6],
-        jnp.sum(ggain, axis=0),
+        gvec[6],
+        ggain[0],
     ]
 
 
@@ -632,7 +659,7 @@
     return jnp.pad(value, widths)
 
 
-def gather_params(weights, owners, rank, matches):
+def gather_params(weights, owners, rank):
     size = lax.axis_size("dp")
     me = lax.axis_index("dp")
     core = lax.axis_index("seq")
@@ -647,7 +674,12 @@
     many = pad_rows(mine, padded, 1).reshape(pair * padded, LANES)
     first = MATRIX_END // block_len
     last = (PARAMS - 1) // block_len + 1
-    here = matches[:, first:last].T[:, :, None, None]
+    own = owners == me
+    order = jnp.arange(blocks, dtype=jnp.int32)
+    before = order[None, :] < order[first:last, None]
+    earlier = jnp.sum((before & own[None, :]).astype(jnp.int32), axis=1)
+    slot = jnp.where(own[first:last], earlier, SLOTS)
+    here = (slot[:, None] == jnp.arange(SLOTS, dtype=jnp.int32)[None, :])[:, :, None, None]
     fine = jnp.sum(jnp.where(here, (tiles - rounded)[None], 0.0), axis=1).astype(BF)
     fine_rows = (last - first) * rows
     fine_half = up_to(fine_rows, 32) // 2
@@ -671,12 +703,10 @@
         fine = fine + item[count:]
     spot = (spot + (away & (near - 1)) * (size // near)) * pair + rank % pair
     chosen = many.reshape(size * pair, padded, LANES)[spot]
-    sent = jnp.concatenate([chosen.reshape(blocks * padded, LANES), fine], axis=0)
-    got = swap(sent, "seq", 1)
-    theirs = got[: blocks * padded].reshape(blocks, padded, LANES)
+    theirs = swap(chosen, "seq", 1)
+    fine_got = swap(fine, "seq", 1)
     local = (rank // pair == core)[:, None, None]
     theta = jnp.where(local, chosen, theirs)[:, :rows].reshape(blocks * rows, LANES)
-    fine_got = got[blocks * padded :]
     fine = jnp.concatenate(
         [jnp.where(core == 0, fine, fine_got), jnp.where(core == 0, fine_got, fine)], axis=0
     )
@@ -731,7 +761,7 @@
     )
     occupied = jnp.any(matches, axis=1)
     block_of = jnp.sum(jnp.where(matches, order[None, :], 0), axis=1)
-    theta, fine = gather_params(weights, owners, rank, matches)
+    theta, fine = gather_params(weights, owners, rank)
     upstream = cotangent * loss_mask.astype(BF)[..., None]
     x_got = other_half(inputs, core)
     up_got = other_half(upstream, core)

time: 273 us -> 266 us (0.974)
  Pallas kernels: 188 us -> 180 us
  local copies, waits for them, and re-layouts: 13.4 us -> 19.2 us
  other arithmetic: 19.3 us -> 16.2 us
  waiting for transfers between devices: 27.2 us -> 24.1 us
    pallas_call x1, Pallas kernels: 188 us -> 180 us  [run_layer(): pl.pallas_call(layer_kernel, grid_spec=pltpu.PrefetchScalarGridSpec(num_s...]
    ppermute x18 -> x19, waiting for transfers between devices: 27.2 us -> 24.1 us  [swap(): return lax.ppermute(value, axis, [(i, i ^ bit) for i in range(size)])]
    ppermute x18 -> x19, starting transfers between devices: 23.3 us -> 22.8 us  [swap(): return lax.ppermute(value, axis, [(i, i ^ bit) for i in range(size)])]
  transfers between devices with their start and end apart: 18 -> 19, of which waited for: 10 -> 9; matrix products, arithmetic and copies ran while one was open for 6% -> 7% of each run, Pallas kernels for 0% -> 0%
where the time goes in v5:
time: 266 us; the launch traced here: 265 us
  Pallas kernels  180 us (68%)
  waiting for transfers between devices  24.1 us (9%)
  starting transfers between devices  22.8 us (9%)
  local copies, waits for them, and re-layouts  19.2 us (7%)
  other arithmetic  16.2 us (6%)
    pallas_call x1, Pallas kernels, run_layer(): pl.pallas_call(layer_kernel, grid_spec=pltpu.PrefetchScalarGridSpec(num_s...  180 us
    ppermute x19, waiting for transfers between devices, swap(): return lax.ppermute(value, axis, [(i, i ^ bit) for i in range(size)])  24.1 us
    ppermute x19, starting transfers between devices, swap(): return lax.ppermute(value, axis, [(i, i ^ bit) for i in range(size)])  22.8 us
  transfers between devices with their start and end apart: 19, of which 9 were waited for; matrix products, arithmetic and copies ran while one was open for 7% of the time, Pallas kernels for 0%

profile of v5, /device:TPU:1, one launch (start us, length us, event | category | flops | bytes accessed | tf_op | source)
XLA Modules:
  0.0 265.3 jit_solution(3575767566365841108)
XLA Ops:
  2.1 1.9 compare_select_fusion.2
  7.0 1.2 select_reduce_fusion
  8.4 3.2 %collective-permute-start.2 = (bf16[288,128]{1,0:T(8,128)(2,1)S(1)}, bf16[288,128]{1,0:T(8,128)(2,1)S(1)}, u32[]{:S(2)}, u32[]{:S(2)}) collective-permute-start(bf16[288,128]{1,0:T(8,128)(2,1)S(1)} %pad_maximum_fusion.5), channel_id=1, source_target_pairs={{0,16},{2,18},{4,20},{6,22},{8,24},{10,26},{12,28},{14,30},{16,0},... | collective-permute-start | bytes 221192 | tf_op jit(solution)/shard_map/ppermute | solution.py:649
  12.3 1.6 broadcast_multiply_fusion.up_kept_ref
  14.0 2.3 collective-permute-start.3
  16.3 1.1 collective-permute-start.1
  19.4 2.2 collective-permute-start.6
  22.6 2.8 %collective-permute-done.6 = bf16[960,128]{1,0:T(8,128)(2,1)S(1)} collective-permute-done((bf16[960,128]{1,0:T(8,128)(2,1)S(1)}, bf16[960,128]{1,0:T(8,128)(2,1)S(1)}, u32[]{:S(2)}, u32[]{:S(2)}) %collective-permute-start.6) | collective-permute-done | bytes 245792 | tf_op jit(solution)/shard_map/ppermute | solution.py:649
  25.5 6.5 %collective-permute-done.5 = bf16[960,128]{1,0:T(8,128)(2,1)S(1)} collective-permute-done((bf16[960,128]{1,0:T(8,128)(2,1)S(1)}, bf16[960,128]{1,0:T(8,128)(2,1)S(1)}, u32[]{:S(2)}, u32[]{:S(2)}) %collective-permute-start.5) | collective-permute-done | bytes 245792 | tf_op jit(solution)/shard_map/ppermute | solution.py:649
  32.9 2.1 collective-permute-start.7
  43.4 180.3 %shard_map.119 = (bf16[2,512,256]{2,1,0:T(8,128)(2,1)}, bf16[2,512,256]{2,1,0:T(8,128)(2,1)}, f32[2,512,256]{2,1,0:T(8,128)}, f32[2,512,256]{2,1,0:T(8,128)}, bf...) custom-call(s32[1]{0:T(128)} %bitcast.core_ref, ...), custom_call_target="tpu_custom_call" | custom-call | tf_op jit(solution)/shard_map/pallas_call | solution.py:585
  226.8 1.3 reshape.219
  235.4 1.4 fusion
  236.9 1.3 collective-permute-start.12
  238.2 1.2 collective-permute-start.13
  240.8 3.0 %collective-permute-done.12 = bf16[4,224,128]{2,1,0:T(8,128)(2,1)S(1)} collective-permute-done((bf16[4,224,128]{2,1,0:T(8,128)(2,1)S(1)}, bf16[4,224,128]{2,1,0:T(8,128)(2,1)S(1)}, u32[]{:S(2)}, u32[]{:S(2)}) %collective-permute-start.12) | collective-permute-done | bytes 229408 | tf_op jit(solution)/shard_map/ppermute | solution.py:649
  244.7 5.0 %collective-permute-done.14 = bf16[4,224,128]{2,1,0:T(8,128)(2,1)S(1)} collective-permute-done((bf16[4,224,128]{2,1,0:T(8,128)(2,1)S(1)}, bf16[4,224,128]{2,1,0:T(8,128)(2,1)S(1)}, u32[]{:S(2)}, u32[]{:S(2)}) %collective-permute-start.14) | collective-permute-done | bytes 229408 | tf_op jit(solution)/shard_map/ppermute | solution.py:649
  249.8 1.4 collective-permute-start.15
  251.2 3.0 %collective-permute-start.16 = (bf16[1,224,128]{2,1,0:T(8,128)(2,1)S(1)}, bf16[1,224,128]{2,1,0:T(8,128)(2,1)S(1)}, u32[]{:S(2)}, u32[]{:S(2)}) collective-permute-start(bf16[1,224,128]{2,1,0:T(8,128)(2,1)S(1)} %get-tuple-element.53), channel_id=1, source_target_pairs={{0,16},{2,18},{4,20},{6,22},{8,24},{10,26},{12,28},{14,30},{16,0},... | collective-permute-start | bytes 172040 | tf_op jit(solution)/shard_map/ppermute | solution.py:649
  254.4 1.3 collective-permute-done.16
  255.8 3.3 %collective-permute-done.17 = bf16[1,224,128]{2,1,0:T(8,128)(2,1)S(1)} collective-permute-done((bf16[1,224,128]{2,1,0:T(8,128)(2,1)S(1)}, bf16[1,224,128]{2,1,0:T(8,128)(2,1)S(1)}, u32[]{:S(2)}, u32[]{:S(2)}) %collective-permute-start.17) | collective-permute-done | bytes 57376 | tf_op jit(solution)/shard_map/ppermute | solution.py:649
  259.1 3.2 %collective-permute-start.18 = (f32[2,107,128]{2,1,0:T(8,128)S(1)}, f32[2,107,128]{2,1,0:T(8,128)S(1)}, u32[]{:S(2)}, u32[]{:S(2)}) collective-permute-start(f32[2,107,128]{2,1,0:T(8,128)S(1)} %bitcast.77), channel_id=1, source_target_pairs={{0,1},{1,0},{2,3},{3,2},{4,5},{5,4},{6,7},{7,6},{8,9},{9,8},{10,11... | collective-permute-start | bytes 328712 | tf_op jit(solution)/shard_map/ppermute | solution.py:649
  262.3 1.5 pad_maximum_fusion
  263.9 1.4 broadcast_select_fusion.5
  (143 shorter events, 29.2 us)
Async XLA Ops:
  1.5 33.4 %copy-start.9 = (s32[32]{0:T(128)}, s32[32]{0:T(128)S(1)}, u32[]{:S(2)}) copy-start(s32[32]{0:T(128)S(1)} %convert_reduce_fusion) | copy-start | bytes 388
  8.2 9.2 %copy-start.1 = (bf16[4,512,256]{2,1,0:T(8,128)(2,1)S(1)}, bf16[4,512,256]{2,1,0:T(8,128)(2,1)}, u32[]{:S(2)}) copy-start(bf16[4,512,256]{2,1,0:T(8,128)(2,1)} %x_kept_ref.1) | copy-start | bytes 3145732
  8.4 5.5 %collective-permute-start.2 = (bf16[288,128]{1,0:T(8,128)(2,1)S(1)}, bf16[288,128]{1,0:T(8,128)(2,1)S(1)}, u32[]{:S(2)}, u32[]{:S(2)}) collective-permute-start(bf16[288,128]{1,0:T(8,128)(2,1)S(1)} %pad_maximum_fusion.5), channel_id=1, source_target_pairs={{0,16},{2,18},{4,20},{6,22},{8,24},{10,26},{12,28},{14,30},{16,0},... | collective-permute-start | bytes 221192 | tf_op jit(solution)/shard_map/ppermute | solution.py:649
  13.9 11.6 %copy-start = (bf16[4,512,256]{2,1,0:T(8,128)(2,1)}, bf16[4,512,256]{2,1,0:T(8,128)(2,1)S(1)}, u32[]{:S(2)}) copy-start(bf16[4,512,256]{2,1,0:T(8,128)(2,1)S(1)} %broadcast_multiply_fusion.up_kept_ref) | copy-start | bytes 3145732
  14.0 5.3 %collective-permute-start.3 = (bf16[512,128]{1,0:T(8,128)(2,1)S(1)}, bf16[512,128]{1,0:T(8,128)(2,1)S(1)}, u32[]{:S(2)}, u32[]{:S(2)}) collective-permute-start(bf16[512,128]{1,0:T(8,128)(2,1)S(1)} %pad_maximum_fusion.4), channel_id=1, source_target_pairs={{0,8},{2,10},{4,12},{6,14},{8,0},{10,2},{12,4},{14,6},{16,24},{18,... | collective-permute-start | bytes 393224 | tf_op jit(solution)/shard_map/ppermute | solution.py:649
  16.3 27.1 %collective-permute-start.1 = (bf16[2,512,256]{2,1,0:T(8,128)(2,1)S(1)}, bf16[2,512,256]{2,1,0:T(8,128)(2,1)}, u32[]{:S(2)}, u32[]{:S(2)}) collective-permute-start(bf16[2,512,256]{2,1,0:T(8,128)(2,1)S(1)} %constant_dynamic-slice_fusion.3), channel_id=1, source_target_pairs={{0,1},{1,0},{2,3},{3,2},{4,5},{5,4},{6,7},{7,6},{8,9},{9,8},{10,11... | collective-permute-start | bytes 1572872 | tf_op jit(solution)/shard_map/ppermute | solution.py:649
  18.2 25.2 %collective-permute-start = (bf16[2,512,256]{2,1,0:T(8,128)(2,1)}, bf16[2,512,256]{2,1,0:T(8,128)(2,1)}, u32[]{:S(2)}, u32[]{:S(2)}) collective-permute-start(bf16[2,512,256]{2,1,0:T(8,128)(2,1)} %constant_dynamic-slice_fusion.4), channel_id=1, source_target_pairs={{0,1},{1,0},{2,3},{3,2},{4,5},{5,4},{6,7},{7,6},{8,9},{9,8},{10,11... | collective-permute-start | bytes 1572872 | tf_op jit(solution)/shard_map/ppermute | solution.py:649
  19.4 6.1 %collective-permute-start.6 = (bf16[960,128]{1,0:T(8,128)(2,1)S(1)}, bf16[960,128]{1,0:T(8,128)(2,1)S(1)}, u32[]{:S(2)}, u32[]{:S(2)}) collective-permute-start(bf16[960,128]{1,0:T(8,128)(2,1)S(1)} %pad_maximum_fusion.3), channel_id=1, source_target_pairs={{0,6},{2,4},{4,2},{6,0},{8,14},{10,12},{12,10},{14,8},{16,22},{18,... | collective-permute-start | bytes 737288 | tf_op jit(solution)/shard_map/ppermute | solution.py:649
  22.1 9.8 %collective-permute-start.4 = (bf16[960,128]{1,0:T(8,128)(2,1)S(1)}, bf16[960,128]{1,0:T(8,128)(2,1)S(1)}, u32[]{:S(2)}, u32[]{:S(2)}) collective-permute-start(bf16[960,128]{1,0:T(8,128)(2,1)S(1)} %pad_maximum_fusion.3), channel_id=1, source_target_pairs={{0,2},{2,0},{4,6},{6,4},{8,10},{10,8},{12,14},{14,12},{16,18},{18,... | collective-permute-start | bytes 737288 | tf_op jit(solution)/shard_map/ppermute | solution.py:649
  22.4 9.6 %collective-permute-start.5 = (bf16[960,128]{1,0:T(8,128)(2,1)S(1)}, bf16[960,128]{1,0:T(8,128)(2,1)S(1)}, u32[]{:S(2)}, u32[]{:S(2)}) collective-permute-start(bf16[960,128]{1,0:T(8,128)(2,1)S(1)} %pad_maximum_fusion.3), channel_id=1, source_target_pairs={{0,4},{2,6},{4,0},{6,2},{8,12},{10,14},{12,8},{14,10},{16,20},{18,... | collective-permute-start | bytes 737288 | tf_op jit(solution)/shard_map/ppermute | solution.py:649
  32.9 4.2 %collective-permute-start.7 = (bf16[32,112,128]{2,1,0:T(8,128)(2,1)S(1)}, bf16[32,112,128]{2,1,0:T(8,128)(2,1)S(1)}, u32[]{:S(2)}, u32[]{:S(2)}) collective-permute-start(bf16[32,112,128]{2,1,0:T(8,128)(2,1)S(1)} %gather_fusion), channel_id=1, source_target_pairs={{0,1},{1,0},{2,3},{3,2},{4,5},{5,4},{6,7},{7,6},{8,9},{9,8},{10,11... | collective-permute-start | bytes 2752520 | tf_op jit(solution)/shard_map/ppermute | solution.py:649
  35.8 1.3 collective-permute-start.8
  232.7 2.7 %collective-permute-start.11 = (bf16[3584,128]{1,0:T(8,128)(2,1)S(1)}, bf16[3584,128]{1,0:T(8,128)(2,1)}, u32[]{:S(2)}, u32[]{:S(2)}) collective-permute-start(bf16[3584,128]{1,0:T(8,128)(2,1)S(1)} %bitcast.76), channel_id=1, source_target_pairs={{0,1},{1,0},{2,3},{3,2},{4,5},{5,4},{6,7},{7,6},{8,9},{9,8},{10,11... | collective-permute-start | bytes 2752520 | tf_op jit(solution)/shard_map/ppermute | solution.py:649
  234.3 5.3 %copy-start.4 = (bf16[2,512,256]{2,1,0:T(8,128)(2,1)S(1)}, bf16[2,512,256]{2,1,0:T(8,128)(2,1)}, u32[]{:S(2)}) copy-start(bf16[2,512,256]{2,1,0:T(8,128)(2,1)} %get-tuple-element.18) | copy-start | bytes 1572868
  234.3 20.0 %collective-permute-start.10 = (f32[2,512,256]{2,1,0:T(8,128)}, f32[2,512,256]{2,1,0:T(8,128)S(1)}, u32[]{:S(2)}, u32[]{:S(2)}) collective-permute-start(f32[2,512,256]{2,1,0:T(8,128)} %get-tuple-element.21), channel_id=1, source_target_pairs={{0,1},{1,0},{2,3},{3,2},{4,5},{5,4},{6,7},{7,6},{8,9},{9,8},{10,11... | collective-permute-start | bytes 3145736 | tf_op jit(solution)/shard_map/ppermute | solution.py:649
  234.5 5.1 %collective-permute-start.9 = (bf16[2,512,256]{2,1,0:T(8,128)(2,1)S(1)}, bf16[2,512,256]{2,1,0:T(8,128)(2,1)S(1)}, u32[]{:S(2)}, u32[]{:S(2)}) collective-permute-start(bf16[2,512,256]{2,1,0:T(8,128)(2,1)S(1)} %copy-done.13), channel_id=1, source_target_pairs={{0,1},{1,0},{2,3},{3,2},{4,5},{5,4},{6,7},{7,6},{8,9},{9,8},{10,11... | collective-permute-start | bytes 1572872 | tf_op jit(solution)/shard_map/ppermute | solution.py:649
  236.9 6.9 %collective-permute-start.12 = (bf16[4,224,128]{2,1,0:T(8,128)(2,1)S(1)}, bf16[4,224,128]{2,1,0:T(8,128)(2,1)S(1)}, u32[]{:S(2)}, u32[]{:S(2)}) collective-permute-start(bf16[4,224,128]{2,1,0:T(8,128)(2,1)S(1)} %get-tuple-element.40), channel_id=1, source_target_pairs={{0,2},{2,0},{4,6},{6,4},{8,10},{10,8},{12,14},{14,12},{16,18},{18,... | collective-permute-start | bytes 688136 | tf_op jit(solution)/shard_map/ppermute | solution.py:649
  238.2 6.5 %collective-permute-start.13 = (bf16[4,224,128]{2,1,0:T(8,128)(2,1)S(1)}, bf16[4,224,128]{2,1,0:T(8,128)(2,1)S(1)}, u32[]{:S(2)}, u32[]{:S(2)}) collective-permute-start(bf16[4,224,128]{2,1,0:T(8,128)(2,1)S(1)} %get-tuple-element.42), channel_id=1, source_target_pairs={{0,4},{2,6},{4,0},{6,2},{8,12},{10,14},{12,8},{14,10},{16,20},{18,... | collective-permute-start | bytes 688136 | tf_op jit(solution)/shard_map/ppermute | solution.py:649
  239.4 10.3 %collective-permute-start.14 = (bf16[4,224,128]{2,1,0:T(8,128)(2,1)S(1)}, bf16[4,224,128]{2,1,0:T(8,128)(2,1)S(1)}, u32[]{:S(2)}, u32[]{:S(2)}) collective-permute-start(bf16[4,224,128]{2,1,0:T(8,128)(2,1)S(1)} %get-tuple-element.41), channel_id=1, source_target_pairs={{0,6},{2,4},{4,2},{6,0},{8,14},{10,12},{12,10},{14,8},{16,22},{18,... | collective-permute-start | bytes 688136 | tf_op jit(solution)/shard_map/ppermute | solution.py:649
  239.7 14.6 %copy-start.3 = (f32[2,512,256]{2,1,0:T(8,128)S(1)}, f32[2,512,256]{2,1,0:T(8,128)}, u32[]{:S(2)}) copy-start(f32[2,512,256]{2,1,0:T(8,128)} %get-tuple-element.20) | copy-start | bytes 3145732
  249.8 4.6 %collective-permute-start.15 = (bf16[1,224,128]{2,1,0:T(8,128)(2,1)S(1)}, bf16[1,224,128]{2,1,0:T(8,128)(2,1)S(1)}, u32[]{:S(2)}, u32[]{:S(2)}) collective-permute-start(bf16[1,224,128]{2,1,0:T(8,128)(2,1)S(1)} %get-tuple-element.51), channel_id=1, source_target_pairs={{0,8},{2,10},{4,12},{6,14},{8,0},{10,2},{12,4},{14,6},{16,24},{18,... | collective-permute-start | bytes 172040 | tf_op jit(solution)/shard_map/ppermute | solution.py:649
  251.2 4.6 %collective-permute-start.16 = (bf16[1,224,128]{2,1,0:T(8,128)(2,1)S(1)}, bf16[1,224,128]{2,1,0:T(8,128)(2,1)S(1)}, u32[]{:S(2)}, u32[]{:S(2)}) collective-permute-start(bf16[1,224,128]{2,1,0:T(8,128)(2,1)S(1)} %get-tuple-element.53), channel_id=1, source_target_pairs={{0,16},{2,18},{4,20},{6,22},{8,24},{10,26},{12,28},{14,30},{16,0},... | collective-permute-start | bytes 172040 | tf_op jit(solution)/shard_map/ppermute | solution.py:649
  254.2 4.9 %collective-permute-start.17 = (bf16[1,224,128]{2,1,0:T(8,128)(2,1)S(1)}, bf16[1,224,128]{2,1,0:T(8,128)(2,1)S(1)}, u32[]{:S(2)}, u32[]{:S(2)}) collective-permute-start(bf16[1,224,128]{2,1,0:T(8,128)(2,1)S(1)} %get-tuple-element.52), channel_id=1, source_target_pairs={{0,24},{2,26},{4,28},{6,30},{8,16},{10,18},{12,20},{14,22},{16,8},... | collective-permute-start | bytes 172040 | tf_op jit(solution)/shard_map/ppermute | solution.py:649
  259.1 4.7 %collective-permute-start.18 = (f32[2,107,128]{2,1,0:T(8,128)S(1)}, f32[2,107,128]{2,1,0:T(8,128)S(1)}, u32[]{:S(2)}, u32[]{:S(2)}) collective-permute-start(f32[2,107,128]{2,1,0:T(8,128)S(1)} %bitcast.77), channel_id=1, source_target_pairs={{0,1},{1,0},{2,3},{3,2},{4,5},{5,4},{6,7},{7,6},{8,9},{9,8},{10,11... | collective-permute-start | bytes 328712 | tf_op jit(solution)/shard_map/ppermute | solution.py:649
  (9 other events, 15.6 us)

commit v6 on v5

--- a/solution.py
+++ b/solution.py
@@ -104,7 +104,6 @@
     gsilu_s,
     gslope_s,
     inner_s,
-    proj_s,
     dread_s,
     projt_s,
     dproj_s,
@@ -132,6 +131,7 @@
     gsmall_ref,
     gvec_ref,
     ggain_ref,
+    flat_s,
 ):
     window = pl.program_id(0)
     natural = pl.program_id(1)
@@ -239,7 +239,6 @@
             slope_s[rows, :] = sig + act * (1.0 - sig)
         act_high, act_low = split_low(act_s[span(row, SLAB), :])
         proj = dot(act_high, wx_s[...]) + dot(act_low, wx_s[...])
-        proj_s[span(row, SLAB), :] = proj.astype(BF)
         for k in range(SLAB // CHUNK):
             turned = jnp.transpose(proj[k * CHUNK : (k + 1) * CHUNK])
             projt_s[slab * (SLAB // CHUNK) + k] = turned[: 3 * STATE]
@@ -448,8 +447,12 @@
             + dread_s[span(row, SLAB), :].astype(F32)
         )
         extra = dot(dproj.astype(BF), wx_s[...], NT)
-        low = proj_s[span(row, SLAB), :]
-        gsmall_ref[STATE : 2 * STATE, :] += dot(low, dpre_all, TN)[:RANK]
+        low_sum = None
+        for k in range(SLAB // CHUNK):
+            low = projt_s[slab * (SLAB // CHUNK) + k][:RANK].astype(BF)
+            part = dot(low, dpre_all[k * CHUNK : (k + 1) * CHUNK])
+            low_sum = part if low_sum is None else low_sum + part
+        gsmall_ref[STATE : 2 * STATE, :] += low_sum
         gsmall_ref[2 * STATE : 5 * STATE, :] += dot(
             dproj.astype(BF), act_s[span(row, SLAB), :].astype(BF), TN
         )[: 3 * STATE]
@@ -512,8 +515,15 @@
 
     @pl.when((window == pl.num_programs(0) - 1) & (natural == 1))
     def _():
-        gwin_out[...] = gwin_ref[...].astype(BF)
-        gwout_out[...] = gwout_ref[...].astype(BF)
+        for source, target in ((gwin_ref, gwin_out), (gwout_ref, gwout_out)):
+            parts = source.shape[1] // LANES
+            count = flat_s.shape[0] // parts
+            for p in range(source.shape[0] // count):
+                for k in range(parts):
+                    flat_s[pl.ds(k, count, stride=parts), :] = source[
+                        p * count : (p + 1) * count, k * LANES : (k + 1) * LANES
+                    ]
+                target[p * flat_s.shape[0] : (p + 1) * flat_s.shape[0], :] = flat_s[...].astype(BF)
         gsmall_out[...] = gsmall_ref[...].astype(BF)
         vectors = [jnp.sum(gvec_ref[j], axis=0, keepdims=True) for j in range(7)]
         vectors.append(jnp.zeros((9, INNER), F32))
@@ -539,8 +549,8 @@
     got = pl.BlockSpec((1, half, D), lambda w, q, core: (w, 0, 0))
     fixed = (perm, w_in, w_out, w_x, w_dt, vec, rate, gain[None])
     grads = [
-        jax.ShapeDtypeStruct((D, 2 * INNER), BF),
-        jax.ShapeDtypeStruct((INNER, D), BF),
+        jax.ShapeDtypeStruct((D * 2 * INNER // LANES, LANES), BF),
+        jax.ShapeDtypeStruct((INNER * D // LANES, LANES), BF),
         jax.ShapeDtypeStruct((5 * STATE, INNER), BF),
         jax.ShapeDtypeStruct((16, INNER), BF),
         jax.ShapeDtypeStruct((16, D), BF),
@@ -555,7 +565,7 @@
         + halo_f32
         + inner_f32
         + [pltpu.VMEM((length + 16, INNER), BF)]
-        + [pltpu.VMEM((length, LANES), BF)] * 2
+        + [pltpu.VMEM((length, LANES), BF)]
         + [
             pltpu.VMEM((length // CHUNK, 3 * STATE, CHUNK), F32),
             pltpu.VMEM((length, 2 * INNER), BF),
@@ -580,6 +590,7 @@
             pltpu.VMEM((5 * STATE, INNER), F32),
             pltpu.VMEM((7, 8, INNER), F32),
             pltpu.VMEM((8, D), F32),
+            pltpu.VMEM((SLAB, LANES), F32),
         ]
     )
     return pl.pallas_call(
@@ -659,7 +670,7 @@
     return jnp.pad(value, widths)
 
 
-def gather_params(weights, owners, rank):
+def gather_params(weights, owners, rank, matches):
     size = lax.axis_size("dp")
     me = lax.axis_index("dp")
     core = lax.axis_index("seq")
@@ -674,12 +685,7 @@
     many = pad_rows(mine, padded, 1).reshape(pair * padded, LANES)
     first = MATRIX_END // block_len
     last = (PARAMS - 1) // block_len + 1
-    own = owners == me
-    order = jnp.arange(blocks, dtype=jnp.int32)
-    before = order[None, :] < order[first:last, None]
-    earlier = jnp.sum((before & own[None, :]).astype(jnp.int32), axis=1)
-    slot = jnp.where(own[first:last], earlier, SLOTS)
-    here = (slot[:, None] == jnp.arange(SLOTS, dtype=jnp.int32)[None, :])[:, :, None, None]
+    here = matches[:, first:last].T[:, :, None, None]
     fine = jnp.sum(jnp.where(here, (tiles - rounded)[None], 0.0), axis=1).astype(BF)
     fine_rows = (last - first) * rows
     fine_half = up_to(fine_rows, 32) // 2
@@ -689,10 +695,14 @@
     spot = jnp.zeros_like(owners)
     bit, step = size // 2, 0
     while bit >= near:
-        got = swap(jnp.concatenate([many, fine], axis=0), "dp", bit)
         count = many.shape[0]
-        many = jnp.concatenate([many, got[:count]], axis=0)
-        fine = fine + got[count:]
+        if step == 0:
+            got_many, got_fine = swap(many, "dp", bit), swap(fine, "dp", bit)
+        else:
+            got = swap(jnp.concatenate([many, fine], axis=0), "dp", bit)
+            got_many, got_fine = got[:count], got[count:]
+        many = jnp.concatenate([many, got_many], axis=0)
+        fine = fine + got_fine
         spot = spot + jnp.where((away & bit) != 0, 1 << step, 0)
         bit, step = bit // 2, step + 1
     count = many.shape[0]
@@ -761,7 +771,7 @@
     )
     occupied = jnp.any(matches, axis=1)
     block_of = jnp.sum(jnp.where(matches, order[None, :], 0), axis=1)
-    theta, fine = gather_params(weights, owners, rank)
+    theta, fine = gather_params(weights, owners, rank, matches)
     upstream = cotangent * loss_mask.astype(BF)[..., None]
     x_got = other_half(inputs, core)
     up_got = other_half(upstream, core)

time: 266 us -> 265 us (level)
    concatenate x1, local copies, waits for them, and re-layouts: 0.64 us -> 3.3 us  [on_device(): jnp.concatenate(tiles, axis=0).reshape(blocks + 1, rows, LANES)]
    ppermute x19 -> x20, waiting for transfers between devices: 24.1 us -> 26.5 us  [swap(): return lax.ppermute(value, axis, [(i, i ^ bit) for i in range(size)])]
    ppermute x19 -> x20, starting transfers between devices: 22.8 us -> 21.4 us  [swap(): return lax.ppermute(value, axis, [(i, i ^ bit) for i in range(size)])]
  transfers between devices with their start and end apart: 19 -> 20, of which waited for: 9 -> 10; matrix products, arithmetic and copies ran while one was open for 7% -> 7% of each run, Pallas kernels for 0% -> 0%
where the time goes in v6:
time: 265 us
  Pallas kernels  181 us (68%)
  waiting for transfers between devices  26.5 us (10%)
  starting transfers between devices  21.4 us (8%)
  local copies, waits for them, and re-layouts  19.4 us (7%)
  other arithmetic  15.6 us (6%)
    pallas_call x1, Pallas kernels, run_layer(): pl.pallas_call(layer_kernel, grid_spec=pltpu.PrefetchScalarGridSpec(num_s...  181 us
    ppermute x20, waiting for transfers between devices, swap(): return lax.ppermute(value, axis, [(i, i ^ bit) for i in range(size)])  26.5 us
    ppermute x20, starting transfers between devices, swap(): return lax.ppermute(value, axis, [(i, i ^ bit) for i in range(size)])  21.4 us
  transfers between devices with their start and end apart: 20, of which 10 were waited for; matrix products, arithmetic and copies ran while one was open for 7% of the time, Pallas kernels for 0%

profile of v6, /device:TPU:1, one launch (start us, length us, event | category | flops | bytes accessed | tf_op | source)
XLA Modules:
  0.0 264.8 jit_solution(16038180795758729709)
XLA Ops:
  2.9 1.3 select_reduce_fusion
  4.3 3.2 %collective-permute-start.3 = (bf16[64,128]{1,0:T(8,128)(2,1)S(1)}, bf16[64,128]{1,0:T(8,128)(2,1)S(1)}, u32[]{:S(2)}, u32[]{:S(2)}) collective-permute-start(bf16[64,128]{1,0:T(8,128)(2,1)S(1)} %pad_dynamic-slice_fusion), channel_id=1, source_target_pairs={{0,16},{2,18},{4,20},{6,22},{8,24},{10,26},{12,28},{14,30},{16,0},... | collective-permute-start | bytes 49160 | tf_op jit(solution)/shard_map/ppermute | solution.py:660
  9.4 1.6 broadcast_multiply_fusion.up_kept_ref
  13.9 1.7 collective-permute-start.4
  16.7 1.6 collective-permute-done.4
  18.4 2.6 collective-permute-start.7
  21.8 3.5 %collective-permute-done.7 = bf16[960,128]{1,0:T(8,128)(2,1)S(1)} collective-permute-done((bf16[960,128]{1,0:T(8,128)(2,1)S(1)}, bf16[960,128]{1,0:T(8,128)(2,1)S(1)}, u32[]{:S(2)}, u32[]{:S(2)}) %collective-permute-start.7) | collective-permute-done | bytes 245792 | tf_op jit(solution)/shard_map/ppermute | solution.py:660
  25.4 6.4 %collective-permute-done.6 = bf16[960,128]{1,0:T(8,128)(2,1)S(1)} collective-permute-done((bf16[960,128]{1,0:T(8,128)(2,1)S(1)}, bf16[960,128]{1,0:T(8,128)(2,1)S(1)}, u32[]{:S(2)}, u32[]{:S(2)}) %collective-permute-start.6) | collective-permute-done | bytes 245792 | tf_op jit(solution)/shard_map/ppermute | solution.py:660
  32.7 1.6 collective-permute-start.8
  42.8 180.6 %shard_map.119 = (bf16[2,512,256]{2,1,0:T(8,128)(2,1)}, bf16[2,512,256]{2,1,0:T(8,128)(2,1)}, f32[2,512,256]{2,1,0:T(8,128)}, f32[2,512,256]{2,1,0:T(8,128)}, bf...) custom-call(s32[1]{0:T(128)} %bitcast.core_ref, ...), custom_call_target="tpu_custom_call" | custom-call | tf_op jit(solution)/shard_map/pallas_call | solution.py:596
  228.2 3.3 %concatenate.38 = bf16[3531,128]{1,0:T(8,128)(2,1)S(1)} concatenate(bf16[2048,128]{1,0:T(8,128)(2,1)} %get-tuple-element.22, bf16[192,128]{1,0:T(8,128)(2,1)S(1)} %reshape.197, bf16[64,128]{1,0:T(8,128)(2,1)S(1)} %reshape.198, bf16[1024,128]{1,0:T(8,128)(2,1)} %get-tuple-element.24, bf16[16,128]{1,0:T(8,128)(2,1)S(1)} %reshape.199, bf16[4,128]{1,0:T(4,128)(2,1)S(1)} %bitcast.87, ...), dimensions={0} | concatenate | bytes 1807872 | tf_op jit(solution)/shard_map/concatenate | solution.py:806
  235.4 1.4 fusion
  236.9 1.3 collective-permute-start.13
  238.2 1.2 collective-permute-start.14
  239.7 1.1 pad_maximum_fusion.1
  240.8 3.0 %collective-permute-done.13 = bf16[4,224,128]{2,1,0:T(8,128)(2,1)S(1)} collective-permute-done((bf16[4,224,128]{2,1,0:T(8,128)(2,1)S(1)}, bf16[4,224,128]{2,1,0:T(8,128)(2,1)S(1)}, u32[]{:S(2)}, u32[]{:S(2)}) %collective-permute-start.13) | collective-permute-done | bytes 229408 | tf_op jit(solution)/shard_map/ppermute | solution.py:660
  244.7 5.0 %collective-permute-done.15 = bf16[4,224,128]{2,1,0:T(8,128)(2,1)S(1)} collective-permute-done((bf16[4,224,128]{2,1,0:T(8,128)(2,1)S(1)}, bf16[4,224,128]{2,1,0:T(8,128)(2,1)S(1)}, u32[]{:S(2)}, u32[]{:S(2)}) %collective-permute-start.15) | collective-permute-done | bytes 229408 | tf_op jit(solution)/shard_map/ppermute | solution.py:660
  249.8 1.6 collective-permute-start.16
  251.4 2.3 collective-permute-start.17
  253.9 2.0 collective-permute-done.17
  256.0 2.6 collective-permute-done.18
  258.6 3.2 %collective-permute-start.19 = (f32[2,107,128]{2,1,0:T(8,128)S(1)}, f32[2,107,128]{2,1,0:T(8,128)S(1)}, u32[]{:S(2)}, u32[]{:S(2)}) collective-permute-start(f32[2,107,128]{2,1,0:T(8,128)S(1)} %bitcast.76), channel_id=1, source_target_pairs={{0,1},{1,0},{2,3},{3,2},{4,5},{5,4},{6,7},{7,6},{8,9},{9,8},{10,11... | collective-permute-start | bytes 328712 | tf_op jit(solution)/shard_map/ppermute | solution.py:660
  261.8 1.5 pad_maximum_fusion
  263.4 1.4 broadcast_select_fusion.5
  (143 shorter events, 28.5 us)
Async XLA Ops:
  1.5 32.8 %copy-start.9 = (s32[32]{0:T(128)}, s32[32]{0:T(128)S(1)}, u32[]{:S(2)}) copy-start(s32[32]{0:T(128)S(1)} %convert_reduce_fusion) | copy-start | bytes 388
  2.9 10.1 %copy-start.1 = (bf16[4,512,256]{2,1,0:T(8,128)(2,1)S(1)}, bf16[4,512,256]{2,1,0:T(8,128)(2,1)}, u32[]{:S(2)}) copy-start(bf16[4,512,256]{2,1,0:T(8,128)(2,1)} %x_kept_ref.1) | copy-start | bytes 3145732
  4.3 9.6 %collective-permute-start.3 = (bf16[64,128]{1,0:T(8,128)(2,1)S(1)}, bf16[64,128]{1,0:T(8,128)(2,1)S(1)}, u32[]{:S(2)}, u32[]{:S(2)}) collective-permute-start(bf16[64,128]{1,0:T(8,128)(2,1)S(1)} %pad_dynamic-slice_fusion), channel_id=1, source_target_pairs={{0,16},{2,18},{4,20},{6,22},{8,24},{10,26},{12,28},{14,30},{16,0},... | collective-permute-start | bytes 49160 | tf_op jit(solution)/shard_map/ppermute | solution.py:660
  8.6 5.3 %collective-permute-start.2 = (bf16[224,128]{1,0:T(8,128)(2,1)S(1)}, bf16[224,128]{1,0:T(8,128)(2,1)S(1)}, u32[]{:S(2)}, u32[]{:S(2)}) collective-permute-start(bf16[224,128]{1,0:T(8,128)(2,1)S(1)} %bitcast.72), channel_id=1, source_target_pairs={{0,16},{2,18},{4,20},{6,22},{8,24},{10,26},{12,28},{14,30},{16,0},... | collective-permute-start | bytes 172040 | tf_op jit(solution)/shard_map/ppermute | solution.py:660
  9.4 6.2 %copy-start.12 = (s32[32]{0:T(128)S(1)}, s32[32]{0:T(128)}, u32[]{:S(2)}) copy-start(s32[32]{0:T(128)} %param.12) | copy-start | bytes 388
  12.0 30.8 %collective-permute-start.1 = (bf16[2,512,256]{2,1,0:T(8,128)(2,1)S(1)}, bf16[2,512,256]{2,1,0:T(8,128)(2,1)}, u32[]{:S(2)}, u32[]{:S(2)}) collective-permute-start(bf16[2,512,256]{2,1,0:T(8,128)(2,1)S(1)} %constant_dynamic-slice_fusion.3), channel_id=1, source_target_pairs={{0,1},{1,0},{2,3},{3,2},{4,5},{5,4},{6,7},{7,6},{8,9},{9,8},{10,11... | collective-permute-start | bytes 1572872 | tf_op jit(solution)/shard_map/ppermute | solution.py:660
  13.8 28.9 %collective-permute-start = (bf16[2,512,256]{2,1,0:T(8,128)(2,1)}, bf16[2,512,256]{2,1,0:T(8,128)(2,1)}, u32[]{:S(2)}, u32[]{:S(2)}) collective-permute-start(bf16[2,512,256]{2,1,0:T(8,128)(2,1)} %constant_dynamic-slice_fusion.4), channel_id=1, source_target_pairs={{0,1},{1,0},{2,3},{3,2},{4,5},{5,4},{6,7},{7,6},{8,9},{9,8},{10,11... | collective-permute-start | bytes 1572872 | tf_op jit(solution)/shard_map/ppermute | solution.py:660
  13.9 4.4 %collective-permute-start.4 = (bf16[512,128]{1,0:T(8,128)(2,1)S(1)}, bf16[512,128]{1,0:T(8,128)(2,1)S(1)}, u32[]{:S(2)}, u32[]{:S(2)}) collective-permute-start(bf16[512,128]{1,0:T(8,128)(2,1)S(1)} %pad_maximum_fusion.4), channel_id=1, source_target_pairs={{0,8},{2,10},{4,12},{6,14},{8,0},{10,2},{12,4},{14,6},{16,24},{18,... | collective-permute-start | bytes 393224 | tf_op jit(solution)/shard_map/ppermute | solution.py:660
  18.4 7.0 %collective-permute-start.7 = (bf16[960,128]{1,0:T(8,128)(2,1)S(1)}, bf16[960,128]{1,0:T(8,128)(2,1)S(1)}, u32[]{:S(2)}, u32[]{:S(2)}) collective-permute-start(bf16[960,128]{1,0:T(8,128)(2,1)S(1)} %pad_maximum_fusion.3), channel_id=1, source_target_pairs={{0,6},{2,4},{4,2},{6,0},{8,14},{10,12},{12,10},{14,8},{16,22},{18,... | collective-permute-start | bytes 737288 | tf_op jit(solution)/shard_map/ppermute | solution.py:660
  21.5 10.4 %collective-permute-start.5 = (bf16[960,128]{1,0:T(8,128)(2,1)S(1)}, bf16[960,128]{1,0:T(8,128)(2,1)S(1)}, u32[]{:S(2)}, u32[]{:S(2)}) collective-permute-start(bf16[960,128]{1,0:T(8,128)(2,1)S(1)} %pad_maximum_fusion.3), channel_id=1, source_target_pairs={{0,2},{2,0},{4,6},{6,4},{8,10},{10,8},{12,14},{14,12},{16,18},{18,... | collective-permute-start | bytes 737288 | tf_op jit(solution)/shard_map/ppermute | solution.py:660
  21.7 10.1 %collective-permute-start.6 = (bf16[960,128]{1,0:T(8,128)(2,1)S(1)}, bf16[960,128]{1,0:T(8,128)(2,1)S(1)}, u32[]{:S(2)}, u32[]{:S(2)}) collective-permute-start(bf16[960,128]{1,0:T(8,128)(2,1)S(1)} %pad_maximum_fusion.3), channel_id=1, source_target_pairs={{0,4},{2,6},{4,0},{6,2},{8,12},{10,14},{12,8},{14,10},{16,20},{18,... | collective-permute-start | bytes 737288 | tf_op jit(solution)/shard_map/ppermute | solution.py:660
  32.7 3.8 %collective-permute-start.8 = (bf16[32,112,128]{2,1,0:T(8,128)(2,1)S(1)}, bf16[32,112,128]{2,1,0:T(8,128)(2,1)S(1)}, u32[]{:S(2)}, u32[]{:S(2)}) collective-permute-start(bf16[32,112,128]{2,1,0:T(8,128)(2,1)S(1)} %gather_fusion), channel_id=1, source_target_pairs={{0,1},{1,0},{2,3},{3,2},{4,5},{5,4},{6,7},{7,6},{8,9},{9,8},{10,11... | collective-permute-start | bytes 2752520 | tf_op jit(solution)/shard_map/ppermute | solution.py:660
  35.1 1.3 collective-permute-start.9
  232.7 2.7 %collective-permute-start.12 = (bf16[3584,128]{1,0:T(8,128)(2,1)S(1)}, bf16[3584,128]{1,0:T(8,128)(2,1)}, u32[]{:S(2)}, u32[]{:S(2)}) collective-permute-start(bf16[3584,128]{1,0:T(8,128)(2,1)S(1)} %bitcast.71), channel_id=1, source_target_pairs={{0,1},{1,0},{2,3},{3,2},{4,5},{5,4},{6,7},{7,6},{8,9},{9,8},{10,11... | collective-permute-start | bytes 2752520 | tf_op jit(solution)/shard_map/ppermute | solution.py:660
  234.2 19.6 %collective-permute-start.11 = (f32[2,512,256]{2,1,0:T(8,128)}, f32[2,512,256]{2,1,0:T(8,128)S(1)}, u32[]{:S(2)}, u32[]{:S(2)}) collective-permute-start(f32[2,512,256]{2,1,0:T(8,128)} %get-tuple-element.21), channel_id=1, source_target_pairs={{0,1},{1,0},{2,3},{3,2},{4,5},{5,4},{6,7},{7,6},{8,9},{9,8},{10,11... | collective-permute-start | bytes 3145736 | tf_op jit(solution)/shard_map/ppermute | solution.py:660
  234.3 5.3 %collective-permute-start.10 = (bf16[2,512,256]{2,1,0:T(8,128)(2,1)S(1)}, bf16[2,512,256]{2,1,0:T(8,128)(2,1)S(1)}, u32[]{:S(2)}, u32[]{:S(2)}) collective-permute-start(bf16[2,512,256]{2,1,0:T(8,128)(2,1)S(1)} %copy-done.15), channel_id=1, source_target_pairs={{0,1},{1,0},{2,3},{3,2},{4,5},{5,4},{6,7},{7,6},{8,9},{9,8},{10,11... | collective-permute-start | bytes 1572872 | tf_op jit(solution)/shard_map/ppermute | solution.py:660
  236.9 6.9 %collective-permute-start.13 = (bf16[4,224,128]{2,1,0:T(8,128)(2,1)S(1)}, bf16[4,224,128]{2,1,0:T(8,128)(2,1)S(1)}, u32[]{:S(2)}, u32[]{:S(2)}) collective-permute-start(bf16[4,224,128]{2,1,0:T(8,128)(2,1)S(1)} %get-tuple-element.38), channel_id=1, source_target_pairs={{0,2},{2,0},{4,6},{6,4},{8,10},{10,8},{12,14},{14,12},{16,18},{18,... | collective-permute-start | bytes 688136 | tf_op jit(solution)/shard_map/ppermute | solution.py:660
  238.2 6.5 %collective-permute-start.14 = (bf16[4,224,128]{2,1,0:T(8,128)(2,1)S(1)}, bf16[4,224,128]{2,1,0:T(8,128)(2,1)S(1)}, u32[]{:S(2)}, u32[]{:S(2)}) collective-permute-start(bf16[4,224,128]{2,1,0:T(8,128)(2,1)S(1)} %get-tuple-element.40), channel_id=1, source_target_pairs={{0,4},{2,6},{4,0},{6,2},{8,12},{10,14},{12,8},{14,10},{16,20},{18,... | collective-permute-start | bytes 688136 | tf_op jit(solution)/shard_map/ppermute | solution.py:660
  239.4 10.3 %collective-permute-start.15 = (bf16[4,224,128]{2,1,0:T(8,128)(2,1)S(1)}, bf16[4,224,128]{2,1,0:T(8,128)(2,1)S(1)}, u32[]{:S(2)}, u32[]{:S(2)}) collective-permute-start(bf16[4,224,128]{2,1,0:T(8,128)(2,1)S(1)} %get-tuple-element.39), channel_id=1, source_target_pairs={{0,6},{2,4},{4,2},{6,0},{8,14},{10,12},{12,10},{14,8},{16,22},{18,... | collective-permute-start | bytes 688136 | tf_op jit(solution)/shard_map/ppermute | solution.py:660
  239.7 14.0 %copy-start.3 = (f32[2,512,256]{2,1,0:T(8,128)S(1)}, f32[2,512,256]{2,1,0:T(8,128)}, u32[]{:S(2)}) copy-start(f32[2,512,256]{2,1,0:T(8,128)} %get-tuple-element.20) | copy-start | bytes 3145732
  249.8 4.1 %collective-permute-start.16 = (bf16[1,224,128]{2,1,0:T(8,128)(2,1)S(1)}, bf16[1,224,128]{2,1,0:T(8,128)(2,1)S(1)}, u32[]{:S(2)}, u32[]{:S(2)}) collective-permute-start(bf16[1,224,128]{2,1,0:T(8,128)(2,1)S(1)} %get-tuple-element.49), channel_id=1, source_target_pairs={{0,8},{2,10},{4,12},{6,14},{8,0},{10,2},{12,4},{14,6},{16,24},{18,... | collective-permute-start | bytes 172040 | tf_op jit(solution)/shard_map/ppermute | solution.py:660
  251.4 4.5 %collective-permute-start.17 = (bf16[1,224,128]{2,1,0:T(8,128)(2,1)S(1)}, bf16[1,224,128]{2,1,0:T(8,128)(2,1)S(1)}, u32[]{:S(2)}, u32[]{:S(2)}) collective-permute-start(bf16[1,224,128]{2,1,0:T(8,128)(2,1)S(1)} %get-tuple-element.51), channel_id=1, source_target_pairs={{0,16},{2,18},{4,20},{6,22},{8,24},{10,26},{12,28},{14,30},{16,0},... | collective-permute-start | bytes 172040 | tf_op jit(solution)/shard_map/ppermute | solution.py:660
  253.7 4.8 %collective-permute-start.18 = (bf16[1,224,128]{2,1,0:T(8,128)(2,1)S(1)}, bf16[1,224,128]{2,1,0:T(8,128)(2,1)S(1)}, u32[]{:S(2)}, u32[]{:S(2)}) collective-permute-start(bf16[1,224,128]{2,1,0:T(8,128)(2,1)S(1)} %get-tuple-element.50), channel_id=1, source_target_pairs={{0,24},{2,26},{4,28},{6,30},{8,16},{10,18},{12,20},{14,22},{16,8},... | collective-permute-start | bytes 172040 | tf_op jit(solution)/shard_map/ppermute | solution.py:660
  258.6 4.7 %collective-permute-start.19 = (f32[2,107,128]{2,1,0:T(8,128)S(1)}, f32[2,107,128]{2,1,0:T(8,128)S(1)}, u32[]{:S(2)}, u32[]{:S(2)}) collective-permute-start(f32[2,107,128]{2,1,0:T(8,128)S(1)} %bitcast.76), channel_id=1, source_target_pairs={{0,1},{1,0},{2,3},{3,2},{4,5},{5,4},{6,7},{7,6},{8,9},{9,8},{10,11... | collective-permute-start | bytes 328712 | tf_op jit(solution)/shard_map/ppermute | solution.py:660
  (12 other events, 21.8 us)

commit v7 on v5

--- a/solution.py
+++ b/solution.py
@@ -104,7 +104,6 @@
     gsilu_s,
     gslope_s,
     inner_s,
-    proj_s,
     dread_s,
     projt_s,
     dproj_s,
@@ -217,7 +216,7 @@
             rows = span(row + a, BLOCK)
             gate = gate_all[a : a + BLOCK].astype(F32)
             dgated = dgated_all[a : a + BLOCK].astype(F32)
-            sig = 0.5 + 0.5 * jnp.tanh(0.5 * gate)
+            sig = 1.0 / (1.0 + jnp.exp(-gate))
             silu = gate * sig
             gsilu_s[rows, :] = silu
             dscan_s[rows, :] = dgated * silu
@@ -233,13 +232,12 @@
             conv = vec_ref[4:5, :]
             for j in range(KERNEL):
                 conv = conv + vec_ref[j : j + 1, :] * near_s[a + 13 + j : a + 13 + j + BLOCK, :]
-            sig = 0.5 + 0.5 * jnp.tanh(0.5 * conv)
+            sig = 1.0 / (1.0 + jnp.exp(-conv))
             act = conv * sig
             act_s[rows, :] = act
             slope_s[rows, :] = sig + act * (1.0 - sig)
         act_high, act_low = split_low(act_s[span(row, SLAB), :])
         proj = dot(act_high, wx_s[...]) + dot(act_low, wx_s[...])
-        proj_s[span(row, SLAB), :] = proj.astype(BF)
         for k in range(SLAB // CHUNK):
             turned = jnp.transpose(proj[k * CHUNK : (k + 1) * CHUNK])
             projt_s[slab * (SLAB // CHUNK) + k] = turned[: 3 * STATE]
@@ -448,8 +446,12 @@
             + dread_s[span(row, SLAB), :].astype(F32)
         )
         extra = dot(dproj.astype(BF), wx_s[...], NT)
-        low = proj_s[span(row, SLAB), :]
-        gsmall_ref[STATE : 2 * STATE, :] += dot(low, dpre_all, TN)[:RANK]
+        low_sum = None
+        for k in range(SLAB // CHUNK):
+            low = projt_s[slab * (SLAB // CHUNK) + k][:RANK].astype(BF)
+            part = dot(low, dpre_all[k * CHUNK : (k + 1) * CHUNK])
+            low_sum = part if low_sum is None else low_sum + part
+        gsmall_ref[STATE : 2 * STATE, :] += low_sum
         gsmall_ref[2 * STATE : 5 * STATE, :] += dot(
             dproj.astype(BF), act_s[span(row, SLAB), :].astype(BF), TN
         )[: 3 * STATE]
@@ -555,7 +557,7 @@
         + halo_f32
         + inner_f32
         + [pltpu.VMEM((length + 16, INNER), BF)]
-        + [pltpu.VMEM((length, LANES), BF)] * 2
+        + [pltpu.VMEM((length, LANES), BF)]
         + [
             pltpu.VMEM((length // CHUNK, 3 * STATE, CHUNK), F32),
             pltpu.VMEM((length, 2 * INNER), BF),
@@ -659,7 +661,7 @@
     return jnp.pad(value, widths)
 
 
-def gather_params(weights, owners, rank):
+def gather_params(weights, owners, rank, matches):
     size = lax.axis_size("dp")
     me = lax.axis_index("dp")
     core = lax.axis_index("seq")
@@ -674,12 +676,7 @@
     many = pad_rows(mine, padded, 1).reshape(pair * padded, LANES)
     first = MATRIX_END // block_len
     last = (PARAMS - 1) // block_len + 1
-    own = owners == me
-    order = jnp.arange(blocks, dtype=jnp.int32)
-    before = order[None, :] < order[first:last, None]
-    earlier = jnp.sum((before & own[None, :]).astype(jnp.int32), axis=1)
-    slot = jnp.where(own[first:last], earlier, SLOTS)
-    here = (slot[:, None] == jnp.arange(SLOTS, dtype=jnp.int32)[None, :])[:, :, None, None]
+    here = matches[:, first:last].T[:, :, None, None]
     fine = jnp.sum(jnp.where(here, (tiles - rounded)[None], 0.0), axis=1).astype(BF)
     fine_rows = (last - first) * rows
     fine_half = up_to(fine_rows, 32) // 2
@@ -715,7 +712,7 @@
     return lax.optimization_barrier((theta, fine))
 
 
-def scatter_sum(value, size):
+def scatter_sum(value, size, beside):
     me = lax.axis_index("dp")
     stride = 1
     total = value
@@ -729,8 +726,10 @@
             given = lax.dynamic_index_in_dim(low, digit ^ k, 1, keepdims=False)
             kept = kept + swap(given, "dp", k * stride).astype(F32)
         total = kept
+        if stride == 1:
+            total, beside = lax.optimization_barrier((total, beside))
         stride *= radix
-    return total[0]
+    return total[0], beside
 
 
 def other_half(value, core):
@@ -761,7 +760,7 @@
     )
     occupied = jnp.any(matches, axis=1)
     block_of = jnp.sum(jnp.where(matches, order[None, :], 0), axis=1)
-    theta, fine = gather_params(weights, owners, rank)
+    theta, fine = gather_params(weights, owners, rank, matches)
     upstream = cotangent * loss_mask.astype(BF)[..., None]
     x_got = other_half(inputs, core)
     up_got = other_half(upstream, core)
@@ -805,13 +804,14 @@
     got = swap(for_core(1 - core), "seq", 1)
     chip = (for_core(core).astype(F32) + got.astype(F32)).astype(BF)
     chip = chip.reshape(size, pair * padded, LANES)
-    summed = scatter_sum(chip, size).reshape(pair, -1, LANES)[:, :rows]
+    output = by_position(results[0], results[1], core)
+    grad_input = by_position(results[2], results[3], core)
+    summed, grad_input = scatter_sum(chip, size, grad_input)
+    summed = summed.reshape(pair, -1, LANES)[:, :rows]
     other = swap(summed, "seq", 1)
     owned = jnp.concatenate(
         [jnp.where(core == 0, summed, other), jnp.where(core == 0, other, summed)], axis=0
     ).reshape(SLOTS, block_len)
-    output = by_position(results[0], results[1], core)
-    grad_input = by_position(results[2], results[3], core)
     new_first = BETA_ONE * first_moment + (1.0 - BETA_ONE) * owned
     new_second = BETA_TWO * second_moment + (1.0 - BETA_TWO) * owned * owned
     position = block_of[:, None] * block_len + jnp.arange(block_len, dtype=jnp.int32)[None, :]

time: 266 us -> 265 us (level)
  starting transfers between devices: 22.8 us -> 19.7 us
    ppermute x19, starting transfers between devices: 22.8 us -> 19.7 us  [swap(): return lax.ppermute(value, axis, [(i, i ^ bit) for i in range(size)])]
  transfers between devices with their start and end apart: 19 -> 19, of which waited for: 9 -> 10; matrix products, arithmetic and copies ran while one was open for 7% -> 7% of each run, Pallas kernels for 0% -> 0%
where the time goes in v7:
time: 265 us; the launch traced here: 264 us
  Pallas kernels  181 us (68%)
  waiting for transfers between devices  26.1 us (10%)
  local copies, waits for them, and re-layouts  20 us (8%)
  starting transfers between devices  19.7 us (7%)
  other arithmetic  15.6 us (6%)
    pallas_call x1, Pallas kernels, run_layer(): pl.pallas_call(layer_kernel, grid_spec=pltpu.PrefetchScalarGridSpec(num_s...  181 us
    ppermute x19, waiting for transfers between devices, swap(): return lax.ppermute(value, axis, [(i, i ^ bit) for i in range(size)])  26.1 us
    ppermute x19, starting transfers between devices, swap(): return lax.ppermute(value, axis, [(i, i ^ bit) for i in range(size)])  19.7 us
  transfers between devices with their start and end apart: 19, of which 10 were waited for; matrix products, arithmetic and copies ran while one was open for 7% of the time, Pallas kernels for 0%

profile of v7, /device:TPU:1, one launch (start us, length us, event | category | flops | bytes accessed | tf_op | source)
XLA Modules:
  0.0 264.0 jit_solution(6649613420880647794)
XLA Ops:
  3.9 1.3 select_reduce_fusion
  5.4 3.2 %collective-permute-start.2 = (bf16[288,128]{1,0:T(8,128)(2,1)S(1)}, bf16[288,128]{1,0:T(8,128)(2,1)S(1)}, u32[]{:S(2)}, u32[]{:S(2)}) collective-permute-start(bf16[288,128]{1,0:T(8,128)(2,1)S(1)} %pad_maximum_fusion.5), channel_id=1, source_target_pairs={{0,16},{2,18},{4,20},{6,22},{8,24},{10,26},{12,28},{14,30},{16,0},... | collective-permute-start | bytes 221192 | tf_op jit(solution)/shard_map/ppermute | solution.py:651
  9.3 1.6 broadcast_multiply_fusion.up_kept_ref
  13.8 1.4 collective-permute-start.3
  16.3 2.2 collective-permute-done.3
  18.5 2.2 collective-permute-start.6
  21.8 3.8 %collective-permute-done.6 = bf16[960,128]{1,0:T(8,128)(2,1)S(1)} collective-permute-done((bf16[960,128]{1,0:T(8,128)(2,1)S(1)}, bf16[960,128]{1,0:T(8,128)(2,1)S(1)}, u32[]{:S(2)}, u32[]{:S(2)}) %collective-permute-start.6) | collective-permute-done | bytes 245792 | tf_op jit(solution)/shard_map/ppermute | solution.py:651
  25.6 6.5 %collective-permute-done.5 = bf16[960,128]{1,0:T(8,128)(2,1)S(1)} collective-permute-done((bf16[960,128]{1,0:T(8,128)(2,1)S(1)}, bf16[960,128]{1,0:T(8,128)(2,1)S(1)}, u32[]{:S(2)}, u32[]{:S(2)}) %collective-permute-start.5) | collective-permute-done | bytes 245792 | tf_op jit(solution)/shard_map/ppermute | solution.py:651
  33.1 1.1 collective-permute-start.7
  42.6 181.5 %shard_map.119 = (bf16[2,512,256]{2,1,0:T(8,128)(2,1)}, bf16[2,512,256]{2,1,0:T(8,128)(2,1)}, f32[2,512,256]{2,1,0:T(8,128)}, f32[2,512,256]{2,1,0:T(8,128)}, bf...) custom-call(s32[1]{0:T(128)} %bitcast.core_ref, ...), custom_call_target="tpu_custom_call" | custom-call | tf_op jit(solution)/shard_map/pallas_call | solution.py:587
  227.1 1.3 reshape.203
  236.8 1.4 fusion
  238.2 1.3 collective-permute-start.11
  239.5 1.2 collective-permute-start.12
  241.1 1.5 pad_maximum_fusion
  242.6 2.5 collective-permute-done.11
  246.0 5.0 %collective-permute-done.13 = bf16[4,224,128]{2,1,0:T(8,128)(2,1)S(1)} collective-permute-done((bf16[4,224,128]{2,1,0:T(8,128)(2,1)S(1)}, bf16[4,224,128]{2,1,0:T(8,128)(2,1)S(1)}, u32[]{:S(2)}, u32[]{:S(2)}) %collective-permute-start.13) | collective-permute-done | bytes 229408 | tf_op jit(solution)/shard_map/ppermute | solution.py:651
  251.2 1.4 collective-permute-start.15
  253.4 1.4 collective-permute-start.17
  254.9 2.0 collective-permute-done.16
  257.0 1.6 collective-permute-done.17
  258.6 2.9 %collective-permute-start.18 = (f32[2,107,128]{2,1,0:T(8,128)S(1)}, f32[2,107,128]{2,1,0:T(8,128)S(1)}, u32[]{:S(2)}, u32[]{:S(2)}) collective-permute-start(f32[2,107,128]{2,1,0:T(8,128)S(1)} %bitcast.74), channel_id=1, source_target_pairs={{0,1},{1,0},{2,3},{3,2},{4,5},{5,4},{6,7},{7,6},{8,9},{9,8},{10,11... | collective-permute-start | bytes 328712 | tf_op jit(solution)/shard_map/ppermute | solution.py:651
  261.5 1.1 pad_maximum_fusion.1
  262.6 1.4 broadcast_select_fusion.5
  (146 shorter events, 32.2 us)
Async XLA Ops:
  1.5 32.6 %copy-start.9 = (s32[32]{0:T(128)}, s32[32]{0:T(128)S(1)}, u32[]{:S(2)}) copy-start(s32[32]{0:T(128)S(1)} %convert_reduce_fusion) | copy-start | bytes 388
  3.8 9.1 %copy-start.1 = (bf16[4,512,256]{2,1,0:T(8,128)(2,1)S(1)}, bf16[4,512,256]{2,1,0:T(8,128)(2,1)}, u32[]{:S(2)}) copy-start(bf16[4,512,256]{2,1,0:T(8,128)(2,1)} %x_kept_ref.1) | copy-start | bytes 3145732
  5.4 8.4 %collective-permute-start.2 = (bf16[288,128]{1,0:T(8,128)(2,1)S(1)}, bf16[288,128]{1,0:T(8,128)(2,1)S(1)}, u32[]{:S(2)}, u32[]{:S(2)}) collective-permute-start(bf16[288,128]{1,0:T(8,128)(2,1)S(1)} %pad_maximum_fusion.5), channel_id=1, source_target_pairs={{0,16},{2,18},{4,20},{6,22},{8,24},{10,26},{12,28},{14,30},{16,0},... | collective-permute-start | bytes 221192 | tf_op jit(solution)/shard_map/ppermute | solution.py:651
  11.9 30.7 %collective-permute-start.1 = (bf16[2,512,256]{2,1,0:T(8,128)(2,1)S(1)}, bf16[2,512,256]{2,1,0:T(8,128)(2,1)}, u32[]{:S(2)}, u32[]{:S(2)}) collective-permute-start(bf16[2,512,256]{2,1,0:T(8,128)(2,1)S(1)} %constant_dynamic-slice_fusion.3), channel_id=1, source_target_pairs={{0,1},{1,0},{2,3},{3,2},{4,5},{5,4},{6,7},{7,6},{8,9},{9,8},{10,11... | collective-permute-start | bytes 1572872 | tf_op jit(solution)/shard_map/ppermute | solution.py:651
  13.7 28.8 %collective-permute-start = (bf16[2,512,256]{2,1,0:T(8,128)(2,1)}, bf16[2,512,256]{2,1,0:T(8,128)(2,1)}, u32[]{:S(2)}, u32[]{:S(2)}) collective-permute-start(bf16[2,512,256]{2,1,0:T(8,128)(2,1)} %constant_dynamic-slice_fusion.4), channel_id=1, source_target_pairs={{0,1},{1,0},{2,3},{3,2},{4,5},{5,4},{6,7},{7,6},{8,9},{9,8},{10,11... | collective-permute-start | bytes 1572872 | tf_op jit(solution)/shard_map/ppermute | solution.py:651
  13.8 4.7 %collective-permute-start.3 = (bf16[512,128]{1,0:T(8,128)(2,1)S(1)}, bf16[512,128]{1,0:T(8,128)(2,1)S(1)}, u32[]{:S(2)}, u32[]{:S(2)}) collective-permute-start(bf16[512,128]{1,0:T(8,128)(2,1)S(1)} %pad_maximum_fusion.4), channel_id=1, source_target_pairs={{0,8},{2,10},{4,12},{6,14},{8,0},{10,2},{12,4},{14,6},{16,24},{18,... | collective-permute-start | bytes 393224 | tf_op jit(solution)/shard_map/ppermute | solution.py:651
  18.5 7.1 %collective-permute-start.6 = (bf16[960,128]{1,0:T(8,128)(2,1)S(1)}, bf16[960,128]{1,0:T(8,128)(2,1)S(1)}, u32[]{:S(2)}, u32[]{:S(2)}) collective-permute-start(bf16[960,128]{1,0:T(8,128)(2,1)S(1)} %pad_maximum_fusion.3), channel_id=1, source_target_pairs={{0,6},{2,4},{4,2},{6,0},{8,14},{10,12},{12,10},{14,8},{16,22},{18,... | collective-permute-start | bytes 737288 | tf_op jit(solution)/shard_map/ppermute | solution.py:651
  21.3 10.9 %collective-permute-start.4 = (bf16[960,128]{1,0:T(8,128)(2,1)S(1)}, bf16[960,128]{1,0:T(8,128)(2,1)S(1)}, u32[]{:S(2)}, u32[]{:S(2)}) collective-permute-start(bf16[960,128]{1,0:T(8,128)(2,1)S(1)} %pad_maximum_fusion.3), channel_id=1, source_target_pairs={{0,2},{2,0},{4,6},{6,4},{8,10},{10,8},{12,14},{14,12},{16,18},{18,... | collective-permute-start | bytes 737288 | tf_op jit(solution)/shard_map/ppermute | solution.py:651
  21.6 10.6 %collective-permute-start.5 = (bf16[960,128]{1,0:T(8,128)(2,1)S(1)}, bf16[960,128]{1,0:T(8,128)(2,1)S(1)}, u32[]{:S(2)}, u32[]{:S(2)}) collective-permute-start(bf16[960,128]{1,0:T(8,128)(2,1)S(1)} %pad_maximum_fusion.3), channel_id=1, source_target_pairs={{0,4},{2,6},{4,0},{6,2},{8,12},{10,14},{12,8},{14,10},{16,20},{18,... | collective-permute-start | bytes 737288 | tf_op jit(solution)/shard_map/ppermute | solution.py:651
  33.1 3.2 %collective-permute-start.7 = (bf16[32,112,128]{2,1,0:T(8,128)(2,1)S(1)}, bf16[32,112,128]{2,1,0:T(8,128)(2,1)S(1)}, u32[]{:S(2)}, u32[]{:S(2)}) collective-permute-start(bf16[32,112,128]{2,1,0:T(8,128)(2,1)S(1)} %gather_fusion), channel_id=1, source_target_pairs={{0,1},{1,0},{2,3},{3,2},{4,5},{5,4},{6,7},{7,6},{8,9},{9,8},{10,11... | collective-permute-start | bytes 2752520 | tf_op jit(solution)/shard_map/ppermute | solution.py:651
  35.0 1.3 collective-permute-start.8
  233.9 2.8 %collective-permute-start.10 = (bf16[3584,128]{1,0:T(8,128)(2,1)}, bf16[3584,128]{1,0:T(8,128)(2,1)}, u32[]{:S(2)}, u32[]{:S(2)}) collective-permute-start(bf16[3584,128]{1,0:T(8,128)(2,1)} %bitcast.21), channel_id=1, source_target_pairs={{0,1},{1,0},{2,3},{3,2},{4,5},{5,4},{6,7},{7,6},{8,9},{9,8},{10,11... | collective-permute-start | bytes 2752520 | tf_op jit(solution)/shard_map/ppermute | solution.py:651
  234.5 6.5 %collective-permute-start.14 = (f32[2,512,256]{2,1,0:T(8,128)}, f32[2,512,256]{2,1,0:T(8,128)S(1)}, u32[]{:S(2)}, u32[]{:S(2)}) collective-permute-start(f32[2,512,256]{2,1,0:T(8,128)} %get-tuple-element.28), channel_id=1, source_target_pairs={{0,1},{1,0},{2,3},{3,2},{4,5},{5,4},{6,7},{7,6},{8,9},{9,8},{10,11... | collective-permute-start | bytes 3145736 | tf_op jit(solution)/shard_map/ppermute | solution.py:651
  235.5 19.3 %collective-permute-start.9 = (bf16[2,512,256]{2,1,0:T(8,128)(2,1)S(1)}, bf16[2,512,256]{2,1,0:T(8,128)(2,1)S(1)}, u32[]{:S(2)}, u32[]{:S(2)}) collective-permute-start(bf16[2,512,256]{2,1,0:T(8,128)(2,1)S(1)} %copy-done.15), channel_id=1, source_target_pairs={{0,1},{1,0},{2,3},{3,2},{4,5},{5,4},{6,7},{7,6},{8,9},{9,8},{10,11... | collective-permute-start | bytes 1572872 | tf_op jit(solution)/shard_map/ppermute | solution.py:651
  238.2 6.9 %collective-permute-start.11 = (bf16[4,224,128]{2,1,0:T(8,128)(2,1)S(1)}, bf16[4,224,128]{2,1,0:T(8,128)(2,1)S(1)}, u32[]{:S(2)}, u32[]{:S(2)}) collective-permute-start(bf16[4,224,128]{2,1,0:T(8,128)(2,1)S(1)} %get-tuple-element.40), channel_id=1, source_target_pairs={{0,2},{2,0},{4,6},{6,4},{8,10},{10,8},{12,14},{14,12},{16,18},{18,... | collective-permute-start | bytes 688136 | tf_op jit(solution)/shard_map/ppermute | solution.py:651
  239.5 6.5 %collective-permute-start.12 = (bf16[4,224,128]{2,1,0:T(8,128)(2,1)S(1)}, bf16[4,224,128]{2,1,0:T(8,128)(2,1)S(1)}, u32[]{:S(2)}, u32[]{:S(2)}) collective-permute-start(bf16[4,224,128]{2,1,0:T(8,128)(2,1)S(1)} %get-tuple-element.42), channel_id=1, source_target_pairs={{0,4},{2,6},{4,0},{6,2},{8,12},{10,14},{12,8},{14,10},{16,20},{18,... | collective-permute-start | bytes 688136 | tf_op jit(solution)/shard_map/ppermute | solution.py:651
  240.7 10.3 %collective-permute-start.13 = (bf16[4,224,128]{2,1,0:T(8,128)(2,1)S(1)}, bf16[4,224,128]{2,1,0:T(8,128)(2,1)S(1)}, u32[]{:S(2)}, u32[]{:S(2)}) collective-permute-start(bf16[4,224,128]{2,1,0:T(8,128)(2,1)S(1)} %get-tuple-element.41), channel_id=1, source_target_pairs={{0,6},{2,4},{4,2},{6,0},{8,14},{10,12},{12,10},{14,8},{16,22},{18,... | collective-permute-start | bytes 688136 | tf_op jit(solution)/shard_map/ppermute | solution.py:651
  242.6 12.2 %copy-start.4 = (bf16[2,512,256]{2,1,0:T(8,128)(2,1)S(1)}, bf16[2,512,256]{2,1,0:T(8,128)(2,1)}, u32[]{:S(2)}) copy-start(bf16[2,512,256]{2,1,0:T(8,128)(2,1)} %get-tuple-element.20) | copy-start | bytes 1572868
  251.2 3.7 %collective-permute-start.15 = (bf16[1,224,128]{2,1,0:T(8,128)(2,1)S(1)}, bf16[1,224,128]{2,1,0:T(8,128)(2,1)S(1)}, u32[]{:S(2)}, u32[]{:S(2)}) collective-permute-start(bf16[1,224,128]{2,1,0:T(8,128)(2,1)S(1)} %get-tuple-element.51), channel_id=1, source_target_pairs={{0,8},{2,10},{4,12},{6,14},{8,0},{10,2},{12,4},{14,6},{16,24},{18,... | collective-permute-start | bytes 172040 | tf_op jit(solution)/shard_map/ppermute | solution.py:651
  252.5 4.4 %collective-permute-start.16 = (bf16[1,224,128]{2,1,0:T(8,128)(2,1)S(1)}, bf16[1,224,128]{2,1,0:T(8,128)(2,1)S(1)}, u32[]{:S(2)}, u32[]{:S(2)}) collective-permute-start(bf16[1,224,128]{2,1,0:T(8,128)(2,1)S(1)} %get-tuple-element.53), channel_id=1, source_target_pairs={{0,16},{2,18},{4,20},{6,22},{8,24},{10,26},{12,28},{14,30},{16,0},... | collective-permute-start | bytes 172040 | tf_op jit(solution)/shard_map/ppermute | solution.py:651
  253.4 5.2 %collective-permute-start.17 = (bf16[1,224,128]{2,1,0:T(8,128)(2,1)S(1)}, bf16[1,224,128]{2,1,0:T(8,128)(2,1)S(1)}, u32[]{:S(2)}, u32[]{:S(2)}) collective-permute-start(bf16[1,224,128]{2,1,0:T(8,128)(2,1)S(1)} %get-tuple-element.52), channel_id=1, source_target_pairs={{0,24},{2,26},{4,28},{6,30},{8,16},{10,18},{12,20},{14,22},{16,8},... | collective-permute-start | bytes 172040 | tf_op jit(solution)/shard_map/ppermute | solution.py:651
  254.9 7.7 %copy-start.2 = (f32[4,13696]{1,0:T(4,128)S(1)}, f32[4,13696]{1,0:T(4,128)}, u32[]{:S(2)}) copy-start(f32[4,13696]{1,0:T(4,128)} %param.13) | copy-start | bytes 657412
  254.9 7.7 %copy-start.5 = (f32[4,13696]{1,0:T(4,128)S(1)}, f32[4,13696]{1,0:T(4,128)}, u32[]{:S(2)}) copy-start(f32[4,13696]{1,0:T(4,128)} %param.15) | copy-start | bytes 657412
  258.6 3.9 %collective-permute-start.18 = (f32[2,107,128]{2,1,0:T(8,128)S(1)}, f32[2,107,128]{2,1,0:T(8,128)S(1)}, u32[]{:S(2)}, u32[]{:S(2)}) collective-permute-start(f32[2,107,128]{2,1,0:T(8,128)S(1)} %bitcast.74), channel_id=1, source_target_pairs={{0,1},{1,0},{2,3},{3,2},{4,5},{5,4},{6,7},{7,6},{8,9},{9,8},{10,11... | collective-permute-start | bytes 328712 | tf_op jit(solution)/shard_map/ppermute | solution.py:651
  (11 other events, 38.9 us)

commit v8 on v7

--- a/solution.py
+++ b/solution.py
@@ -92,7 +92,6 @@
     gwout_out,
     gsmall_out,
     gvec_out,
-    ggain_out,
     states,
     act_s,
     slope_s,
@@ -518,10 +517,10 @@
         gwout_out[...] = gwout_ref[...].astype(BF)
         gsmall_out[...] = gsmall_ref[...].astype(BF)
         vectors = [jnp.sum(gvec_ref[j], axis=0, keepdims=True) for j in range(7)]
-        vectors.append(jnp.zeros((9, INNER), F32))
+        gain = jnp.sum(ggain_ref[...], axis=0, keepdims=True)
+        vectors.append(jnp.concatenate([gain, jnp.zeros((1, INNER - D), F32)], axis=1))
+        vectors.append(jnp.zeros((8, INNER), F32))
         gvec_out[...] = jnp.concatenate(vectors, axis=0).astype(BF)
-        gain = jnp.sum(ggain_ref[...], axis=0, keepdims=True)
-        ggain_out[...] = jnp.broadcast_to(gain, (16, D)).astype(BF)
 
 
 def run_layer(
@@ -545,7 +544,6 @@
         jax.ShapeDtypeStruct((INNER, D), BF),
         jax.ShapeDtypeStruct((5 * STATE, INNER), BF),
         jax.ShapeDtypeStruct((16, INNER), BF),
-        jax.ShapeDtypeStruct((16, D), BF),
     ]
     inner_f32 = [pltpu.VMEM((length, INNER), F32)]
     outer_bf = [pltpu.VMEM((length, D), BF)]
@@ -602,18 +600,16 @@
 
 
 def layer_grads(results):
-    gwin, gwout, gsmall, gvec, ggain = results
+    gwin, gwout, gsmall, gvec = results
     return [
         gwin,
         gsmall[2 * STATE :].T,
         gsmall[STATE : 2 * STATE],
         gwout,
         gvec[:KERNEL].T,
-        gvec[4],
-        gvec[5],
+        gvec[4:6],
         gsmall[:STATE].T,
-        gvec[6],
-        ggain[0],
+        gvec[6:8],
     ]
 
 
@@ -790,7 +786,7 @@
     )
     pieces = layer_grads(results[4:])
     padded = up_to(rows, 16)
-    spare = jnp.zeros(((blocks + 1) * rows - PARAMS // LANES, LANES), BF)
+    spare = jnp.zeros(((blocks + 1) * rows - (PARAMS + INNER - D) // LANES, LANES), BF)
     tiles = [item.astype(BF).reshape(-1, LANES) for item in pieces] + [spare]
     grad_blocks = jnp.concatenate(tiles, axis=0).reshape(blocks + 1, rows, LANES)
     grad_blocks = pad_rows(grad_blocks, padded, 1)
@@ -806,7 +802,7 @@
     chip = chip.reshape(size, pair * padded, LANES)
     output = by_position(results[0], results[1], core)
     grad_input = by_position(results[2], results[3], core)
-    summed, grad_input = scatter_sum(chip, size, grad_input)
+    summed, (output, grad_input) = scatter_sum(chip, size, (output, grad_input))
     summed = summed.reshape(pair, -1, LANES)[:, :rows]
     other = swap(summed, "seq", 1)
     owned = jnp.concatenate(

time: 265 us -> 264 us (level)
  transfers between devices with their start and end apart: 19 -> 19, of which waited for: 10 -> 10; matrix products, arithmetic and copies ran while one was open for 7% -> 9% of each run, Pallas kernels for 0% -> 0%
where the time goes in v8:
time: 264 us; the launch traced here: 263 us
  Pallas kernels  182 us (69%)
  waiting for transfers between devices  26.6 us (10%)
  starting transfers between devices  19.4 us (7%)
  local copies, waits for them, and re-layouts  17.8 us (7%)
  other arithmetic  16.7 us (6%)
    pallas_call x1, Pallas kernels, run_layer(): pl.pallas_call(layer_kernel, grid_spec=pltpu.PrefetchScalarGridSpec(num_s...  182 us
    ppermute x19, waiting for transfers between devices, swap(): return lax.ppermute(value, axis, [(i, i ^ bit) for i in range(size)])  26.6 us
    ppermute x19, starting transfers between devices, swap(): return lax.ppermute(value, axis, [(i, i ^ bit) for i in range(size)])  19.4 us
  transfers between devices with their start and end apart: 19, of which 10 were waited for; matrix products, arithmetic and copies ran while one was open for 9% of the time, Pallas kernels for 0%

profile of v8, /device:TPU:1, one launch (start us, length us, event | category | flops | bytes accessed | tf_op | source)
XLA Modules:
  0.0 263.4 jit_solution(1415398138091556151)
XLA Ops:
  3.8 1.3 select_reduce_fusion
  5.4 3.2 %collective-permute-start.2 = (bf16[288,128]{1,0:T(8,128)(2,1)S(1)}, bf16[288,128]{1,0:T(8,128)(2,1)S(1)}, u32[]{:S(2)}, u32[]{:S(2)}) collective-permute-start(bf16[288,128]{1,0:T(8,128)(2,1)S(1)} %pad_maximum_fusion.5), channel_id=1, source_target_pairs={{0,16},{2,18},{4,20},{6,22},{8,24},{10,26},{12,28},{14,30},{16,0},... | collective-permute-start | bytes 221192 | tf_op jit(solution)/shard_map/ppermute | solution.py:647
  9.3 1.6 broadcast_multiply_fusion.up_kept_ref
  13.8 1.4 collective-permute-start.3
  16.2 2.2 collective-permute-done.3
  18.5 2.2 collective-permute-start.6
  21.8 3.7 %collective-permute-done.6 = bf16[960,128]{1,0:T(8,128)(2,1)S(1)} collective-permute-done((bf16[960,128]{1,0:T(8,128)(2,1)S(1)}, bf16[960,128]{1,0:T(8,128)(2,1)S(1)}, u32[]{:S(2)}, u32[]{:S(2)}) %collective-permute-start.6) | collective-permute-done | bytes 245792 | tf_op jit(solution)/shard_map/ppermute | solution.py:647
  25.6 6.5 %collective-permute-done.5 = bf16[960,128]{1,0:T(8,128)(2,1)S(1)} collective-permute-done((bf16[960,128]{1,0:T(8,128)(2,1)S(1)}, bf16[960,128]{1,0:T(8,128)(2,1)S(1)}, u32[]{:S(2)}, u32[]{:S(2)}) %collective-permute-start.5) | collective-permute-done | bytes 245792 | tf_op jit(solution)/shard_map/ppermute | solution.py:647
  33.0 1.1 collective-permute-start.7
  42.6 181.6 %shard_map.119 = (bf16[2,512,256]{2,1,0:T(8,128)(2,1)}, bf16[2,512,256]{2,1,0:T(8,128)(2,1)}, f32[2,512,256]{2,1,0:T(8,128)}, f32[2,512,256]{2,1,0:T(8,128)}, bf...) custom-call(s32[1]{0:T(128)} %bitcast.core_ref, ...), custom_call_target="tpu_custom_call" | custom-call | tf_op jit(solution)/shard_map/pallas_call | solution.py:585
  227.6 1.3 reshape.209
  233.8 1.1 broadcast_select_fusion.3
  236.0 1.5 fusion
  237.5 1.3 collective-permute-start.10
  238.9 1.2 collective-permute-start.11
  240.5 1.5 pad_maximum_fusion
  242.0 2.8 %collective-permute-done.10 = bf16[4,224,128]{2,1,0:T(8,128)(2,1)S(1)} collective-permute-done((bf16[4,224,128]{2,1,0:T(8,128)(2,1)S(1)}, bf16[4,224,128]{2,1,0:T(8,128)(2,1)S(1)}, u32[]{:S(2)}, u32[]{:S(2)}) %collective-permute-start.10) | collective-permute-done | bytes 229408 | tf_op jit(solution)/shard_map/ppermute | solution.py:647
  245.7 5.0 %collective-permute-done.12 = bf16[4,224,128]{2,1,0:T(8,128)(2,1)S(1)} collective-permute-done((bf16[4,224,128]{2,1,0:T(8,128)(2,1)S(1)}, bf16[4,224,128]{2,1,0:T(8,128)(2,1)S(1)}, u32[]{:S(2)}, u32[]{:S(2)}) %collective-permute-start.12) | collective-permute-done | bytes 229408 | tf_op jit(solution)/shard_map/ppermute | solution.py:647
  250.8 1.4 collective-permute-start.15
  252.9 1.5 collective-permute-start.17
  254.6 2.1 collective-permute-done.16
  256.6 1.7 collective-permute-done.17
  258.3 2.6 collective-permute-start.18
  262.0 1.4 broadcast_select_fusion.5
  (154 shorter events, 31.0 us)
Async XLA Ops:
  1.5 32.6 %copy-start.10 = (s32[32]{0:T(128)}, s32[32]{0:T(128)S(1)}, u32[]{:S(2)}) copy-start(s32[32]{0:T(128)S(1)} %convert_reduce_fusion) | copy-start | bytes 388
  5.4 8.4 %collective-permute-start.2 = (bf16[288,128]{1,0:T(8,128)(2,1)S(1)}, bf16[288,128]{1,0:T(8,128)(2,1)S(1)}, u32[]{:S(2)}, u32[]{:S(2)}) collective-permute-start(bf16[288,128]{1,0:T(8,128)(2,1)S(1)} %pad_maximum_fusion.5), channel_id=1, source_target_pairs={{0,16},{2,18},{4,20},{6,22},{8,24},{10,26},{12,28},{14,30},{16,0},... | collective-permute-start | bytes 221192 | tf_op jit(solution)/shard_map/ppermute | solution.py:647
  11.9 30.7 %collective-permute-start.1 = (bf16[2,512,256]{2,1,0:T(8,128)(2,1)S(1)}, bf16[2,512,256]{2,1,0:T(8,128)(2,1)}, u32[]{:S(2)}, u32[]{:S(2)}) collective-permute-start(bf16[2,512,256]{2,1,0:T(8,128)(2,1)S(1)} %constant_dynamic-slice_fusion.3), channel_id=1, source_target_pairs={{0,1},{1,0},{2,3},{3,2},{4,5},{5,4},{6,7},{7,6},{8,9},{9,8},{10,11... | collective-permute-start | bytes 1572872 | tf_op jit(solution)/shard_map/ppermute | solution.py:647
  13.7 28.9 %collective-permute-start = (bf16[2,512,256]{2,1,0:T(8,128)(2,1)}, bf16[2,512,256]{2,1,0:T(8,128)(2,1)}, u32[]{:S(2)}, u32[]{:S(2)}) collective-permute-start(bf16[2,512,256]{2,1,0:T(8,128)(2,1)} %constant_dynamic-slice_fusion.4), channel_id=1, source_target_pairs={{0,1},{1,0},{2,3},{3,2},{4,5},{5,4},{6,7},{7,6},{8,9},{9,8},{10,11... | collective-permute-start | bytes 1572872 | tf_op jit(solution)/shard_map/ppermute | solution.py:647
  13.8 4.7 %collective-permute-start.3 = (bf16[512,128]{1,0:T(8,128)(2,1)S(1)}, bf16[512,128]{1,0:T(8,128)(2,1)S(1)}, u32[]{:S(2)}, u32[]{:S(2)}) collective-permute-start(bf16[512,128]{1,0:T(8,128)(2,1)S(1)} %pad_maximum_fusion.4), channel_id=1, source_target_pairs={{0,8},{2,10},{4,12},{6,14},{8,0},{10,2},{12,4},{14,6},{16,24},{18,... | collective-permute-start | bytes 393224 | tf_op jit(solution)/shard_map/ppermute | solution.py:647
  18.5 7.1 %collective-permute-start.6 = (bf16[960,128]{1,0:T(8,128)(2,1)S(1)}, bf16[960,128]{1,0:T(8,128)(2,1)S(1)}, u32[]{:S(2)}, u32[]{:S(2)}) collective-permute-start(bf16[960,128]{1,0:T(8,128)(2,1)S(1)} %pad_maximum_fusion.3), channel_id=1, source_target_pairs={{0,6},{2,4},{4,2},{6,0},{8,14},{10,12},{12,10},{14,8},{16,22},{18,... | collective-permute-start | bytes 737288 | tf_op jit(solution)/shard_map/ppermute | solution.py:647
  21.3 10.8 %collective-permute-start.4 = (bf16[960,128]{1,0:T(8,128)(2,1)S(1)}, bf16[960,128]{1,0:T(8,128)(2,1)S(1)}, u32[]{:S(2)}, u32[]{:S(2)}) collective-permute-start(bf16[960,128]{1,0:T(8,128)(2,1)S(1)} %pad_maximum_fusion.3), channel_id=1, source_target_pairs={{0,2},{2,0},{4,6},{6,4},{8,10},{10,8},{12,14},{14,12},{16,18},{18,... | collective-permute-start | bytes 737288 | tf_op jit(solution)/shard_map/ppermute | solution.py:647
  21.6 10.5 %collective-permute-start.5 = (bf16[960,128]{1,0:T(8,128)(2,1)S(1)}, bf16[960,128]{1,0:T(8,128)(2,1)S(1)}, u32[]{:S(2)}, u32[]{:S(2)}) collective-permute-start(bf16[960,128]{1,0:T(8,128)(2,1)S(1)} %pad_maximum_fusion.3), channel_id=1, source_target_pairs={{0,4},{2,6},{4,0},{6,2},{8,12},{10,14},{12,8},{14,10},{16,20},{18,... | collective-permute-start | bytes 737288 | tf_op jit(solution)/shard_map/ppermute | solution.py:647
  33.0 3.3 %collective-permute-start.7 = (bf16[32,112,128]{2,1,0:T(8,128)(2,1)S(1)}, bf16[32,112,128]{2,1,0:T(8,128)(2,1)S(1)}, u32[]{:S(2)}, u32[]{:S(2)}) collective-permute-start(bf16[32,112,128]{2,1,0:T(8,128)(2,1)S(1)} %gather_fusion), channel_id=1, source_target_pairs={{0,1},{1,0},{2,3},{3,2},{4,5},{5,4},{6,7},{7,6},{8,9},{9,8},{10,11... | collective-permute-start | bytes 2752520 | tf_op jit(solution)/shard_map/ppermute | solution.py:647
  34.9 1.3 collective-permute-start.8
  227.2 6.5 %collective-permute-start.13 = (bf16[2,512,256]{2,1,0:T(8,128)(2,1)}, bf16[2,512,256]{2,1,0:T(8,128)(2,1)}, u32[]{:S(2)}, u32[]{:S(2)}) collective-permute-start(bf16[2,512,256]{2,1,0:T(8,128)(2,1)} %get-tuple-element.25), channel_id=1, source_target_pairs={{0,1},{1,0},{2,3},{3,2},{4,5},{5,4},{6,7},{7,6},{8,9},{9,8},{10,11... | collective-permute-start | bytes 1572872 | tf_op jit(solution)/shard_map/ppermute | solution.py:647
  232.4 3.6 %collective-permute-start.9 = (bf16[3584,128]{1,0:T(8,128)(2,1)}, bf16[3584,128]{1,0:T(8,128)(2,1)}, u32[]{:S(2)}, u32[]{:S(2)}) collective-permute-start(bf16[3584,128]{1,0:T(8,128)(2,1)} %bitcast.21), channel_id=1, source_target_pairs={{0,1},{1,0},{2,3},{3,2},{4,5},{5,4},{6,7},{7,6},{8,9},{9,8},{10,11... | collective-permute-start | bytes 2752520 | tf_op jit(solution)/shard_map/ppermute | solution.py:647
  232.5 7.8 %collective-permute-start.14 = (f32[2,512,256]{2,1,0:T(8,128)}, f32[2,512,256]{2,1,0:T(8,128)S(1)}, u32[]{:S(2)}, u32[]{:S(2)}) collective-permute-start(f32[2,512,256]{2,1,0:T(8,128)} %get-tuple-element.27), channel_id=1, source_target_pairs={{0,1},{1,0},{2,3},{3,2},{4,5},{5,4},{6,7},{7,6},{8,9},{9,8},{10,11... | collective-permute-start | bytes 3145736 | tf_op jit(solution)/shard_map/ppermute | solution.py:647
  237.5 7.2 %collective-permute-start.10 = (bf16[4,224,128]{2,1,0:T(8,128)(2,1)S(1)}, bf16[4,224,128]{2,1,0:T(8,128)(2,1)S(1)}, u32[]{:S(2)}, u32[]{:S(2)}) collective-permute-start(bf16[4,224,128]{2,1,0:T(8,128)(2,1)S(1)} %get-tuple-element.37), channel_id=1, source_target_pairs={{0,2},{2,0},{4,6},{6,4},{8,10},{10,8},{12,14},{14,12},{16,18},{18,... | collective-permute-start | bytes 688136 | tf_op jit(solution)/shard_map/ppermute | solution.py:647
  238.9 6.8 %collective-permute-start.11 = (bf16[4,224,128]{2,1,0:T(8,128)(2,1)S(1)}, bf16[4,224,128]{2,1,0:T(8,128)(2,1)S(1)}, u32[]{:S(2)}, u32[]{:S(2)}) collective-permute-start(bf16[4,224,128]{2,1,0:T(8,128)(2,1)S(1)} %get-tuple-element.39), channel_id=1, source_target_pairs={{0,4},{2,6},{4,0},{6,2},{8,12},{10,14},{12,8},{14,10},{16,20},{18,... | collective-permute-start | bytes 688136 | tf_op jit(solution)/shard_map/ppermute | solution.py:647
  240.0 10.6 %collective-permute-start.12 = (bf16[4,224,128]{2,1,0:T(8,128)(2,1)S(1)}, bf16[4,224,128]{2,1,0:T(8,128)(2,1)S(1)}, u32[]{:S(2)}, u32[]{:S(2)}) collective-permute-start(bf16[4,224,128]{2,1,0:T(8,128)(2,1)S(1)} %get-tuple-element.38), channel_id=1, source_target_pairs={{0,6},{2,4},{4,2},{6,0},{8,14},{10,12},{12,10},{14,8},{16,22},{18,... | collective-permute-start | bytes 688136 | tf_op jit(solution)/shard_map/ppermute | solution.py:647
  242.0 20.0 %copy-start.2 = (f32[4,13696]{1,0:T(4,128)S(1)}, f32[4,13696]{1,0:T(4,128)}, u32[]{:S(2)}) copy-start(f32[4,13696]{1,0:T(4,128)} %param.13) | copy-start | bytes 657412
  242.0 20.0 %copy-start.6 = (f32[4,13696]{1,0:T(4,128)S(1)}, f32[4,13696]{1,0:T(4,128)}, u32[]{:S(2)}) copy-start(f32[4,13696]{1,0:T(4,128)} %param.15) | copy-start | bytes 657412
  242.0 20.0 %copy-start.7 = (f32[4,13696]{1,0:T(4,128)S(1)}, f32[4,13696]{1,0:T(4,128)}, u32[]{:S(2)}) copy-start(f32[4,13696]{1,0:T(4,128)} %param.14) | copy-start | bytes 657412
  242.0 20.0 %copy-start.8 = (pred[4]{0:T(512)(128)(4,1)S(1)}, pred[4]{0:T(512)(128)(4,1)}, u32[]{:S(2)}) copy-start(pred[4]{0:T(512)(128)(4,1)} %get-tuple-element.57) | copy-start | bytes 16
  250.8 3.7 %collective-permute-start.15 = (bf16[1,224,128]{2,1,0:T(8,128)(2,1)S(1)}, bf16[1,224,128]{2,1,0:T(8,128)(2,1)S(1)}, u32[]{:S(2)}, u32[]{:S(2)}) collective-permute-start(bf16[1,224,128]{2,1,0:T(8,128)(2,1)S(1)} %get-tuple-element.48), channel_id=1, source_target_pairs={{0,8},{2,10},{4,12},{6,14},{8,0},{10,2},{12,4},{14,6},{16,24},{18,... | collective-permute-start | bytes 172040 | tf_op jit(solution)/shard_map/ppermute | solution.py:647
  252.2 4.4 %collective-permute-start.16 = (bf16[1,224,128]{2,1,0:T(8,128)(2,1)S(1)}, bf16[1,224,128]{2,1,0:T(8,128)(2,1)S(1)}, u32[]{:S(2)}, u32[]{:S(2)}) collective-permute-start(bf16[1,224,128]{2,1,0:T(8,128)(2,1)S(1)} %get-tuple-element.50), channel_id=1, source_target_pairs={{0,16},{2,18},{4,20},{6,22},{8,24},{10,26},{12,28},{14,30},{16,0},... | collective-permute-start | bytes 172040 | tf_op jit(solution)/shard_map/ppermute | solution.py:647
  252.9 5.4 %collective-permute-start.17 = (bf16[1,224,128]{2,1,0:T(8,128)(2,1)S(1)}, bf16[1,224,128]{2,1,0:T(8,128)(2,1)S(1)}, u32[]{:S(2)}, u32[]{:S(2)}) collective-permute-start(bf16[1,224,128]{2,1,0:T(8,128)(2,1)S(1)} %get-tuple-element.49), channel_id=1, source_target_pairs={{0,24},{2,26},{4,28},{6,30},{8,16},{10,18},{12,20},{14,22},{16,8},... | collective-permute-start | bytes 172040 | tf_op jit(solution)/shard_map/ppermute | solution.py:647
  258.3 3.5 %collective-permute-start.18 = (f32[2,107,128]{2,1,0:T(8,128)S(1)}, f32[2,107,128]{2,1,0:T(8,128)S(1)}, u32[]{:S(2)}, u32[]{:S(2)}) collective-permute-start(f32[2,107,128]{2,1,0:T(8,128)S(1)} %bitcast.70), channel_id=1, source_target_pairs={{0,1},{1,0},{2,3},{3,2},{4,5},{5,4},{6,7},{7,6},{8,9},{9,8},{10,11... | collective-permute-start | bytes 328712 | tf_op jit(solution)/shard_map/ppermute | solution.py:647
  (11 other events, 56.5 us)
